TPU v7x, 512 devices: a whole 4x8x8 slice. The times are simulated.
512 devices in a mesh: cp: 64 (over z_lo, y, core), tp: 8 (over z_hi, x).
Axes of the slice: x: 4, y: 8, z: 8 (z_hi: 2, z_lo: 4; z = z_hi * 4 + z_lo), core: 2. Of those that a mesh axis runs over, the one named last changes fastest.
Arguments:
- queries: bfloat16 [8192, 8192], P('cp', 'tp'), may hold values from -8 to 8
- keys: bfloat16 [8192, 1024], P('cp', 'tp'), may hold values from -8 to 8
- values: bfloat16 [8192, 1024], P('cp', 'tp'), may hold values from -6 to 6
- positions: int32 [8192], replicated, may hold values from 0 to 8191, as said below
- counts: int32 [64], replicated, may hold values from 1 to 128, as said below
- owner_row: int32 [8, 64], replicated, may hold values from 0 to 63, as said below
- owner_col: int32 [8, 64], replicated, may hold values from 0 to 7, as said below
- owner_slot: int32 [8, 64], replicated, may hold values from 0 to 1
Outputs:
- attended: bfloat16 [8192, 8192], P('cp', 'tp')
- pool_keys: bfloat16 [1024, 128, 128], P(('cp', 'tp'))
- pool_values: bfloat16 [1024, 128, 128], P(('cp', 'tp'))
Inputs may be any that keep to these rules, and one draw needn't show every extreme that they name: A permutation of the positions. The rows of index c of cp are two runs of 64 consecutive positions, each starting at a multiple of 64: run j first, then run 2 * 64 - 1 - j, every j from 0 to 64 - 1 once. `counts`: some page holds 128 valid tokens and some page holds one. `owner_row`: for every kv head, every index of cp owns exactly one page. `owner_col`: no two (kv head, page) pairs name the same owner row, column and slot; a device keeps at most 2 pages and some device keeps exactly 2.
All inputs are finite; a program needn't handle non-finite values.
Results may differ from a plain program's by a relative error of at most 0.012.
The roundings to bfloat16 on the way count: a program that leaves them out, or rounds other values in their place, can miss the bound.
Values may be sent and summed in bfloat16 or wider, within the bound.
No kernel may reach another device: no remote copies, remote signals or barrier semaphores. Data moves between devices by JAX's collectives and lax.ppermute only.
A program may use at most 64 MiB of HBM per device.

v0:
```python
import math

import jax
import jax.numpy as jnp
from jax import lax
from jax.sharding import PartitionSpec as P

KVH = 8
HD = 128
PAGE = 128
HALF = 64


theta_base = 500000.0
neg_big = -1e30


def rotate(tensor, token_pos):
    half_dim = tensor.shape[-1] // 2
    inv_freq = theta_base ** (-(jnp.arange(half_dim, dtype=jnp.float32) * 2.0 / tensor.shape[-1]))
    angles = token_pos.astype(jnp.float32)[:, None] * inv_freq[None, :]
    cos_part = jnp.concatenate([jnp.cos(angles), jnp.cos(angles)], axis=-1)[:, None, :]
    sin_part = jnp.concatenate([jnp.sin(angles), jnp.sin(angles)], axis=-1)[:, None, :]
    turned = jnp.concatenate([-tensor[..., half_dim:], tensor[..., :half_dim]], axis=-1)
    return tensor * cos_part + turned * sin_part


def pick_flat(lookup, where_in):
    matches = where_in[..., None] == jnp.arange(lookup.shape[0], dtype=jnp.int32)
    return jnp.sum(jnp.where(matches, lookup, 0), axis=-1)


def pick_rows(lookup, where_in):
    matches = where_in[..., None] == jnp.arange(lookup.shape[1], dtype=jnp.int32)
    return jnp.sum(jnp.where(matches, lookup[:, None, :], 0), axis=-1)


def ranks_in_row(row_ids):
    extent = row_ids.shape[1]
    earlier = jnp.arange(extent)[:, None] > jnp.arange(extent)[None, :]
    same_row = row_ids[:, :, None] == row_ids[:, None, :]
    return jnp.sum(same_row & earlier[None], axis=-1)


def pages_of_row(row_ids, row_rank, row_here, per_row):
    extent = row_ids.shape[1]
    matches = (row_ids == row_here)[:, None, :] & (
        row_rank[:, None, :] == jnp.arange(per_row, dtype=jnp.int32)[None, :, None]
    )
    return jnp.sum(
        jnp.where(matches, jnp.arange(extent, dtype=jnp.int32)[None, None, :], 0), axis=-1
    )


def stored_rows(positions, need_pos):
    run_first = positions.reshape(-1, HALF)[:, 0] // HALF
    matches = (need_pos // HALF)[..., None] == run_first
    holder = jnp.sum(
        jnp.where(matches, jnp.arange(run_first.shape[0], dtype=jnp.int32), 0), axis=-1
    )
    return holder * HALF + need_pos % HALF


def attend_block(softmax_state, q_grp, q_pos, key_block, value_block, key_pos, key_valid):
    row_top, totals, summed = softmax_state
    kv_local = q_grp.shape[1]
    key_heads = key_block.reshape(-1, kv_local, HD)
    value_heads = value_block.reshape(-1, kv_local, HD)
    scores = jnp.einsum("tkgd,nkd->kgtn", q_grp, key_heads, preferred_element_type=jnp.float32) * (
        1.0 / math.sqrt(HD)
    )
    allowed = (key_pos[None, :] <= q_pos[:, None]) & key_valid[None, :]
    scores = jnp.where(allowed, scores, neg_big)
    new_top = jnp.maximum(row_top, jnp.max(scores, axis=-1))
    factor = jnp.exp(row_top - new_top)
    weights = jnp.where(allowed, jnp.exp(scores - new_top[..., None]), 0.0)
    totals = totals * factor + jnp.sum(weights, axis=-1)
    summed = summed * factor[..., None] + jnp.einsum(
        "kgtn,nkd->kgtd",
        weights.astype(jnp.bfloat16),
        value_heads,
        preferred_element_type=jnp.float32,
    )
    return (new_top, totals, summed)


def attend_range(softmax_state, q_grp, q_pos, key_rows, value_rows, key_pos, counts):
    row_total = key_rows.shape[0]
    block_rows = 512
    key_valid = key_pos % PAGE < pick_flat(counts, key_pos // PAGE)

    def one_block(carried, block_id):
        first_row = block_id * block_rows
        key_block = lax.dynamic_slice_in_dim(key_rows, first_row, block_rows, 0)
        value_block = lax.dynamic_slice_in_dim(value_rows, first_row, block_rows, 0)
        pos_block = lax.dynamic_slice_in_dim(key_pos, first_row, block_rows, 0)
        valid_block = lax.dynamic_slice_in_dim(key_valid, first_row, block_rows, 0)
        return (
            attend_block(carried, q_grp, q_pos, key_block, value_block, pos_block, valid_block),
            None,
        )

    softmax_state, _ = lax.scan(
        one_block, softmax_state, jnp.arange(row_total // block_rows, dtype=jnp.int32)
    )
    return softmax_state


def shards(queries, keys, values, positions, counts, owner_row, owner_col, owner_slot):
    cp_rank = lax.axis_index("cp")
    tp_rank = lax.axis_index("tp")
    tok_rows = queries.shape[0]
    q_local = queries.shape[1] // HD
    kv_local = keys.shape[1] // HD
    group = q_local // kv_local
    per_row = tok_rows // PAGE
    slot_count = 2 * KVH * per_row // lax.axis_size("tp")
    my_pos = lax.dynamic_slice_in_dim(positions, cp_rank * tok_rows, tok_rows, 0)
    q_rot = rotate(queries.astype(jnp.float32).reshape(tok_rows, q_local, HD), my_pos).astype(
        jnp.bfloat16
    )
    q_grp = q_rot.reshape(tok_rows, kv_local, group, HD)
    k_rot = (
        rotate(keys.astype(jnp.float32).reshape(tok_rows, kv_local, HD), my_pos)
        .astype(jnp.bfloat16)
        .reshape(tok_rows, kv_local * HD)
    )
    row_rank = ranks_in_row(owner_row)
    page_all = pages_of_row(owner_row, row_rank, cp_rank, per_row)
    page_mine = lax.dynamic_slice_in_dim(page_all, tp_rank * kv_local, kv_local, 0)
    offsets = jnp.arange(PAGE, dtype=jnp.int32)
    need_pos = (page_mine[:, :, None] * PAGE + offsets).reshape(kv_local, per_row * PAGE)
    need_ok = (offsets < pick_flat(counts, page_mine)[:, :, None]).reshape(kv_local, per_row * PAGE)
    start_state = (
        jnp.full((kv_local, group, tok_rows), neg_big, jnp.float32),
        jnp.zeros((kv_local, group, tok_rows), jnp.float32),
        jnp.zeros((kv_local, group, tok_rows, HD), jnp.float32),
    )
    whole_keys, whole_values = (
        lax.all_gather(k_rot, "cp", axis=0, tiled=True),
        lax.all_gather(values, "cp", axis=0, tiled=True),
    )
    softmax_state = attend_range(
        start_state, q_grp, my_pos, whole_keys, whole_values, positions, counts
    )
    stored = stored_rows(positions, need_pos)
    zero_half = jnp.zeros((), jnp.bfloat16)
    picked_keys = jnp.take(whole_keys.reshape(-1, kv_local, HD), stored[0], axis=0)[:, 0]
    picked_values = jnp.take(whole_values.reshape(-1, kv_local, HD), stored[0], axis=0)[:, 0]
    key_list = [jnp.where(need_ok[0][:, None], picked_keys, zero_half)]
    value_list = [jnp.where(need_ok[0][:, None], picked_values, zero_half)]
    kept_keys = jnp.stack(key_list)
    kept_values = jnp.stack(value_list)
    row_top, totals, summed = softmax_state
    attended = (
        (summed / totals[..., None])
        .transpose(2, 0, 1, 3)
        .astype(jnp.bfloat16)
        .reshape(tok_rows, q_local * HD)
    )
    all_keys, all_values = (
        lax.all_gather(kept_keys, "tp", axis=0, tiled=True),
        lax.all_gather(kept_values, "tp", axis=0, tiled=True),
    )
    dest_col = pick_rows(owner_col, page_all).reshape(-1)
    dest_slot = pick_rows(owner_slot, page_all).reshape(-1)
    select = (
        (dest_col == tp_rank)[None, :]
        & (dest_slot[None, :] == jnp.arange(slot_count, dtype=jnp.int32)[:, None])
    ).astype(jnp.bfloat16)
    pool_keys = jnp.einsum(
        "se,epd->spd", select, all_keys, preferred_element_type=jnp.float32
    ).astype(jnp.bfloat16)
    pool_values = jnp.einsum(
        "se,epd->spd", select, all_values, preferred_element_type=jnp.float32
    ).astype(jnp.bfloat16)
    return (attended, pool_keys, pool_values)


def solution(mesh):
    return jax.shard_map(
        shards,
        mesh=mesh,
        in_specs=(P("cp", "tp"), P("cp", "tp"), P("cp", "tp"), P(), P(), P(), P(), P()),
        out_specs=(P("cp", "tp"), P(("cp", "tp"), None, None), P(("cp", "tp"), None, None)),
        check_vma=False,
    )
```

profile of v0, /device:TPU:6, one launch (start us, length us, event | category | flops | bytes accessed | tf_op | source)
XLA Modules:
  0.0 440.4 jit_solution(12833369907008418935)
XLA Ops:
  7.2 0.8 convert_bitcast_fusion
  8.1 0.8 fusion.43
  9.2 1.5 pad_maximum_fusion
  10.7 0.7 all-gather.5.cloned.1.call-update
  11.5 0.8 reshape.441
  12.5 1.1 copy.46
  14.5 0.6 dynamic-slice.3
  15.8 1.3 fusion.40
  17.1 0.6 iota_compare_fusion.3
  18.8 115.2 %all-gather.3.cloned.1.call-done = bf16[8192,128]{1,0:T(8,128)(2,1)} async-done(((bf16[128,128]{1,0:T(8,128)(2,1)}), bf16[8192,128]{1,0:T(8,128)(2,1)}) %all-gather.3.cloned.1.call-update) | async-done | bytes 2097168 | tf_op jit(solution)/shard_map/all_gather | solution.py:140
  134.0 118.2 %all-gather.5.cloned.1.call-done = bf16[8192,128]{1,0:T(8,128)(2,1)} async-done(((bf16[128,128]{1,0:T(8,128)(2,1)}), bf16[8192,128]{1,0:T(8,128)(2,1)}) %all-gather.5.cloned.1.call-update) | async-done | bytes 2097168 | tf_op jit(solution)/shard_map/all_gather | solution.py:141
  252.1 85.3 %while.15 = (s32[]{:T(128)}, f32[1,8,128]{2,1,0:T(8,128)S(1)}, f32[1,8,128]{2,1,0:T(8,128)S(1)}, f32[1,8,128,128]{3,2,1,0:T(8,128)S(1)}, s32[16]{0:T(128)S(1)}, ...) while((s32[]{:T(128)}, f32[1,8,128]{2,1,0:T(8,128)S(1)}, ...), condition=%wide.region_4.5_spmd.clone, body=%wide.region_1.4_spmd.clone.sunk | while | flops 275781632 | bytes 8200419 | solution.py:103
  253.7 1.4 fusion.52
  255.1 1.8 fusion.55
  257.5 0.6 dynamic_slice.44
  259.1 1.4 fusion.52
  260.5 1.8 fusion.55
  262.8 0.6 dynamic_slice.44
  264.4 1.4 fusion.52
  265.8 1.8 fusion.55
  268.1 0.6 dynamic_slice.44
  269.7 1.4 fusion.52
  271.1 1.8 fusion.55
  273.5 0.6 dynamic_slice.44
  275.1 1.4 fusion.52
  276.5 1.8 fusion.55
  278.8 0.6 dynamic_slice.44
  280.4 1.4 fusion.52
  281.8 1.8 fusion.55
  285.7 1.4 fusion.52
  287.1 1.8 fusion.55
  291.1 1.4 fusion.52
  292.5 1.8 fusion.55
  294.8 0.6 dynamic_slice.44
  296.4 1.4 fusion.52
  297.8 1.8 fusion.55
  300.1 0.6 dynamic_slice.44
  301.7 1.4 fusion.52
  303.1 1.8 fusion.55
  305.4 0.6 dynamic_slice.44
  307.1 1.4 fusion.52
  308.4 1.8 fusion.55
  310.8 0.6 dynamic_slice.44
  312.4 1.4 fusion.52
  313.8 1.8 fusion.55
  316.1 0.6 dynamic_slice.44
  317.7 1.4 fusion.52
  319.1 1.8 fusion.55
  321.4 0.6 dynamic_slice.44
  323.1 1.4 fusion.52
  324.4 1.8 fusion.55
  326.8 0.6 dynamic_slice.44
  328.4 1.4 fusion.52
  329.8 1.8 fusion.55
  332.1 0.6 dynamic_slice.44
  333.7 1.4 fusion.52
  335.1 1.8 fusion.55
  337.8 0.8 copy.62
  338.6 2.5 gather_fusion
  341.1 2.5 gather_fusion.1
  343.7 44.0 %all_gather.14 = bf16[8,128,128]{2,1,0:T(8,128)(2,1)S(1)} all-gather(bf16[1,128,128]{2,1,0:T(8,128)(2,1)S(1)} %get-tuple-element.199), channel_id=1, replica_groups=mesh['cp'=64,'tp'=8] {'tp'}, dimensions={0}, use_global_device_ids=true | all-gather | bytes 294912 | tf_op jit(solution)/shard_map/all_gather | solution.py:162
  388.0 0.6 copy.53
  388.6 44.0 %all_gather.15 = bf16[8,128,128]{2,1,0:T(8,128)(2,1)S(1)} all-gather(bf16[1,128,128]{2,1,0:T(8,128)(2,1)S(1)} %get-tuple-element.198), channel_id=1, replica_groups=mesh['cp'=64,'tp'=8] {'tp'}, dimensions={0}, use_global_device_ids=true | all-gather | bytes 294912 | tf_op jit(solution)/shard_map/all_gather | solution.py:163
  432.9 0.6 copy.54
  (159 shorter events, 19.6 us)
Async XLA Ops:
  7.2 126.8 %all-gather.3.cloned.1.call-start = ((), (), s32[]{:S(2)}) async-start(), calls=%async_computation | async-start | bytes 2129920 | tf_op jit(solution)/shard_map/all_gather | solution.py:140
  10.7 241.4 %all-gather.5.cloned.1.call-start = ((), (), s32[]{:S(2)}) async-start(), calls=%async_computation.1 | async-start | bytes 2129920 | tf_op jit(solution)/shard_map/all_gather | solution.py:141
  12.5 1.6 copy-start.1
  12.5 3.3 copy-start.4
  13.7 4.4 copy-start.2
  13.7 4.4 copy-start.3
  13.7 4.6 %copy-start = (s32[8192]{0:T(1024)S(1)}, s32[8192]{0:T(1024)}, u32[]{:S(2)}) copy-start(s32[8192]{0:T(1024)} %param.15) | copy-start | bytes 98308
Sparse Core Ops, SparseCore 0:
  10.8 123.0 all-gather.2
  136.1 115.9 all-gather.4
where the time goes:
time: 442 us; the launch traced here: 440 us
  waiting for transfers between devices  234 us (53%)
  blocking collectives  88 us (20%)
  matrix products  50.6 us (11%)
  local copies, waits for them, and re-layouts  22.2 us (5%)
  other arithmetic  19 us (4%)
  between operations  15 us (3%)
  loops' own time  11.5 us (3%)
    all_gather x1, waiting for transfers between devices, shards(): lax.all_gather(values, 'cp', axis=0, tiled=True)  118 us
    all_gather x1, waiting for transfers between devices, shards(): lax.all_gather(k_rot, 'cp', axis=0, tiled=True)  115 us
    all_gather x1, blocking collectives, shards(): lax.all_gather(kept_keys, 'tp', axis=0, tiled=True)  44 us
    all_gather x1, blocking collectives, shards(): lax.all_gather(kept_values, 'tp', axis=0, tiled=True)  44 us
    dot_general x16, matrix products, attend_block(): jnp.einsum('kgtn,nkd->kgtd', weights.astype(jnp.bfloat16), value_heads, p...  28.2 us
    dot_general x16, matrix products, attend_block(): jnp.einsum('tkgd,nkd->kgtn', q_grp, key_heads, preferred_element_type=jnp...  21.9 us
    another operation x1, loops' own time, attend_range(): lax.scan(one_block, softmax_state, jnp.arange(row_total // block_rows, dt...  11.5 us
    dynamic_slice x16, local copies, waits for them, and re-layouts, attend_range(): lax.scan(one_block, softmax_state, jnp.arange(row_total // block_rows, dt...  9.38 us
  transfers between devices with their start and end apart: 2, of which 2 were waited for; matrix products, arithmetic and copies ran while one was open for 1% of the time, Pallas kernels for 0%

commit v1 on v0

v1 whole, which is shorter than its diff:
```python
import functools
import math

import jax
import jax.numpy as jnp
import numpy as np
from jax import lax
from jax.experimental import pallas as pl
from jax.experimental.pallas import tpu as pltpu
from jax.sharding import PartitionSpec as P

KVH = 8
HD = 128
PAGE = 128
HALF = 64
ROWS = 128
N_CP = 64
N_Z = 4
N_Y = 8
N_TP = 8
N_X = 4
SRC = N_CP // 2
CHUNK = 4
RUNS = 2 * N_CP
BIG = 1e30

THETA = 500000.0
FREQ = np.concatenate([THETA ** (-np.arange(HALF) * 2.0 / HD)] * 2).astype(np.float32)[None, :]
OFFSETS = (0, -1, 1, -2, 2, -3, 3, 4)


def cp_index(z, y, core):
    return ((z % N_Z) * N_Y + y % N_Y) * 2 + core


def cp_pairs(step):
    return [
        (cp_index(z, y, c), cp_index(z, y + step, c))
        for z in range(N_Z)
        for y in range(N_Y)
        for c in range(2)
    ]


CORE_PAIRS = [(i, i ^ 1) for i in range(N_CP)]
Z_GROUPS = [[cp_index(z, y, c) for z in range(N_Z)] for y in range(N_Y) for c in range(2)]
ZHI_PAIRS = [(i, (i + N_X) % N_TP) for i in range(N_TP)]


def x_pairs(step):
    return [(i, (i // N_X) * N_X + (i + step) % N_X) for i in range(N_TP)]


def angles_of(freq, first_run, second_run, rows):
    row = lax.broadcasted_iota(jnp.int32, (rows, HD), 0)
    pos = jnp.where(row < HALF, first_run * HALF + row, second_run * HALF + row - HALF)
    angles = pos.astype(jnp.float32) * freq
    low = lax.broadcasted_iota(jnp.int32, (rows, HD), 1) < HALF
    sin = jnp.sin(angles)
    return jnp.cos(angles), jnp.where(low, -sin, sin)


def turned(x, cos, sin):
    return x * cos + pltpu.roll(x, HALF, 1) * sin


def pack_kernel(runs, keys, values, freq, out):
    first = runs[0]
    cos, sin = angles_of(freq[...], first, RUNS - 1 - first, ROWS)
    k_rot = turned(keys[...].astype(jnp.float32), cos, sin).astype(jnp.bfloat16)
    v = values[...]
    for i in range(N_Z):
        out[i, 0] = k_rot
        out[i, 1] = v


def pack(my_run, keys, values):
    smem = pl.BlockSpec(memory_space=pltpu.SMEM)
    vmem = pl.BlockSpec(memory_space=pltpu.VMEM)
    return pl.pallas_call(
        pack_kernel,
        out_shape=jax.ShapeDtypeStruct((N_Z, 2, ROWS, HD), jnp.bfloat16),
        in_specs=[smem, vmem, vmem, vmem],
        out_specs=vmem,
        cost_estimate=pl.CostEstimate(flops=1_000_000, bytes_accessed=400_000, transcendentals=0),
        name="pack",
    )(my_run, keys, values, jnp.asarray(FREQ))


def attend_kernel(place, run_of, counts, queries, freq, own, other, out, kv, q_rot, blk, sems):
    copies = [
        pltpu.make_async_copy(own, kv.at[pl.ds(0, SRC)], sems.at[0]),
        pltpu.make_async_copy(other, kv.at[pl.ds(SRC, SRC)], sems.at[1]),
    ]
    for copy in copies:
        copy.start()
    y, core = place[0], place[1]
    me = place[2]
    my_run = run_of[me]

    for side in range(2):
        for i, off in enumerate(OFFSETS):
            src_y = lax.rem(y + off + N_Y, N_Y)
            src_c = core if side == 0 else 1 - core
            for z in range(N_Z):
                blk[run_of[(z * N_Y + src_y) * 2 + src_c]] = side * SRC + i * N_Z + z

    cos, sin = angles_of(freq[...], my_run, RUNS - 1 - my_run, ROWS)
    for h in range(KVH):
        x = turned(queries[:, h * HD : (h + 1) * HD].astype(jnp.float32), cos, sin)
        x = x.astype(jnp.bfloat16)
        q_rot[0, h * HALF : (h + 1) * HALF, :] = x[:HALF]
        q_rot[1, h * HALF : (h + 1) * HALF, :] = x[HALF:]
    for copy in copies:
        copy.wait()

    cols = KVH * HALF
    width = CHUNK * HALF
    scale = math.log2(math.e) / math.sqrt(HD)
    key_at = lax.broadcasted_iota(jnp.int32, (HALF, HD), 0)
    dot = functools.partial(lax.dot_general, preferred_element_type=jnp.float32)

    def half_block(run):
        second = run >= N_CP
        j = jnp.where(second, RUNS - 1 - run, run)
        b = blk[jnp.clip(j, 0, N_CP - 1)]
        rows = pl.ds(pl.multiple_of(jnp.where(second, HALF, 0), HALF), HALF)
        valid = jnp.clip(counts[lax.shift_right_logical(run, 1)] - (run & 1) * HALF, 0, HALF)
        return kv[b, 0, rows, :], kv[b, 1, rows, :], valid

    def step(q, q_run, last, i, state):
        top, total, acc = state
        ks, vs, biases = [], [], []
        for r in range(CHUNK):
            run = i * CHUNK + r
            k, v, valid = half_block(jnp.minimum(run, RUNS - 1))
            ks.append(k)
            vs.append(v)
            if last:
                valid = jnp.where(run <= q_run, valid, 0)
            biases.append(jnp.where(key_at < valid, 0.0, -BIG))
        keys = jnp.concatenate(ks, axis=0)
        vals = jnp.concatenate(vs, axis=0)
        bias = jnp.concatenate(biases, axis=0)
        s = dot(keys, q, (((1,), (1,)), ((), ()))) * scale
        s = s + jnp.concatenate([bias] * (cols // HD), axis=1)
        if last:
            key = lax.broadcasted_iota(jnp.int32, (width, cols), 0)
            row = lax.broadcasted_iota(jnp.int32, (width, cols), 1)
            ahead = (q_run - i * CHUNK) * HALF
            s = jnp.where(key <= ahead + (row & (HALF - 1)), s, -BIG)
        new_top = jnp.maximum(top, jnp.max(s, axis=0, keepdims=True))
        factor = jnp.exp2(top - new_top)
        w = jnp.exp2(s - new_top)
        total = total * factor + jnp.sum(w, axis=0, keepdims=True)
        acc = acc * factor + dot(vals, w.astype(jnp.bfloat16), (((0,), (0,)), ((), ())))
        return new_top, total, acc

    for part in range(2):
        q = q_rot[part]
        q_run = my_run if part == 0 else RUNS - 1 - my_run
        state = (
            jnp.full((1, cols), -BIG, jnp.float32),
            jnp.zeros((1, cols), jnp.float32),
            jnp.zeros((HD, cols), jnp.float32),
        )
        full = lax.shift_right_logical(q_run, CHUNK.bit_length() - 1)
        state = lax.fori_loop(0, full, functools.partial(step, q, q_run, False), state)
        _, total, acc = step(q, q_run, True, full, state)
        res = jnp.transpose(acc / total).astype(jnp.bfloat16)
        for h in range(KVH):
            out[part * HALF : (part + 1) * HALF, h * HD : (h + 1) * HD] = res[
                h * HALF : (h + 1) * HALF
            ]


def attend(place, run_of, counts, queries, own, other):
    smem = pl.BlockSpec(memory_space=pltpu.SMEM)
    vmem = pl.BlockSpec(memory_space=pltpu.VMEM)
    anywhere = pl.BlockSpec(memory_space=pl.ANY)
    return pl.pallas_call(
        attend_kernel,
        out_shape=jax.ShapeDtypeStruct((ROWS, KVH * HD), jnp.bfloat16),
        in_specs=[smem, smem, smem, vmem, vmem, anywhere, anywhere],
        out_specs=vmem,
        scratch_shapes=[
            pltpu.VMEM((2 * SRC, 2, ROWS, HD), jnp.bfloat16),
            pltpu.VMEM((2, KVH * HALF, HD), jnp.bfloat16),
            pltpu.SMEM((N_CP,), jnp.int32),
            pltpu.SemaphoreType.DMA((2,)),
        ],
        compiler_params=pltpu.CompilerParams(vmem_limit_bytes=40 * 2**20),
        cost_estimate=pl.CostEstimate(
            flops=20_000_000_000, bytes_accessed=5_000_000, transcendentals=4_000_000
        ),
        name="attend",
    )(place, run_of, counts, queries, jnp.asarray(FREQ), own, other)


def pick_kernel(where, own_a, other_a, own_b, other_b, out):
    row = lax.broadcasted_iota(jnp.int32, (HALF, HD), 0)
    for half, own, other in ((0, own_a, other_a), (1, own_b, other_b)):
        mine = where[half * 4] == 1
        keep = row < where[half * 4 + 3]
        for i in range(2):
            block = jnp.where(mine, own[0, i], other[0, i])
            out[i, half * HALF : (half + 1) * HALF, :] = jnp.where(
                keep, block, jnp.zeros_like(block)
            )


def pick(where, own, other):
    def spec(half):
        return pl.BlockSpec((1, 2, HALF, HD), lambda i, w: (w[half * 4 + 1], 0, w[half * 4 + 2], 0))

    return pl.pallas_call(
        pick_kernel,
        grid_spec=pltpu.PrefetchScalarGridSpec(
            num_scalar_prefetch=1,
            grid=(1,),
            in_specs=[spec(0), spec(0), spec(1), spec(1)],
            out_specs=pl.BlockSpec((2, PAGE, HD), lambda i, w: (0, 0, 0)),
        ),
        out_shape=jax.ShapeDtypeStruct((2, PAGE, HD), jnp.bfloat16),
        cost_estimate=pl.CostEstimate(flops=100_000, bytes_accessed=200_000, transcendentals=0),
        name="pick",
    )(where, own, other, own, other)


def place_kernel(table, near, right, left, far, pool_k, pool_v):
    zero = jnp.zeros((PAGE, HD), jnp.bfloat16)
    for slot in range(2):
        pool_k[slot] = zero
        pool_v[slot] = zero
    for i, pages in enumerate((near, right, left, far)):
        for hi in range(2):
            for slot in range(2):

                @pl.when(table[i * 2 + hi] == slot)
                def _(pages=pages, hi=hi, slot=slot):
                    pool_k[slot] = pages[hi, 0]
                    pool_v[slot] = pages[hi, 1]


def place(table, near, right, left, far):
    smem = pl.BlockSpec(memory_space=pltpu.SMEM)
    vmem = pl.BlockSpec(memory_space=pltpu.VMEM)
    shape = jax.ShapeDtypeStruct((2, PAGE, HD), jnp.bfloat16)
    return pl.pallas_call(
        place_kernel,
        out_shape=(shape, shape),
        in_specs=[smem, vmem, vmem, vmem, vmem],
        out_specs=(vmem, vmem),
        cost_estimate=pl.CostEstimate(flops=100_000, bytes_accessed=800_000, transcendentals=0),
        name="place",
    )(table, near, right, left, far)


def shards(queries, keys, values, positions, counts, owner_row, owner_col, owner_slot):
    cp_rank = lax.axis_index("cp")
    tp_rank = lax.axis_index("tp")
    y = (cp_rank // 2) % N_Y
    core = cp_rank % 2
    run_of = positions.reshape(N_CP, ROWS)[:, 0] // HALF
    my_run = lax.dynamic_slice_in_dim(run_of, cp_rank, 1, 0)

    packed = pack(my_run, keys, values)
    unit = lax.all_to_all(packed, "cp", 0, 0, axis_index_groups=Z_GROUPS)
    ahead, back = cp_pairs(1), cp_pairs(-1)
    f1 = lax.ppermute(unit, "cp", ahead)
    b1 = lax.ppermute(unit, "cp", back)
    f2 = lax.ppermute(f1, "cp", ahead)
    b2 = lax.ppermute(b1, "cp", back)
    f3 = lax.ppermute(f2, "cp", ahead)
    b3 = lax.ppermute(b2, "cp", back)
    f4 = lax.ppermute(f3, "cp", ahead)
    own = jnp.concatenate([unit, f1, b1, f2, b2, f3, b3, f4], axis=0)
    other = lax.ppermute(own, "cp", CORE_PAIRS)

    here = owner_row == cp_rank
    pages = jnp.sum(jnp.where(here, jnp.arange(N_CP, dtype=jnp.int32)[None, :], 0), axis=1)
    cols = jnp.sum(jnp.where(here, owner_col, 0), axis=1)
    slots = jnp.sum(jnp.where(here, owner_slot, 0), axis=1)
    page = lax.dynamic_slice_in_dim(pages, tp_rank, 1, 0)
    valid = jnp.sum(jnp.where(jnp.arange(N_CP) == page, counts, 0))
    where = []
    for half in range(2):
        run = page[0] * 2 + half
        second = run >= N_CP
        j = jnp.where(second, RUNS - 1 - run, run)
        src = jnp.sum(jnp.where(run_of == j, jnp.arange(N_CP, dtype=jnp.int32), 0))
        src_y = (src // 2) % N_Y
        off = (src_y - y) % N_Y
        order = jnp.where(off <= N_Y // 2, 2 * off, 2 * (N_Y - off) - 1)
        order = jnp.where(off == N_Y // 2, N_Y - 1, order)
        where += [
            (src % 2 == core).astype(jnp.int32),
            order * N_Z + src // (2 * N_Y),
            second.astype(jnp.int32),
            jnp.clip(valid - half * HALF, 0, HALF),
        ]
    picked = pick(jnp.stack(where), own, other)

    across = lax.ppermute(picked, "tp", ZHI_PAIRS)
    near = jnp.stack([picked, across])
    right = lax.ppermute(near, "tp", x_pairs(1))
    left = lax.ppermute(near, "tp", x_pairs(-1))
    far = lax.ppermute(near, "tp", x_pairs(2))

    attended = attend(jnp.stack([y, core, cp_rank]), run_of, counts, queries, own, other)

    goes = jnp.where(cols == tp_rank, slots, -1)
    hi, x = tp_rank // N_X, tp_rank % N_X
    heads = jnp.stack(
        [((hi + d) % 2) * N_X + (x - step) % N_X for step in (0, 1, -1, 2) for d in range(2)]
    )
    matches = heads[:, None] == jnp.arange(KVH)[None, :]
    table = jnp.sum(jnp.where(matches, goes[None, :], 0), axis=1)
    pool_keys, pool_values = place(table, near, right, left, far)
    return attended, pool_keys, pool_values


def solution(mesh):
    return jax.shard_map(
        shards,
        mesh=mesh,
        in_specs=(P("cp", "tp"), P("cp", "tp"), P("cp", "tp"), P(), P(), P(), P(), P()),
        out_specs=(P("cp", "tp"), P(("cp", "tp"), None, None), P(("cp", "tp"), None, None)),
        check_vma=False,
    )
```

time: 442 us -> 124 us (0.28)
  the two profiles are of different devices: /device:TPU:6 before, /device:TPU:1 now
where the time goes in v1:
time: 124 us; the launch traced here: 123 us
  starting transfers between devices  49.8 us (40%)
  Pallas kernels  26.7 us (22%)
  waiting for transfers between devices  14.1 us (11%)
  blocking collectives  13.8 us (11%)
  between operations  8.19 us (7%)
  local copies, waits for them, and re-layouts  6.08 us (5%)
  other arithmetic  4.46 us (4%)
    pallas_call x1, Pallas kernels, attend(): pl.pallas_call(attend_kernel, out_shape=jax.ShapeDtypeStruct((ROWS, KVH *...  20.1 us
    all_to_all x1, blocking collectives, shards(): unit = lax.all_to_all(packed, 'cp', 0, 0, axis_index_groups=Z_GROUPS)  13.8 us
    ppermute x1, starting transfers between devices, shards(): other = lax.ppermute(own, 'cp', CORE_PAIRS)  9.17 us
    ppermute x1, starting transfers between devices, shards(): across = lax.ppermute(picked, 'tp', ZHI_PAIRS)  7.93 us
    ppermute x1, waiting for transfers between devices, shards(): f4 = lax.ppermute(f3, 'cp', ahead)  6.26 us
    ppermute x1, starting transfers between devices, shards(): b3 = lax.ppermute(b2, 'cp', back)  4.57 us
    ppermute x1, starting transfers between devices, shards(): b2 = lax.ppermute(b1, 'cp', back)  4.57 us
    ppermute x1, starting transfers between devices, shards(): f1 = lax.ppermute(unit, 'cp', ahead)  4.05 us
  transfers between devices with their start and end apart: 12, of which 5 were waited for; matrix products, arithmetic and copies ran while one was open for 2% of the time, Pallas kernels for 16%

profile of v1, /device:TPU:1, one launch (start us, length us, event | category | flops | bytes accessed | tf_op | source)
XLA Modules:
  0.0 123.1 jit_solution(12873139533065284563)
XLA Ops:
  0.6 0.9 select_reduce_fusion
  1.5 0.6 dynamic_slice.7
  2.8 0.9 slice_reduce_fusion
  3.6 0.7 fusion.2
  4.3 0.7 dynamic_slice.6.runs
  5.0 2.4 %pack.1 = bf16[4,2,128,128]{3,2,1,0:T(8,128)(2,1)} custom-call(s32[1]{0:T(128)} %dynamic_slice.6.runs, bf16[128,128]{1,0:T(8,128)(2,1)} %keys.1, bf16[128,128]{1,0:T(8,128)(2,1)} %values.1, f32[1,128]{1,0:T(1,128)} %constant.190.clone.freq), custom_call_target="tpu_custom_call" | custom-call | flops 1000000 | bytes 400000 | tf_op jit(solution)/shard_map/pack/pallas_call | solution.py:80
  7.4 13.8 %all_to_all.5 = bf16[4,2,128,128]{3,2,1,0:T(8,128)(2,1)S(1)} all-to-all(bf16[4,2,128,128]{3,2,1,0:T(8,128)(2,1)} %pack.1), channel_id=1, replica_groups={{0,128,256,384},{8,136,264,392},{16,144,272,400},{24,152,280,408},{32,1..., dimensions={0} | all-to-all | bytes 524288 | tf_op jit(solution)/shard_map/all_to_all | solution.py:268
  21.3 4.0 %collective-permute-start = (bf16[4,2,128,128]{3,2,1,0:T(8,128)(2,1)S(1)}, bf16[4,2,128,128]{3,2,1,0:T(8,128)(2,1)S(1)}, u32[]{:S(2)}, u32[]{:S(2)}) collective-permute-start(bf16[4,2,128,128]{3,2,1,0:T(8,128)(2,1)S(1)} %all_to_all.5), channel_id=1, source_target_pairs={{0,16},{8,24},{16,32},{24,40},{32,48},{40,56},{48,64},{56,72},{64,... | collective-permute-start | bytes 786440 | tf_op jit(solution)/shard_map/ppermute | solution.py:270
  25.3 3.8 %collective-permute-start.1 = (bf16[4,2,128,128]{3,2,1,0:T(8,128)(2,1)S(1)}, bf16[4,2,128,128]{3,2,1,0:T(8,128)(2,1)S(1)}, u32[]{:S(2)}, u32[]{:S(2)}) collective-permute-start(bf16[4,2,128,128]{3,2,1,0:T(8,128)(2,1)S(1)} %all_to_all.5), channel_id=1, source_target_pairs={{0,112},{8,120},{16,0},{24,8},{32,16},{40,24},{48,32},{56,40},{64,... | collective-permute-start | bytes 786440 | tf_op jit(solution)/shard_map/ppermute | solution.py:271
  29.2 1.8 %collective-permute-done = bf16[4,2,128,128]{3,2,1,0:T(8,128)(2,1)S(1)} collective-permute-done((bf16[4,2,128,128]{3,2,1,0:T(8,128)(2,1)S(1)}, bf16[4,2,128,128]{3,2,1,0:T(8,128)(2,1)S(1)}, u32[]{:S(2)}, u32[]{:S(2)}) %collective-permute-start) | collective-permute-done | bytes 262176 | tf_op jit(solution)/shard_map/ppermute | solution.py:270
  31.0 1.9 %collective-permute-start.2 = (bf16[4,2,128,128]{3,2,1,0:T(8,128)(2,1)S(1)}, bf16[4,2,128,128]{3,2,1,0:T(8,128)(2,1)S(1)}, u32[]{:S(2)}, u32[]{:S(2)}) collective-permute-start(bf16[4,2,128,128]{3,2,1,0:T(8,128)(2,1)S(1)} %collective-permute-done), channel_id=1, source_target_pairs={{0,16},{8,24},{16,32},{24,40},{32,48},{40,56},{48,64},{56,72},{64,... | collective-permute-start | bytes 786440 | tf_op jit(solution)/shard_map/ppermute | solution.py:272
  32.9 0.0 collective-permute-done.1
  32.9 4.6 %collective-permute-start.3 = (bf16[4,2,128,128]{3,2,1,0:T(8,128)(2,1)S(1)}, bf16[4,2,128,128]{3,2,1,0:T(8,128)(2,1)S(1)}, u32[]{:S(2)}, u32[]{:S(2)}) collective-permute-start(bf16[4,2,128,128]{3,2,1,0:T(8,128)(2,1)S(1)} %collective-permute-done.1), channel_id=1, source_target_pairs={{0,112},{8,120},{16,0},{24,8},{32,16},{40,24},{48,32},{56,40},{64,... | collective-permute-start | bytes 786440 | tf_op jit(solution)/shard_map/ppermute | solution.py:273
  37.5 0.0 copy-start.4
  37.5 1.8 %collective-permute-done.2 = bf16[4,2,128,128]{3,2,1,0:T(8,128)(2,1)S(1)} collective-permute-done((bf16[4,2,128,128]{3,2,1,0:T(8,128)(2,1)S(1)}, bf16[4,2,128,128]{3,2,1,0:T(8,128)(2,1)S(1)}, u32[]{:S(2)}, u32[]{:S(2)}) %collective-permute-start.2) | collective-permute-done | bytes 262176 | tf_op jit(solution)/shard_map/ppermute | solution.py:272
  39.3 1.9 %collective-permute-start.4 = (bf16[4,2,128,128]{3,2,1,0:T(8,128)(2,1)S(1)}, bf16[4,2,128,128]{3,2,1,0:T(8,128)(2,1)S(1)}, u32[]{:S(2)}, u32[]{:S(2)}) collective-permute-start(bf16[4,2,128,128]{3,2,1,0:T(8,128)(2,1)S(1)} %collective-permute-done.2), channel_id=1, source_target_pairs={{0,16},{8,24},{16,32},{24,40},{32,48},{40,56},{48,64},{56,72},{64,... | collective-permute-start | bytes 786440 | tf_op jit(solution)/shard_map/ppermute | solution.py:274
  41.3 0.0 collective-permute-done.3
  41.3 4.6 %collective-permute-start.5 = (bf16[4,2,128,128]{3,2,1,0:T(8,128)(2,1)S(1)}, bf16[4,2,128,128]{3,2,1,0:T(8,128)(2,1)S(1)}, u32[]{:S(2)}, u32[]{:S(2)}) collective-permute-start(bf16[4,2,128,128]{3,2,1,0:T(8,128)(2,1)S(1)} %collective-permute-done.3), channel_id=1, source_target_pairs={{0,112},{8,120},{16,0},{24,8},{32,16},{40,24},{48,32},{56,40},{64,... | collective-permute-start | bytes 786440 | tf_op jit(solution)/shard_map/ppermute | solution.py:275
  45.9 1.7 %collective-permute-done.4 = bf16[4,2,128,128]{3,2,1,0:T(8,128)(2,1)S(1)} collective-permute-done((bf16[4,2,128,128]{3,2,1,0:T(8,128)(2,1)S(1)}, bf16[4,2,128,128]{3,2,1,0:T(8,128)(2,1)S(1)}, u32[]{:S(2)}, u32[]{:S(2)}) %collective-permute-start.4) | collective-permute-done | bytes 262176 | tf_op jit(solution)/shard_map/ppermute | solution.py:274
  47.6 1.9 %collective-permute-start.6 = (bf16[4,2,128,128]{3,2,1,0:T(8,128)(2,1)S(1)}, bf16[4,2,128,128]{3,2,1,0:T(8,128)(2,1)S(1)}, u32[]{:S(2)}, u32[]{:S(2)}) collective-permute-start(bf16[4,2,128,128]{3,2,1,0:T(8,128)(2,1)S(1)} %collective-permute-done.4), channel_id=1, source_target_pairs={{0,16},{8,24},{16,32},{24,40},{32,48},{40,56},{48,64},{56,72},{64,... | collective-permute-start | bytes 786440 | tf_op jit(solution)/shard_map/ppermute | solution.py:276
  49.6 0.0 collective-permute-done.5
  49.7 6.3 %collective-permute-done.6 = bf16[4,2,128,128]{3,2,1,0:T(8,128)(2,1)S(1)} collective-permute-done((bf16[4,2,128,128]{3,2,1,0:T(8,128)(2,1)S(1)}, bf16[4,2,128,128]{3,2,1,0:T(8,128)(2,1)S(1)}, u32[]{:S(2)}, u32[]{:S(2)}) %collective-permute-start.6) | collective-permute-done | bytes 262176 | tf_op jit(solution)/shard_map/ppermute | solution.py:276
  56.0 0.0 copy-start
  56.0 9.2 %collective-permute-start.7 = (bf16[32,2,128,128]{3,2,1,0:T(8,128)(2,1)S(1)}, bf16[32,2,128,128]{3,2,1,0:T(8,128)(2,1)}, u32[]{:S(2)}, u32[]{:S(2)}) collective-permute-start(bf16[32,2,128,128]{3,2,1,0:T(8,128)(2,1)S(1)} %constant_dynamic-update-slice_fusion.own.own_a.own_b), channel_id=1, source_target_pairs={{0,8},{8,0},{16,24},{24,16},{32,40},{40,32},{48,56},{56,48},{64,72... | collective-permute-start | bytes 6291464 | tf_op jit(solution)/shard_map/ppermute | solution.py:278
  70.6 0.0 copy-done.4
  70.6 1.2 %fusion.1 = s32[]{:T(128)} fusion(s32[64]{0:T(128)S(1)} %copy-done.4, s32[]{:T(128)} %bitcast.12), kind=kLoop, calls=%fused_computation.25 | loop fusion | flops 191 | bytes 264 | tf_op jit(solution)/shard_map/reduce_sum | solution.py:285
  73.0 0.1 stack.99
  73.1 0.7 stack.112.where
  73.8 0.7 select_reduce_fusion.1.table
  74.5 0.0 copy-start.2
  74.5 0.0 copy-start.3
  74.5 0.0 collective-permute-done.7.other.other_a.other_b
  74.5 0.0 copy-done
  74.5 2.3 %pick.1 = bf16[2,128,128]{2,1,0:T(8,128)(2,1)} custom-call(s32[8]{0:T(128)} %stack.112.where, bf16[32,2,128,128]{3,2,1,0:T(8,128)(2,1)} %copy-done, bf16[32,2,128,128]{3,2,1,0:T(8,128)(2,1)} %collective-permute-done.7.other.other_a.other_b, bf16[32,2,128,128]{3,2,1,0:T(8,128)(2,1)} %copy-done, ...), custom_call_target="tpu_custom_call" | custom-call | flops 100000 | bytes 200000 | tf_op jit(solution)/shard_map/pick/pallas_call | solution.py:216
  76.8 7.9 %collective-permute-start.8 = (bf16[2,128,128]{2,1,0:T(8,128)(2,1)}, bf16[2,128,128]{2,1,0:T(8,128)(2,1)S(1)}, u32[]{:S(2)}, u32[]{:S(2)}) collective-permute-start(bf16[2,128,128]{2,1,0:T(8,128)(2,1)} %pick.1), channel_id=1, source_target_pairs={{0,4},{1,5},{2,6},{3,7},{4,0},{5,1},{6,2},{7,3},{8,12},{9,13},{10,... | collective-permute-start | bytes 196616 | tf_op jit(solution)/shard_map/ppermute | solution.py:304
  84.7 0.1 pad_add_fusion.place
  84.8 2.6 %collective-permute-done.8 = bf16[2,128,128]{2,1,0:T(8,128)(2,1)S(1)} collective-permute-done((bf16[2,128,128]{2,1,0:T(8,128)(2,1)}, bf16[2,128,128]{2,1,0:T(8,128)(2,1)S(1)}, u32[]{:S(2)}, u32[]{:S(2)}) %collective-permute-start.8) | collective-permute-done | bytes 65568 | tf_op jit(solution)/shard_map/ppermute | solution.py:304
  87.3 0.9 pad_maximum_fusion.near
  88.2 0.0 copy-start.5
  88.2 3.1 %collective-permute-start.9 = (bf16[2,2,128,128]{3,2,1,0:T(8,128)(2,1)S(1)}, bf16[2,2,128,128]{3,2,1,0:T(8,128)(2,1)S(1)}, u32[]{:S(2)}, u32[]{:S(2)}) collective-permute-start(bf16[2,2,128,128]{3,2,1,0:T(8,128)(2,1)S(1)} %pad_maximum_fusion.near), channel_id=1, source_target_pairs={{0,1},{1,2},{2,3},{3,0},{4,5},{5,6},{6,7},{7,4},{8,9},{9,10},{10,1... | collective-permute-start | bytes 393224 | tf_op jit(solution)/shard_map/ppermute | solution.py:306
  91.3 3.4 %collective-permute-start.10 = (bf16[2,2,128,128]{3,2,1,0:T(8,128)(2,1)S(1)}, bf16[2,2,128,128]{3,2,1,0:T(8,128)(2,1)S(1)}, u32[]{:S(2)}, u32[]{:S(2)}) collective-permute-start(bf16[2,2,128,128]{3,2,1,0:T(8,128)(2,1)S(1)} %pad_maximum_fusion.near), channel_id=1, source_target_pairs={{0,3},{1,0},{2,1},{3,2},{4,7},{5,4},{6,5},{7,6},{8,11},{9,8},{10,9... | collective-permute-start | bytes 393224 | tf_op jit(solution)/shard_map/ppermute | solution.py:307
  94.7 3.4 %collective-permute-start.11 = (bf16[2,2,128,128]{3,2,1,0:T(8,128)(2,1)S(1)}, bf16[2,2,128,128]{3,2,1,0:T(8,128)(2,1)S(1)}, u32[]{:S(2)}, u32[]{:S(2)}) collective-permute-start(bf16[2,2,128,128]{3,2,1,0:T(8,128)(2,1)S(1)} %pad_maximum_fusion.near), channel_id=1, source_target_pairs={{0,2},{1,3},{2,0},{3,1},{4,6},{5,7},{6,4},{7,5},{8,10},{9,11},{10,... | collective-permute-start | bytes 393224 | tf_op jit(solution)/shard_map/ppermute | solution.py:308
  98.2 0.0 copy-done.2
  98.2 0.0 copy-done.3
  98.2 0.0 copy-start.1
  98.2 1.6 %copy-done.1 = bf16[32,2,128,128]{3,2,1,0:T(8,128)(2,1)S(1)} copy-done((bf16[32,2,128,128]{3,2,1,0:T(8,128)(2,1)S(1)}, bf16[32,2,128,128]{3,2,1,0:T(8,128)(2,1)}, u32[]{:S(2)}) %copy-start.1) | copy-done | bytes 2097176
  99.8 20.1 %attend.1 = bf16[128,1024]{1,0:T(8,128)(2,1)} custom-call(s32[3]{0:T(128)S(1)} %pad_add_fusion.place, s32[64]{0:T(128)S(1)} %get-tuple-element.12.run_of, s32[64]{0:T(128)S(1)} %copy-done.4, bf16[128,1024]{1,0:T(8,128)(2,1)S(1)} %copy-done.3, f32[1,128]{1,0:T(1,128)S(1)} %copy-done.2, bf16[32,2,128,128]{3,2,1,0:T(8,128)(2,1)S(1)} %copy-done.1, ...), custom_call_target="tpu_custom_call" | custom-call | flops 20000000000 | bytes 5000000 | tf_op jit(solution)/shard_map/attend/pallas_call | solution.py:181
  119.9 0.0 copy-done.5
  119.9 0.0 collective-permute-done.9.right
  119.9 0.0 copy-start.6
  119.9 0.0 collective-permute-done.10.left
  119.9 0.0 copy-start.7
  119.9 0.0 collective-permute-done.11.far
  119.9 0.6 copy-done.6
  120.5 0.0 copy-done.7
  120.6 0.0 copy-start.8
  120.6 0.7 copy-done.8
  121.2 1.9 %place.1 = (bf16[2,128,128]{2,1,0:T(8,128)(2,1)}, bf16[2,128,128]{2,1,0:T(8,128)(2,1)}) custom-call(s32[8]{0:T(128)} %select_reduce_fusion.1.table, bf16[2,2,128,128]{3,2,1,0:T(8,128)(2,1)} %copy-done.5, bf16[2,2,128,128]{3,2,1,0:T(8,128)(2,1)} %copy-done.6, bf16[2,2,128,128]{3,2,1,0:T(8,128)(2,1)} %copy-done.7, bf16[2,2,128,128]{3,2,1,0:T(8,128)(2,1)} %copy-done.8), custom_call_target="tpu_custom_call" | custom-call | flops 100000 | bytes 800000 | tf_op jit(solution)/shard_map/place/pallas_call | solution.py:249
  (9 shorter events, 0.3 us)
Async XLA Ops:
  21.3 9.7 %collective-permute-start = (bf16[4,2,128,128]{3,2,1,0:T(8,128)(2,1)S(1)}, bf16[4,2,128,128]{3,2,1,0:T(8,128)(2,1)S(1)}, u32[]{:S(2)}, u32[]{:S(2)}) collective-permute-start(bf16[4,2,128,128]{3,2,1,0:T(8,128)(2,1)S(1)} %all_to_all.5), channel_id=1, source_target_pairs={{0,16},{8,24},{16,32},{24,40},{32,48},{40,56},{48,64},{56,72},{64,... | collective-permute-start | bytes 786440 | tf_op jit(solution)/shard_map/ppermute | solution.py:270
  25.3 7.6 %collective-permute-start.1 = (bf16[4,2,128,128]{3,2,1,0:T(8,128)(2,1)S(1)}, bf16[4,2,128,128]{3,2,1,0:T(8,128)(2,1)S(1)}, u32[]{:S(2)}, u32[]{:S(2)}) collective-permute-start(bf16[4,2,128,128]{3,2,1,0:T(8,128)(2,1)S(1)} %all_to_all.5), channel_id=1, source_target_pairs={{0,112},{8,120},{16,0},{24,8},{32,16},{40,24},{48,32},{56,40},{64,... | collective-permute-start | bytes 786440 | tf_op jit(solution)/shard_map/ppermute | solution.py:271
  31.0 8.3 %collective-permute-start.2 = (bf16[4,2,128,128]{3,2,1,0:T(8,128)(2,1)S(1)}, bf16[4,2,128,128]{3,2,1,0:T(8,128)(2,1)S(1)}, u32[]{:S(2)}, u32[]{:S(2)}) collective-permute-start(bf16[4,2,128,128]{3,2,1,0:T(8,128)(2,1)S(1)} %collective-permute-done), channel_id=1, source_target_pairs={{0,16},{8,24},{16,32},{24,40},{32,48},{40,56},{48,64},{56,72},{64,... | collective-permute-start | bytes 786440 | tf_op jit(solution)/shard_map/ppermute | solution.py:272
  32.9 8.4 %collective-permute-start.3 = (bf16[4,2,128,128]{3,2,1,0:T(8,128)(2,1)S(1)}, bf16[4,2,128,128]{3,2,1,0:T(8,128)(2,1)S(1)}, u32[]{:S(2)}, u32[]{:S(2)}) collective-permute-start(bf16[4,2,128,128]{3,2,1,0:T(8,128)(2,1)S(1)} %collective-permute-done.1), channel_id=1, source_target_pairs={{0,112},{8,120},{16,0},{24,8},{32,16},{40,24},{48,32},{56,40},{64,... | collective-permute-start | bytes 786440 | tf_op jit(solution)/shard_map/ppermute | solution.py:273
  37.5 33.1 %copy-start.4 = (s32[64]{0:T(128)S(1)}, s32[64]{0:T(128)}, u32[]{:S(2)}) copy-start(s32[64]{0:T(128)} %counts.1) | copy-start | bytes 772
  39.3 8.3 %collective-permute-start.4 = (bf16[4,2,128,128]{3,2,1,0:T(8,128)(2,1)S(1)}, bf16[4,2,128,128]{3,2,1,0:T(8,128)(2,1)S(1)}, u32[]{:S(2)}, u32[]{:S(2)}) collective-permute-start(bf16[4,2,128,128]{3,2,1,0:T(8,128)(2,1)S(1)} %collective-permute-done.2), channel_id=1, source_target_pairs={{0,16},{8,24},{16,32},{24,40},{32,48},{40,56},{48,64},{56,72},{64,... | collective-permute-start | bytes 786440 | tf_op jit(solution)/shard_map/ppermute | solution.py:274
  41.3 8.3 %collective-permute-start.5 = (bf16[4,2,128,128]{3,2,1,0:T(8,128)(2,1)S(1)}, bf16[4,2,128,128]{3,2,1,0:T(8,128)(2,1)S(1)}, u32[]{:S(2)}, u32[]{:S(2)}) collective-permute-start(bf16[4,2,128,128]{3,2,1,0:T(8,128)(2,1)S(1)} %collective-permute-done.3), channel_id=1, source_target_pairs={{0,112},{8,120},{16,0},{24,8},{32,16},{40,24},{48,32},{56,40},{64,... | collective-permute-start | bytes 786440 | tf_op jit(solution)/shard_map/ppermute | solution.py:275
  47.6 8.3 %collective-permute-start.6 = (bf16[4,2,128,128]{3,2,1,0:T(8,128)(2,1)S(1)}, bf16[4,2,128,128]{3,2,1,0:T(8,128)(2,1)S(1)}, u32[]{:S(2)}, u32[]{:S(2)}) collective-permute-start(bf16[4,2,128,128]{3,2,1,0:T(8,128)(2,1)S(1)} %collective-permute-done.4), channel_id=1, source_target_pairs={{0,16},{8,24},{16,32},{24,40},{32,48},{40,56},{48,64},{56,72},{64,... | collective-permute-start | bytes 786440 | tf_op jit(solution)/shard_map/ppermute | solution.py:276
  56.0 18.5 %copy-start = (bf16[32,2,128,128]{3,2,1,0:T(8,128)(2,1)}, bf16[32,2,128,128]{3,2,1,0:T(8,128)(2,1)S(1)}, u32[]{:S(2)}) copy-start(bf16[32,2,128,128]{3,2,1,0:T(8,128)(2,1)S(1)} %constant_dynamic-update-slice_fusion.own.own_a.own_b) | copy-start | bytes 6291460
  56.0 18.5 %collective-permute-start.7 = (bf16[32,2,128,128]{3,2,1,0:T(8,128)(2,1)S(1)}, bf16[32,2,128,128]{3,2,1,0:T(8,128)(2,1)}, u32[]{:S(2)}, u32[]{:S(2)}) collective-permute-start(bf16[32,2,128,128]{3,2,1,0:T(8,128)(2,1)S(1)} %constant_dynamic-update-slice_fusion.own.own_a.own_b), channel_id=1, source_target_pairs={{0,8},{8,0},{16,24},{24,16},{32,40},{40,32},{48,56},{56,48},{64,72... | collective-permute-start | bytes 6291464 | tf_op jit(solution)/shard_map/ppermute | solution.py:278
  74.5 23.7 %copy-start.2 = (f32[1,128]{1,0:T(1,128)S(1)}, f32[1,128]{1,0:T(1,128)}, u32[]{:S(2)}) copy-start(f32[1,128]{1,0:T(1,128)} %constant.190.clone.freq) | copy-start | bytes 1540
  74.5 23.7 %copy-start.3 = (bf16[128,1024]{1,0:T(8,128)(2,1)S(1)}, bf16[128,1024]{1,0:T(8,128)(2,1)}, u32[]{:S(2)}) copy-start(bf16[128,1024]{1,0:T(8,128)(2,1)} %queries.1) | copy-start | bytes 786436
  76.8 10.6 %collective-permute-start.8 = (bf16[2,128,128]{2,1,0:T(8,128)(2,1)}, bf16[2,128,128]{2,1,0:T(8,128)(2,1)S(1)}, u32[]{:S(2)}, u32[]{:S(2)}) collective-permute-start(bf16[2,128,128]{2,1,0:T(8,128)(2,1)} %pick.1), channel_id=1, source_target_pairs={{0,4},{1,5},{2,6},{3,7},{4,0},{5,1},{6,2},{7,3},{8,12},{9,13},{10,... | collective-permute-start | bytes 196616 | tf_op jit(solution)/shard_map/ppermute | solution.py:304
  88.2 31.7 %copy-start.5 = (bf16[2,2,128,128]{3,2,1,0:T(8,128)(2,1)}, bf16[2,2,128,128]{3,2,1,0:T(8,128)(2,1)S(1)}, u32[]{:S(2)}) copy-start(bf16[2,2,128,128]{3,2,1,0:T(8,128)(2,1)S(1)} %pad_maximum_fusion.near) | copy-start | bytes 393220
  88.2 31.7 %collective-permute-start.9 = (bf16[2,2,128,128]{3,2,1,0:T(8,128)(2,1)S(1)}, bf16[2,2,128,128]{3,2,1,0:T(8,128)(2,1)S(1)}, u32[]{:S(2)}, u32[]{:S(2)}) collective-permute-start(bf16[2,2,128,128]{3,2,1,0:T(8,128)(2,1)S(1)} %pad_maximum_fusion.near), channel_id=1, source_target_pairs={{0,1},{1,2},{2,3},{3,0},{4,5},{5,6},{6,7},{7,4},{8,9},{9,10},{10,1... | collective-permute-start | bytes 393224 | tf_op jit(solution)/shard_map/ppermute | solution.py:306
  91.3 28.6 %collective-permute-start.10 = (bf16[2,2,128,128]{3,2,1,0:T(8,128)(2,1)S(1)}, bf16[2,2,128,128]{3,2,1,0:T(8,128)(2,1)S(1)}, u32[]{:S(2)}, u32[]{:S(2)}) collective-permute-start(bf16[2,2,128,128]{3,2,1,0:T(8,128)(2,1)S(1)} %pad_maximum_fusion.near), channel_id=1, source_target_pairs={{0,3},{1,0},{2,1},{3,2},{4,7},{5,4},{6,5},{7,6},{8,11},{9,8},{10,9... | collective-permute-start | bytes 393224 | tf_op jit(solution)/shard_map/ppermute | solution.py:307
  94.7 25.2 %collective-permute-start.11 = (bf16[2,2,128,128]{3,2,1,0:T(8,128)(2,1)S(1)}, bf16[2,2,128,128]{3,2,1,0:T(8,128)(2,1)S(1)}, u32[]{:S(2)}, u32[]{:S(2)}) collective-permute-start(bf16[2,2,128,128]{3,2,1,0:T(8,128)(2,1)S(1)} %pad_maximum_fusion.near), channel_id=1, source_target_pairs={{0,2},{1,3},{2,0},{3,1},{4,6},{5,7},{6,4},{7,5},{8,10},{9,11},{10,... | collective-permute-start | bytes 393224 | tf_op jit(solution)/shard_map/ppermute | solution.py:308
  98.2 1.6 %copy-start.1 = (bf16[32,2,128,128]{3,2,1,0:T(8,128)(2,1)S(1)}, bf16[32,2,128,128]{3,2,1,0:T(8,128)(2,1)}, u32[]{:S(2)}) copy-start(bf16[32,2,128,128]{3,2,1,0:T(8,128)(2,1)} %copy-done) | copy-start | bytes 6291460
  119.9 0.7 copy-start.6
  119.9 0.7 copy-start.7
  120.6 0.7 copy-start.8

commit v2 on v1

v2 whole, which is shorter than its diff:
```python
import functools
import math

import jax
import jax.numpy as jnp
import numpy as np
from jax import lax
from jax.experimental import pallas as pl
from jax.experimental.pallas import tpu as pltpu
from jax.sharding import PartitionSpec as P

KVH = 8
HD = 128
PAGE = 128
HALF = 64
ROWS = 128
N_CP = 64
N_Z = 4
N_Y = 8
N_TP = 8
N_X = 4
SRC = N_CP // 2
FIRST = 28
REST = N_CP - FIRST
LANES = 128
RUNS = 2 * N_CP
BIG = 1e30

THETA = 500000.0
FREQ = np.concatenate([THETA ** (-np.arange(HALF) * 2.0 / HD)] * 2).astype(np.float32)[None, :]
OFFSETS = (0, -1, 1, -2, 2, -3, 3, 4)
BIG_GRANT = 24 * 2**20


def cp_index(z, y, core):
    return ((z % N_Z) * N_Y + y % N_Y) * 2 + core


def cp_pairs(step):
    return [
        (cp_index(z, y, c), cp_index(z, y + step, c))
        for z in range(N_Z)
        for y in range(N_Y)
        for c in range(2)
    ]


CORE_PAIRS = [(i, i ^ 1) for i in range(N_CP)]
Z_GROUPS = [[cp_index(z, y, c) for z in range(N_Z)] for y in range(N_Y) for c in range(2)]
ZHI_PAIRS = [(i, (i + N_X) % N_TP) for i in range(N_TP)]


def x_pairs(step):
    return [(i, (i // N_X) * N_X + (i + step) % N_X) for i in range(N_TP)]


def angles_of(freq, first_run, second_run, rows):
    row = lax.broadcasted_iota(jnp.int32, (rows, HD), 0)
    pos = jnp.where(row < HALF, first_run * HALF + row, second_run * HALF + row - HALF)
    angles = pos.astype(jnp.float32) * freq
    low = lax.broadcasted_iota(jnp.int32, (rows, HD), 1) < HALF
    sin = jnp.sin(angles)
    return jnp.cos(angles), jnp.where(low, -sin, sin)


def turned(x, cos, sin):
    return x * cos + pltpu.roll(x, HALF, 1) * sin


SMEM = pl.BlockSpec(memory_space=pltpu.SMEM)
VMEM = pl.BlockSpec(memory_space=pltpu.VMEM)
ANY = pl.BlockSpec(memory_space=pl.ANY)


def coordinates():
    me = lax.axis_index("cp")
    return me, lax.div(me, 2 * N_Y), lax.rem(lax.div(me, 2), N_Y), lax.rem(me, 2)


def pack_kernel(positions, keys, values, freq, out):
    first = lax.div(positions[lax.axis_index("cp") * ROWS], HALF)
    cos, sin = angles_of(freq[...], first, RUNS - 1 - first, ROWS)
    k_rot = turned(keys[...].astype(jnp.float32), cos, sin).astype(jnp.bfloat16)
    out[0] = k_rot
    out[1] = values[...]


def pack(positions, keys, values):
    return pl.pallas_call(
        pack_kernel,
        out_shape=jax.ShapeDtypeStruct((2, ROWS, HD), jnp.bfloat16),
        in_specs=[SMEM, VMEM, VMEM, VMEM],
        out_specs=VMEM,
        cost_estimate=pl.CostEstimate(flops=1_000_000, bytes_accessed=400_000, transcendentals=0),
        name="pack",
    )(positions, keys, values, jnp.asarray(FREQ))


def turn_kernel(positions, queries, freq, unit, q_rot):
    del unit
    my_run = lax.div(positions[lax.axis_index("cp") * ROWS], HALF)
    cos, sin = angles_of(freq[...], my_run, RUNS - 1 - my_run, ROWS)
    for h in range(KVH):
        q = turned(queries[:, h * HD : (h + 1) * HD].astype(jnp.float32), cos, sin)
        q = q.astype(jnp.bfloat16)
        q_rot[0, h * HALF : (h + 1) * HALF, :] = q[:HALF]
        q_rot[1, h * HALF : (h + 1) * HALF, :] = q[HALF:]


def turn(positions, queries, unit):
    return pl.pallas_call(
        turn_kernel,
        out_shape=jax.ShapeDtypeStruct((2, KVH * HALF, HD), jnp.bfloat16),
        in_specs=[SMEM, VMEM, VMEM, ANY],
        out_specs=VMEM,
        compiler_params=pltpu.CompilerParams(vmem_limit_bytes=BIG_GRANT),
        cost_estimate=pl.CostEstimate(flops=2_000_000, bytes_accessed=600_000, transcendentals=0),
        name="turn",
    )(positions, queries, jnp.asarray(FREQ), unit)


LIST_ROWS = ((0, 1), (2, 3))
MISC = 4
AT_COUNT, AT_RUN = 0, 4


def clip_valid(counts, run):
    return jnp.clip(counts[lax.shift_right_logical(run, 1)] - (run & 1) * HALF, 0, HALF)


def lists_kernel(positions, counts, after, table):
    del after
    me, _, y_me, core = coordinates()
    my_run = lax.shift_right_logical(positions[me * ROWS], 6)
    places = [((y_me + (off + N_Y)) & (N_Y - 1)) * 2 for off in OFFSETS]

    for part in range(2):
        if part == 0:
            blocks = [(0, b) for b in range(FIRST)]
        else:
            blocks = [(0, b) for b in range(FIRST, SRC)] + [(1, b) for b in range(SRC)]
        n_low, n_high = jnp.int32(0), jnp.int32(0)
        low, high = LIST_ROWS[part]
        for b, (side, at) in enumerate(blocks):
            src = at % N_Z * 2 * N_Y + places[at // N_Z] + (core if side == 0 else 1 - core)
            run = lax.shift_right_logical(positions[src * ROWS], 6)
            first = b * 256 + clip_valid(counts, run)
            second = b * 256 + 128 + clip_valid(counts, RUNS - 1 - run)
            table[high, n_high] = first
            n_high = n_high + 1
            table[high, n_high] = second
            n_high = n_high + (run > my_run).astype(jnp.int32)
            table[low, n_low] = first
            n_low = n_low + (run < my_run).astype(jnp.int32)
        for r in range(16):
            table[low, n_low + r] = 0
            table[high, n_high + r] = 0
        table[MISC, AT_COUNT + low] = n_low
        table[MISC, AT_COUNT + high] = n_high
    table[MISC, AT_RUN] = my_run


def lists(positions, counts, after):
    return pl.pallas_call(
        lists_kernel,
        out_shape=jax.ShapeDtypeStruct((8, LANES), jnp.int32),
        in_specs=[SMEM, SMEM, ANY],
        out_specs=SMEM,
        compiler_params=pltpu.CompilerParams(vmem_limit_bytes=BIG_GRANT),
        cost_estimate=pl.CostEstimate(flops=2_000_000, bytes_accessed=300_000, transcendentals=0),
        name="lists",
    )(positions, counts, after)


AT_PICK, AT_PLACE = 0, 8


def route_kernel(positions, counts, owner_row, owner_col, owner_slot, after, table):
    del after
    me, _, y_me, core = coordinates()
    tp = lax.axis_index("tp")

    def page_of(head):
        page = jnp.int32(0)
        for p in range(N_CP):
            page = jnp.where(owner_row[head, p] == me, p, page)
        return page

    page = page_of(tp)
    for half in range(2):
        run = page * 2 + half
        second = run >= N_CP
        j = jnp.where(second, RUNS - 1 - run, run)
        src = jnp.int32(0)
        for s in range(N_CP):
            src = jnp.where(lax.shift_right_logical(positions[s * ROWS], 6) == j, s, src)
        off = (lax.shift_right_logical(src, 1) - y_me) & (N_Y - 1)
        order = jnp.where(off < N_Y // 2, 2 * off, 2 * (N_Y - off) - 1)
        at = AT_PICK + 4 * half
        table[at] = ((src & 1) != core).astype(jnp.int32)
        table[at + 1] = order * N_Z + lax.shift_right_logical(src, 4)
        table[at + 2] = second.astype(jnp.int32)
        table[at + 3] = clip_valid(counts, run)

    hi, x = lax.div(tp, N_X), lax.rem(tp, N_X)
    for i, step in enumerate((0, 1, -1, 2)):
        for d in range(2):
            head = lax.rem(hi + d, 2) * N_X + lax.rem(x - step + N_X, N_X)
            p = page_of(head)
            mine = owner_col[head, p] == tp
            table[AT_PLACE + i * 2 + d] = jnp.where(mine, owner_slot[head, p], -1)


def route(positions, counts, owner_row, owner_col, owner_slot, after):
    return pl.pallas_call(
        route_kernel,
        out_shape=jax.ShapeDtypeStruct((LANES,), jnp.int32),
        in_specs=[SMEM, SMEM, SMEM, SMEM, SMEM, ANY],
        out_specs=SMEM,
        compiler_params=pltpu.CompilerParams(vmem_limit_bytes=BIG_GRANT),
        cost_estimate=pl.CostEstimate(flops=2_000_000, bytes_accessed=300_000, transcendentals=0),
        name="route",
    )(positions, counts, owner_row, owner_col, owner_slot, after)


COLS = KVH * HALF
SCALE = math.log2(math.e) / math.sqrt(HD)
dot = functools.partial(lax.dot_general, preferred_element_type=jnp.float32)


def fold(q, keys, vals, bias, allowed, state):
    top, total, acc = state
    s = dot(keys, q, (((1,), (1,)), ((), ()))) * SCALE
    s = s + jnp.concatenate([bias] * (COLS // HD), axis=1)
    if allowed is not None:
        s = jnp.where(allowed, s, -BIG)
    new_top = jnp.maximum(top, jnp.max(s, axis=0, keepdims=True))
    factor = jnp.exp2(top - new_top)
    w = jnp.exp2(s - new_top)
    total = total * factor + jnp.sum(w, axis=0, keepdims=True)
    acc = acc * factor + dot(vals, w.astype(jnp.bfloat16), (((0,), (0,)), ((), ())))
    return new_top, total, acc


def bias_of(valid):
    return jnp.where(lax.broadcasted_iota(jnp.int32, (HALF, HD), 0) < valid, 0.0, -BIG)


def fold_list(table, row, q, kv, state):
    def chunk(size, start, state):
        ks, vs, biases = [], [], []
        for r in range(size):
            code = table[row, start + r]
            b = lax.shift_right_logical(code, 8)
            rows = pl.ds(pl.multiple_of(lax.shift_right_logical(code & 128, 1), HALF), HALF)
            ks.append(kv[b, 0, rows, :])
            vs.append(kv[b, 1, rows, :])
            biases.append(bias_of(code & 127))
        return fold(
            q,
            jnp.concatenate(ks, axis=0),
            jnp.concatenate(vs, axis=0),
            jnp.concatenate(biases, axis=0),
            None,
            state,
        )

    count = table[MISC, AT_COUNT + row]
    wide = lax.shift_right_logical(count + 7, 4)
    state = lax.fori_loop(0, wide, lambda i, st: chunk(16, i * 16, st), state)
    narrow = (count > wide * 16).astype(jnp.int32)
    return lax.fori_loop(0, narrow, lambda i, st: chunk(8, wide * 16, st), state)


def first_kernel(table, counts, q_rot, own, tops, totals, accs, kv, sem):
    copy = pltpu.make_async_copy(own, kv, sem)
    copy.start()
    _, z_me, _, _ = coordinates()
    my_run = table[MISC, AT_RUN]
    copy.wait()
    key = lax.broadcasted_iota(jnp.int32, (HALF, COLS), 0)
    row = lax.broadcasted_iota(jnp.int32, (HALF, COLS), 1) & (HALF - 1)
    for part in range(2):
        q = q_rot[part]
        state = (
            jnp.full((1, COLS), -BIG, jnp.float32),
            jnp.zeros((1, COLS), jnp.float32),
            jnp.zeros((HD, COLS), jnp.float32),
        )
        run = my_run if part == 0 else RUNS - 1 - my_run
        page = lax.shift_right_logical(run, 1)
        valid = jnp.clip(counts[page] - (run & 1) * HALF, 0, HALF)
        rows = slice(part * HALF, (part + 1) * HALF)
        state = fold(q, kv[z_me, 0, rows], kv[z_me, 1, rows], bias_of(valid), key <= row, state)
        state = fold_list(table, LIST_ROWS[0][part], q, kv, state)
        tops[part], totals[part], accs[part] = state


STATE = (
    jax.ShapeDtypeStruct((2, 1, COLS), jnp.float32),
    jax.ShapeDtypeStruct((2, 1, COLS), jnp.float32),
    jax.ShapeDtypeStruct((2, HD, COLS), jnp.float32),
)


def attend_first(table, counts, q_rot, own):
    return pl.pallas_call(
        first_kernel,
        out_shape=STATE,
        in_specs=[SMEM, SMEM, VMEM, ANY],
        out_specs=(VMEM, VMEM, VMEM),
        scratch_shapes=[
            pltpu.VMEM((FIRST, 2, ROWS, HD), jnp.bfloat16),
            pltpu.SemaphoreType.DMA,
        ],
        compiler_params=pltpu.CompilerParams(vmem_limit_bytes=BIG_GRANT),
        cost_estimate=pl.CostEstimate(
            flops=6_000_000_000, bytes_accessed=3_000_000, transcendentals=2_000_000
        ),
        name="attend_first",
    )(table, counts, q_rot, own)


def rest_kernel(table, q_rot, tops, totals, accs, own, other, out, kv, sems):
    copies = [
        pltpu.make_async_copy(
            own.at[pl.ds(FIRST, SRC - FIRST)], kv.at[pl.ds(0, SRC - FIRST)], sems.at[0]
        ),
        pltpu.make_async_copy(other, kv.at[pl.ds(SRC - FIRST, SRC)], sems.at[1]),
    ]
    for copy in copies:
        copy.start()
    for copy in copies:
        copy.wait()
    for part in range(2):
        state = tops[part], totals[part], accs[part]
        _, total, acc = fold_list(table, LIST_ROWS[1][part], q_rot[part], kv, state)
        res = jnp.transpose(acc / total).astype(jnp.bfloat16)
        for h in range(KVH):
            out[part * HALF : (part + 1) * HALF, h * HD : (h + 1) * HD] = res[
                h * HALF : (h + 1) * HALF
            ]


def attend_rest(table, q_rot, state, own, other):
    return pl.pallas_call(
        rest_kernel,
        out_shape=jax.ShapeDtypeStruct((ROWS, KVH * HD), jnp.bfloat16),
        in_specs=[SMEM, VMEM, VMEM, VMEM, VMEM, ANY, ANY],
        out_specs=VMEM,
        scratch_shapes=[
            pltpu.VMEM((REST, 2, ROWS, HD), jnp.bfloat16),
            pltpu.SemaphoreType.DMA((2,)),
        ],
        compiler_params=pltpu.CompilerParams(vmem_limit_bytes=BIG_GRANT),
        cost_estimate=pl.CostEstimate(
            flops=8_000_000_000, bytes_accessed=4_000_000, transcendentals=2_000_000
        ),
        name="attend_rest",
    )(table, q_rot, *state, own, other)


def pick_kernel(table, own, other, out, near, held, sems):
    for half in range(2):
        at = AT_PICK + 4 * half
        side, index, second = (table[at + i] for i in range(3))
        rows = pl.ds(pl.multiple_of(second * HALF, HALF), HALF)
        for is_other, blocks in ((0, own), (1, other)):

            @pl.when(side == is_other)
            def _(blocks=blocks, half=half, index=index, rows=rows):
                pltpu.make_async_copy(
                    blocks.at[index, :, rows], held.at[half], sems.at[half]
                ).start()

    row = lax.broadcasted_iota(jnp.int32, (HALF, HD), 0)
    for half in range(2):
        pltpu.make_async_copy(own.at[0, :, pl.ds(0, HALF)], held.at[half], sems.at[half]).wait()
        keep = row < table[AT_PICK + 4 * half + 3]
        for i in range(2):
            block = jnp.where(keep, held[half, i].astype(jnp.float32), 0.0).astype(jnp.bfloat16)
            out[i, half * HALF : (half + 1) * HALF, :] = block
            near[0, i, half * HALF : (half + 1) * HALF, :] = block


def pick(table, own, other):
    return pl.pallas_call(
        pick_kernel,
        out_shape=(
            jax.ShapeDtypeStruct((2, PAGE, HD), jnp.bfloat16),
            jax.ShapeDtypeStruct((2, 2, PAGE, HD), jnp.bfloat16),
        ),
        in_specs=[SMEM, ANY, ANY],
        out_specs=(VMEM, VMEM),
        scratch_shapes=[
            pltpu.VMEM((2, 2, HALF, HD), jnp.bfloat16),
            pltpu.SemaphoreType.DMA((2,)),
        ],
        compiler_params=pltpu.CompilerParams(vmem_limit_bytes=BIG_GRANT),
        cost_estimate=pl.CostEstimate(flops=100_000, bytes_accessed=300_000, transcendentals=0),
        name="pick",
    )(table, own, other)


def place_kernel(table, near, right, left, far, pool_k, pool_v, sems):
    for slot in range(2):
        empty = True
        for i, pages in enumerate((near, right, left, far)):
            for hi in range(2):
                hit = table[AT_PLACE + i * 2 + hi] == slot
                empty = jnp.logical_and(empty, jnp.logical_not(hit))

                @pl.when(hit)
                def _(pages=pages, hi=hi, slot=slot):
                    pltpu.make_async_copy(pages.at[hi, 0], pool_k.at[slot], sems.at[slot, 0]).start()
                    pltpu.make_async_copy(pages.at[hi, 1], pool_v.at[slot], sems.at[slot, 1]).start()

        @pl.when(empty)
        def _(slot=slot):
            pool_k[slot] = jnp.zeros((PAGE, HD), jnp.bfloat16)
            pool_v[slot] = jnp.zeros((PAGE, HD), jnp.bfloat16)

        @pl.when(jnp.logical_not(empty))
        def _(slot=slot):
            pltpu.make_async_copy(near.at[0, 0], pool_k.at[slot], sems.at[slot, 0]).wait()
            pltpu.make_async_copy(near.at[0, 1], pool_v.at[slot], sems.at[slot, 1]).wait()


def place(table, near, right, left, far):
    shape = jax.ShapeDtypeStruct((2, PAGE, HD), jnp.bfloat16)
    return pl.pallas_call(
        place_kernel,
        out_shape=(shape, shape),
        in_specs=[SMEM, ANY, ANY, ANY, ANY],
        out_specs=(VMEM, VMEM),
        scratch_shapes=[pltpu.SemaphoreType.DMA((2, 2))],
        compiler_params=pltpu.CompilerParams(vmem_limit_bytes=BIG_GRANT),
        cost_estimate=pl.CostEstimate(flops=100_000, bytes_accessed=800_000, transcendentals=0),
        name="place",
    )(table, near, right, left, far)


def shards(queries, keys, values, positions, counts, owner_row, owner_col, owner_slot):
    tie = lax.optimization_barrier
    ahead, back = cp_pairs(1), cp_pairs(-1)
    packed = pack(positions, keys, values)
    spread = jnp.broadcast_to(packed, (N_Z, 2, ROWS, HD))
    unit = lax.all_to_all(spread, "cp", 0, 0, axis_index_groups=Z_GROUPS)

    f1 = lax.ppermute(unit, "cp", ahead)
    b1 = lax.ppermute(unit, "cp", back)
    f1, q_rot = tie((f1, turn(positions, queries, unit)))
    f2 = lax.ppermute(f1, "cp", ahead)
    b2 = lax.ppermute(b1, "cp", back)
    f2, table = tie((f2, lists(positions, counts, f1)))
    f3 = lax.ppermute(f2, "cp", ahead)
    b3 = lax.ppermute(b2, "cp", back)
    f3, routes = tie((f3, route(positions, counts, owner_row, owner_col, owner_slot, f2)))
    f4 = lax.ppermute(f3, "cp", ahead)
    state = attend_first(
        table, counts, q_rot, jnp.concatenate([unit, f1, b1, f2, b2, f3, b3], axis=0)
    )
    f4, state = tie((f4, state))
    own = jnp.concatenate([unit, f1, b1, f2, b2, f3, b3, f4], axis=0)
    other = lax.ppermute(own, "cp", CORE_PAIRS)

    picked, near = pick(routes, own, other)
    across = lax.ppermute(picked, "tp", ZHI_PAIRS)
    attended = attend_rest(table, q_rot, state, own, other)
    across, attended = tie((across, attended))
    near = lax.dynamic_update_slice(near, across[None], (1, 0, 0, 0))
    right = lax.ppermute(near, "tp", x_pairs(1))
    left = lax.ppermute(near, "tp", x_pairs(-1))
    far = lax.ppermute(near, "tp", x_pairs(2))
    pool_keys, pool_values = place(routes, near, right, left, far)
    return attended, pool_keys, pool_values


def solution(mesh):
    return jax.shard_map(
        shards,
        mesh=mesh,
        in_specs=(P("cp", "tp"), P("cp", "tp"), P("cp", "tp"), P(), P(), P(), P(), P()),
        out_specs=(P("cp", "tp"), P(("cp", "tp"), None, None), P(("cp", "tp"), None, None)),
        check_vma=False,
    )
```

time: 124 us -> 102 us (0.82)
  between operations: 8.19 us -> 0.98 us
  other arithmetic: 4.46 us -> 0 us
  waiting for transfers between devices: 14.1 us -> 9.96 us
  starting transfers between devices: 49.8 us -> 47.4 us
  Pallas kernels: 26.7 us -> 24.4 us
  local copies, waits for them, and re-layouts: 6.08 us -> 4.18 us
    ppermute x1, waiting for transfers between devices: 6.26 us -> 0.01 us  [shards(): f4 = lax.ppermute(f3, 'cp', ahead)]
    ppermute x1, waiting for transfers between devices: 0.01 us -> 3.76 us  [shards(): other = lax.ppermute(own, 'cp', CORE_PAIRS)]
    reduce_sum x4 -> x0, other arithmetic: 3.52 us -> none  [the longest x1 1.25 us: shards(): valid = jnp.sum(jnp.where(jnp.arange(N_CP) == page, counts, 0))]
    ppermute x1, waiting for transfers between devices: 0.01 us -> 3.24 us  [shards(): right = lax.ppermute(near, 'tp', x_pairs(1))]
    ppermute x1, waiting for transfers between devices: 0.01 us -> 2.92 us  [shards(): far = lax.ppermute(near, 'tp', x_pairs(2))]
    ppermute x1, waiting for transfers between devices: 2.57 us -> 0.01 us  [shards(): across = lax.ppermute(picked, 'tp', ZHI_PAIRS)]
    pallas_call x4 -> x8, Pallas kernels: 26.7 us -> 24.4 us  [the longest x1 7.06 us: attend_rest(): pl.pallas_call(rest_kernel, out_shape=jax.ShapeDtypeStruct((ROWS, KVH * H...]
    ppermute x1, waiting for transfers between devices: 1.82 us -> 0.01 us  [shards(): f1 = lax.ppermute(unit, 'cp', ahead)]
  transfers between devices with their start and end apart: 12 -> 12, of which waited for: 5 -> 3; matrix products, arithmetic and copies ran while one was open for 2% -> 1% of each run, Pallas kernels for 16% -> 20%
where the time goes in v2:
time: 102 us; the launch traced here: 101 us
  starting transfers between devices  47.4 us (46%)
  Pallas kernels  24.4 us (24%)
  blocking collectives  13.8 us (14%)
  waiting for transfers between devices  9.96 us (10%)
  local copies, waits for them, and re-layouts  4.18 us (4%)
    all_to_all x1, blocking collectives, shards(): unit = lax.all_to_all(spread, 'cp', 0, 0, axis_index_groups=Z_GROUPS)  13.8 us
    ppermute x1, starting transfers between devices, shards(): across = lax.ppermute(picked, 'tp', ZHI_PAIRS)  7.94 us
    ppermute x1, starting transfers between devices, shards(): other = lax.ppermute(own, 'cp', CORE_PAIRS)  7.4 us
    pallas_call x1, Pallas kernels, attend_rest(): pl.pallas_call(rest_kernel, out_shape=jax.ShapeDtypeStruct((ROWS, KVH * H...  7.06 us
    pallas_call x1, Pallas kernels, attend_first(): pl.pallas_call(first_kernel, out_shape=STATE, in_specs=[SMEM, SMEM, VMEM,...  6.08 us
    ppermute x1, starting transfers between devices, shards(): b2 = lax.ppermute(b1, 'cp', back)  4.57 us
    ppermute x1, starting transfers between devices, shards(): b3 = lax.ppermute(b2, 'cp', back)  4.57 us
    ppermute x1, starting transfers between devices, shards(): left = lax.ppermute(near, 'tp', x_pairs(-1))  4.39 us
  transfers between devices with their start and end apart: 12, of which 3 were waited for; matrix products, arithmetic and copies ran while one was open for 1% of the time, Pallas kernels for 20%

profile of v2, /device:TPU:1, one launch (start us, length us, event | category | flops | bytes accessed | tf_op | source)
XLA Modules:
  0.0 100.8 jit_solution(13116808939201268502)
XLA Ops:
  0.6 0.0 copy-start.5
  0.6 2.2 %pack.1 = bf16[2,128,128]{2,1,0:T(8,128)(2,1)} custom-call(s32[8192]{0:T(1024)} %positions.7, bf16[128,128]{1,0:T(8,128)(2,1)} %keys.1, bf16[128,128]{1,0:T(8,128)(2,1)} %values.1, f32[1,128]{1,0:T(1,128)} %constant.6.clone.freq), custom_call_target="tpu_custom_call" | custom-call | flops 1000000 | bytes 400000 | tf_op jit(solution)/shard_map/pack/pallas_call | solution.py:89
  2.9 0.9 broadcast_in_dim.6
  3.8 0.0 copy-start.2
  3.8 0.0 copy-start.3
  3.8 0.0 copy-start.4
  3.8 13.8 %all_to_all.5.unit = bf16[4,2,128,128]{3,2,1,0:T(8,128)(2,1)S(1)} all-to-all(bf16[4,2,128,128]{3,2,1,0:T(8,128)(2,1)S(1)} %broadcast_in_dim.6), channel_id=1, replica_groups={{0,128,256,384},{8,136,264,392},{16,144,272,400},{24,152,280,408},{32,1..., dimensions={0} | all-to-all | bytes 524288 | tf_op jit(solution)/shard_map/all_to_all | solution.py:448
  17.6 4.0 %collective-permute-start = (bf16[4,2,128,128]{3,2,1,0:T(8,128)(2,1)S(1)}, bf16[4,2,128,128]{3,2,1,0:T(8,128)(2,1)S(1)}, u32[]{:S(2)}, u32[]{:S(2)}) collective-permute-start(bf16[4,2,128,128]{3,2,1,0:T(8,128)(2,1)S(1)} %all_to_all.5.unit), channel_id=1, source_target_pairs={{0,16},{8,24},{16,32},{24,40},{32,48},{40,56},{48,64},{56,72},{64,... | collective-permute-start | bytes 786440 | tf_op jit(solution)/shard_map/ppermute | solution.py:450
  21.6 3.8 %collective-permute-start.3 = (bf16[4,2,128,128]{3,2,1,0:T(8,128)(2,1)S(1)}, bf16[4,2,128,128]{3,2,1,0:T(8,128)(2,1)S(1)}, u32[]{:S(2)}, u32[]{:S(2)}) collective-permute-start(bf16[4,2,128,128]{3,2,1,0:T(8,128)(2,1)S(1)} %all_to_all.5.unit), channel_id=1, source_target_pairs={{0,112},{8,120},{16,0},{24,8},{32,16},{40,24},{48,32},{56,40},{64,... | collective-permute-start | bytes 786440 | tf_op jit(solution)/shard_map/ppermute | solution.py:451
  25.4 0.0 copy-start
  25.5 0.7 copy-done
  26.2 0.0 copy-start.1
  26.2 0.9 copy-done.1
  27.2 0.0 copy-start.6
  27.2 0.7 copy-done.6
  27.8 1.4 %turn.1.q_rot = bf16[2,512,128]{2,1,0:T(8,128)(2,1)S(1)} custom-call(s32[8192]{0:T(1024)S(1)} %copy-done, bf16[128,1024]{1,0:T(8,128)(2,1)S(1)} %copy-done.1, f32[1,128]{1,0:T(1,128)S(1)} %copy-done.6, bf16[4,2,128,128]{3,2,1,0:T(8,128)(2,1)S(1)} %all_to_all.5.unit), custom_call_target="tpu_custom_call" | custom-call | flops 2000000 | bytes 600000 | tf_op jit(solution)/shard_map/turn/pallas_call | solution.py:111
  29.3 0.0 collective-permute-done.after
  29.3 1.9 %collective-permute-start.1 = (bf16[4,2,128,128]{3,2,1,0:T(8,128)(2,1)S(1)}, bf16[4,2,128,128]{3,2,1,0:T(8,128)(2,1)S(1)}, u32[]{:S(2)}, u32[]{:S(2)}) collective-permute-start(bf16[4,2,128,128]{3,2,1,0:T(8,128)(2,1)S(1)} %collective-permute-done.after), channel_id=1, source_target_pairs={{0,16},{8,24},{16,32},{24,40},{32,48},{40,56},{48,64},{56,72},{64,... | collective-permute-start | bytes 786440 | tf_op jit(solution)/shard_map/ppermute | solution.py:453
  31.2 0.0 collective-permute-done.3
  31.2 4.6 %collective-permute-start.4 = (bf16[4,2,128,128]{3,2,1,0:T(8,128)(2,1)S(1)}, bf16[4,2,128,128]{3,2,1,0:T(8,128)(2,1)S(1)}, u32[]{:S(2)}, u32[]{:S(2)}) collective-permute-start(bf16[4,2,128,128]{3,2,1,0:T(8,128)(2,1)S(1)} %collective-permute-done.3), channel_id=1, source_target_pairs={{0,112},{8,120},{16,0},{24,8},{32,16},{40,24},{48,32},{56,40},{64,... | collective-permute-start | bytes 786440 | tf_op jit(solution)/shard_map/ppermute | solution.py:454
  35.8 0.1 constant_dynamic-update-slice_fusion.6
  35.9 0.0 copy-done.5
  35.9 2.8 %lists.1.table = s32[8,128]{1,0:T(8,128)S(1)} custom-call(s32[8192]{0:T(1024)S(1)} %copy-done, s32[64]{0:T(128)S(1)} %copy-done.5, bf16[4,2,128,128]{3,2,1,0:T(8,128)(2,1)S(1)} %collective-permute-done.after), custom_call_target="tpu_custom_call" | custom-call | flops 2000000 | bytes 300000 | tf_op jit(solution)/shard_map/lists/pallas_call | solution.py:164
  38.6 0.1 constant_dynamic-update-slice_fusion.5
  38.8 0.0 collective-permute-done.1.after
  38.8 1.9 %collective-permute-start.2 = (bf16[4,2,128,128]{3,2,1,0:T(8,128)(2,1)S(1)}, bf16[4,2,128,128]{3,2,1,0:T(8,128)(2,1)S(1)}, u32[]{:S(2)}, u32[]{:S(2)}) collective-permute-start(bf16[4,2,128,128]{3,2,1,0:T(8,128)(2,1)S(1)} %collective-permute-done.1.after), channel_id=1, source_target_pairs={{0,16},{8,24},{16,32},{24,40},{32,48},{40,56},{48,64},{56,72},{64,... | collective-permute-start | bytes 786440 | tf_op jit(solution)/shard_map/ppermute | solution.py:456
  40.7 0.1 constant_dynamic-update-slice_fusion.4
  40.9 0.0 collective-permute-done.4
  40.9 4.6 %collective-permute-start.5 = (bf16[4,2,128,128]{3,2,1,0:T(8,128)(2,1)S(1)}, bf16[4,2,128,128]{3,2,1,0:T(8,128)(2,1)S(1)}, u32[]{:S(2)}, u32[]{:S(2)}) collective-permute-start(bf16[4,2,128,128]{3,2,1,0:T(8,128)(2,1)S(1)} %collective-permute-done.4), channel_id=1, source_target_pairs={{0,112},{8,120},{16,0},{24,8},{32,16},{40,24},{48,32},{56,40},{64,... | collective-permute-start | bytes 786440 | tf_op jit(solution)/shard_map/ppermute | solution.py:457
  45.5 0.1 constant_dynamic-update-slice_fusion.3
  45.6 0.0 copy-done.2
  45.6 0.0 copy-done.3
  45.6 0.0 copy-done.4
  45.6 2.7 %route.1.table = s32[128]{0:T(128)S(1)} custom-call(s32[8192]{0:T(1024)S(1)} %copy-done, s32[64]{0:T(128)S(1)} %copy-done.5, s32[8,64]{1,0:T(8,128)S(1)} %copy-done.2, s32[8,64]{1,0:T(8,128)S(1)} %copy-done.3, s32[8,64]{1,0:T(8,128)S(1)} %copy-done.4, bf16[4,2,128,128]{3,2,1,0:T(8,128)(2,1)S(1)} %collective-permute-done.1.after), custom_call_target="tpu_custom_call" | custom-call | flops 2000000 | bytes 300000 | tf_op jit(solution)/shard_map/route/pallas_call | solution.py:215
  48.4 0.1 constant_dynamic-update-slice_fusion.2
  48.5 0.0 collective-permute-done.2
  48.5 1.9 %collective-permute-start.6 = (bf16[4,2,128,128]{3,2,1,0:T(8,128)(2,1)S(1)}, bf16[4,2,128,128]{3,2,1,0:T(8,128)(2,1)S(1)}, u32[]{:S(2)}, u32[]{:S(2)}) collective-permute-start(bf16[4,2,128,128]{3,2,1,0:T(8,128)(2,1)S(1)} %collective-permute-done.2), channel_id=1, source_target_pairs={{0,16},{8,24},{16,32},{24,40},{32,48},{40,56},{48,64},{56,72},{64,... | collective-permute-start | bytes 786440 | tf_op jit(solution)/shard_map/ppermute | solution.py:459
  50.4 0.1 constant_dynamic-update-slice_fusion.1
  50.6 0.0 collective-permute-done.5
  50.6 0.1 constant_dynamic-update-slice_fusion
  50.7 6.1 %attend_first.1 = (f32[2,1,512]{2,1,0:T(1,128)S(1)}, f32[2,1,512]{2,1,0:T(1,128)S(1)}, f32[2,128,512]{2,1,0:T(8,128)S(1)}) custom-call(s32[8,128]{1,0:T(8,128)S(1)} %lists.1.table, s32[64]{0:T(128)S(1)} %copy-done.5, bf16[2,512,128]{2,1,0:T(8,128)(2,1)S(1)} %turn.1.q_rot, bf16[28,2,128,128]{3,2,1,0:T(8,128)(2,1)S(1)} %get-tuple-element.41.own), custom_call_target="tpu_custom_call" | custom-call | flops 6000000000 | bytes 3000000 | tf_op jit(solution)/shard_map/attend_first/pallas_call | solution.py:307
  56.8 0.0 collective-permute-done.6
  56.9 7.4 %collective-permute-start.7 = (bf16[32,2,128,128]{3,2,1,0:T(8,128)(2,1)S(1)}, bf16[32,2,128,128]{3,2,1,0:T(8,128)(2,1)S(1)}, u32[]{:S(2)}, u32[]{:S(2)}) collective-permute-start(bf16[32,2,128,128]{3,2,1,0:T(8,128)(2,1)S(1)} %constant_dynamic-update-slice_fusion.7.own), channel_id=1, source_target_pairs={{0,8},{8,0},{16,24},{24,16},{32,40},{40,32},{48,56},{56,48},{64,72... | collective-permute-start | bytes 6291464 | tf_op jit(solution)/shard_map/ppermute | solution.py:465
  64.3 3.8 %collective-permute-done.7.other = bf16[32,2,128,128]{3,2,1,0:T(8,128)(2,1)S(1)} collective-permute-done((bf16[32,2,128,128]{3,2,1,0:T(8,128)(2,1)S(1)}, bf16[32,2,128,128]{3,2,1,0:T(8,128)(2,1)S(1)}, u32[]{:S(2)}, u32[]{:S(2)}) %collective-permute-start.7) | collective-permute-done | bytes 2097184 | tf_op jit(solution)/shard_map/ppermute | solution.py:465
  68.1 0.6 pick.1
  68.7 7.9 %collective-permute-start.8 = (bf16[2,128,128]{2,1,0:T(8,128)(2,1)S(1)}, bf16[2,128,128]{2,1,0:T(8,128)(2,1)S(1)}, u32[]{:S(2)}, u32[]{:S(2)}) collective-permute-start(bf16[2,128,128]{2,1,0:T(8,128)(2,1)S(1)} %get-tuple-element.32), channel_id=1, source_target_pairs={{0,4},{1,5},{2,6},{3,7},{4,0},{5,1},{6,2},{7,3},{8,12},{9,13},{10,... | collective-permute-start | bytes 196616 | tf_op jit(solution)/shard_map/ppermute | solution.py:468
  76.7 7.1 %attend_rest.1 = bf16[128,1024]{1,0:T(8,128)(2,1)} custom-call(s32[8,128]{1,0:T(8,128)S(1)} %lists.1.table, bf16[2,512,128]{2,1,0:T(8,128)(2,1)S(1)} %turn.1.q_rot, f32[2,1,512]{2,1,0:T(1,128)S(1)} %get-tuple-element.33.tops, f32[2,1,512]{2,1,0:T(1,128)S(1)} %get-tuple-element.34.totals, f32[2,128,512]{2,1,0:T(8,128)S(1)} %get-tuple-element.35.accs, ...), custom_call_target="tpu_custom_call" | custom-call | flops 8000000000 | bytes 4000000 | tf_op jit(solution)/shard_map/attend_rest/pallas_call | solution.py:346
  83.7 0.0 collective-permute-done.8
  83.8 4.4 %collective-permute-start.10 = (bf16[2,2,128,128]{3,2,1,0:T(8,128)(2,1)S(1)}, bf16[2,2,128,128]{3,2,1,0:T(8,128)(2,1)S(1)}, u32[]{:S(2)}, u32[]{:S(2)}) collective-permute-start(bf16[2,2,128,128]{3,2,1,0:T(8,128)(2,1)S(1)} %bitcast_dynamic-update-slice_fusion.near), channel_id=1, source_target_pairs={{0,3},{1,0},{2,1},{3,2},{4,7},{5,4},{6,5},{7,6},{8,11},{9,8},{10,9... | collective-permute-start | bytes 393224 | tf_op jit(solution)/shard_map/ppermute | solution.py:473
  88.2 2.4 %collective-permute-start.11 = (bf16[2,2,128,128]{3,2,1,0:T(8,128)(2,1)S(1)}, bf16[2,2,128,128]{3,2,1,0:T(8,128)(2,1)S(1)}, u32[]{:S(2)}, u32[]{:S(2)}) collective-permute-start(bf16[2,2,128,128]{3,2,1,0:T(8,128)(2,1)S(1)} %bitcast_dynamic-update-slice_fusion.near), channel_id=1, source_target_pairs={{0,2},{1,3},{2,0},{3,1},{4,6},{5,7},{6,4},{7,5},{8,10},{9,11},{10,... | collective-permute-start | bytes 393224 | tf_op jit(solution)/shard_map/ppermute | solution.py:474
  90.6 2.5 %collective-permute-start.9 = (bf16[2,2,128,128]{3,2,1,0:T(8,128)(2,1)S(1)}, bf16[2,2,128,128]{3,2,1,0:T(8,128)(2,1)S(1)}, u32[]{:S(2)}, u32[]{:S(2)}) collective-permute-start(bf16[2,2,128,128]{3,2,1,0:T(8,128)(2,1)S(1)} %bitcast_dynamic-update-slice_fusion.near), channel_id=1, source_target_pairs={{0,1},{1,2},{2,3},{3,0},{4,5},{5,6},{6,7},{7,4},{8,9},{9,10},{10,1... | collective-permute-start | bytes 393224 | tf_op jit(solution)/shard_map/ppermute | solution.py:472
  93.1 0.0 collective-permute-done.10.left
  93.1 2.9 %collective-permute-done.11.far = bf16[2,2,128,128]{3,2,1,0:T(8,128)(2,1)S(1)} collective-permute-done((bf16[2,2,128,128]{3,2,1,0:T(8,128)(2,1)S(1)}, bf16[2,2,128,128]{3,2,1,0:T(8,128)(2,1)S(1)}, u32[]{:S(2)}, u32[]{:S(2)}) %collective-permute-start.11) | collective-permute-done | bytes 131104 | tf_op jit(solution)/shard_map/ppermute | solution.py:474
  96.0 3.2 %collective-permute-done.9.right = bf16[2,2,128,128]{3,2,1,0:T(8,128)(2,1)S(1)} collective-permute-done((bf16[2,2,128,128]{3,2,1,0:T(8,128)(2,1)S(1)}, bf16[2,2,128,128]{3,2,1,0:T(8,128)(2,1)S(1)}, u32[]{:S(2)}, u32[]{:S(2)}) %collective-permute-start.9) | collective-permute-done | bytes 131104 | tf_op jit(solution)/shard_map/ppermute | solution.py:472
  99.3 1.5 %place.1 = (bf16[2,128,128]{2,1,0:T(8,128)(2,1)}, bf16[2,128,128]{2,1,0:T(8,128)(2,1)}) custom-call(s32[128]{0:T(128)S(1)} %route.1.table, bf16[2,2,128,128]{3,2,1,0:T(8,128)(2,1)S(1)} %bitcast_dynamic-update-slice_fusion.near, bf16[2,2,128,128]{3,2,1,0:T(8,128)(2,1)S(1)} %collective-permute-done.9.right, ...), custom_call_target="tpu_custom_call" | custom-call | flops 100000 | bytes 800000 | tf_op jit(solution)/shard_map/place/pallas_call | solution.py:431
  (2 shorter events, 0.0 us)
Async XLA Ops:
  0.6 35.2 %copy-start.5 = (s32[64]{0:T(128)S(1)}, s32[64]{0:T(128)}, u32[]{:S(2)}) copy-start(s32[64]{0:T(128)} %counts.5) | copy-start | bytes 772
  3.8 41.8 %copy-start.2 = (s32[8,64]{1,0:T(8,128)S(1)}, s32[8,64]{1,0:T(8,128)}, u32[]{:S(2)}) copy-start(s32[8,64]{1,0:T(8,128)} %owner_row.1) | copy-start | bytes 6148
  3.8 41.8 %copy-start.3 = (s32[8,64]{1,0:T(8,128)S(1)}, s32[8,64]{1,0:T(8,128)}, u32[]{:S(2)}) copy-start(s32[8,64]{1,0:T(8,128)} %owner_col.1) | copy-start | bytes 6148
  3.8 41.8 %copy-start.4 = (s32[8,64]{1,0:T(8,128)S(1)}, s32[8,64]{1,0:T(8,128)}, u32[]{:S(2)}) copy-start(s32[8,64]{1,0:T(8,128)} %owner_slot.1) | copy-start | bytes 6148
  17.6 11.7 %collective-permute-start = (bf16[4,2,128,128]{3,2,1,0:T(8,128)(2,1)S(1)}, bf16[4,2,128,128]{3,2,1,0:T(8,128)(2,1)S(1)}, u32[]{:S(2)}, u32[]{:S(2)}) collective-permute-start(bf16[4,2,128,128]{3,2,1,0:T(8,128)(2,1)S(1)} %all_to_all.5.unit), channel_id=1, source_target_pairs={{0,16},{8,24},{16,32},{24,40},{32,48},{40,56},{48,64},{56,72},{64,... | collective-permute-start | bytes 786440 | tf_op jit(solution)/shard_map/ppermute | solution.py:450
  21.6 9.6 %collective-permute-start.3 = (bf16[4,2,128,128]{3,2,1,0:T(8,128)(2,1)S(1)}, bf16[4,2,128,128]{3,2,1,0:T(8,128)(2,1)S(1)}, u32[]{:S(2)}, u32[]{:S(2)}) collective-permute-start(bf16[4,2,128,128]{3,2,1,0:T(8,128)(2,1)S(1)} %all_to_all.5.unit), channel_id=1, source_target_pairs={{0,112},{8,120},{16,0},{24,8},{32,16},{40,24},{48,32},{56,40},{64,... | collective-permute-start | bytes 786440 | tf_op jit(solution)/shard_map/ppermute | solution.py:451
  25.4 0.8 copy-start
  26.2 0.9 copy-start.1
  27.2 0.7 copy-start.6
  29.3 9.5 %collective-permute-start.1 = (bf16[4,2,128,128]{3,2,1,0:T(8,128)(2,1)S(1)}, bf16[4,2,128,128]{3,2,1,0:T(8,128)(2,1)S(1)}, u32[]{:S(2)}, u32[]{:S(2)}) collective-permute-start(bf16[4,2,128,128]{3,2,1,0:T(8,128)(2,1)S(1)} %collective-permute-done.after), channel_id=1, source_target_pairs={{0,16},{8,24},{16,32},{24,40},{32,48},{40,56},{48,64},{56,72},{64,... | collective-permute-start | bytes 786440 | tf_op jit(solution)/shard_map/ppermute | solution.py:453
  31.2 9.7 %collective-permute-start.4 = (bf16[4,2,128,128]{3,2,1,0:T(8,128)(2,1)S(1)}, bf16[4,2,128,128]{3,2,1,0:T(8,128)(2,1)S(1)}, u32[]{:S(2)}, u32[]{:S(2)}) collective-permute-start(bf16[4,2,128,128]{3,2,1,0:T(8,128)(2,1)S(1)} %collective-permute-done.3), channel_id=1, source_target_pairs={{0,112},{8,120},{16,0},{24,8},{32,16},{40,24},{48,32},{56,40},{64,... | collective-permute-start | bytes 786440 | tf_op jit(solution)/shard_map/ppermute | solution.py:454
  38.8 9.7 %collective-permute-start.2 = (bf16[4,2,128,128]{3,2,1,0:T(8,128)(2,1)S(1)}, bf16[4,2,128,128]{3,2,1,0:T(8,128)(2,1)S(1)}, u32[]{:S(2)}, u32[]{:S(2)}) collective-permute-start(bf16[4,2,128,128]{3,2,1,0:T(8,128)(2,1)S(1)} %collective-permute-done.1.after), channel_id=1, source_target_pairs={{0,16},{8,24},{16,32},{24,40},{32,48},{40,56},{48,64},{56,72},{64,... | collective-permute-start | bytes 786440 | tf_op jit(solution)/shard_map/ppermute | solution.py:456
  40.9 9.7 %collective-permute-start.5 = (bf16[4,2,128,128]{3,2,1,0:T(8,128)(2,1)S(1)}, bf16[4,2,128,128]{3,2,1,0:T(8,128)(2,1)S(1)}, u32[]{:S(2)}, u32[]{:S(2)}) collective-permute-start(bf16[4,2,128,128]{3,2,1,0:T(8,128)(2,1)S(1)} %collective-permute-done.4), channel_id=1, source_target_pairs={{0,112},{8,120},{16,0},{24,8},{32,16},{40,24},{48,32},{56,40},{64,... | collective-permute-start | bytes 786440 | tf_op jit(solution)/shard_map/ppermute | solution.py:457
  48.5 8.3 %collective-permute-start.6 = (bf16[4,2,128,128]{3,2,1,0:T(8,128)(2,1)S(1)}, bf16[4,2,128,128]{3,2,1,0:T(8,128)(2,1)S(1)}, u32[]{:S(2)}, u32[]{:S(2)}) collective-permute-start(bf16[4,2,128,128]{3,2,1,0:T(8,128)(2,1)S(1)} %collective-permute-done.2), channel_id=1, source_target_pairs={{0,16},{8,24},{16,32},{24,40},{32,48},{40,56},{48,64},{56,72},{64,... | collective-permute-start | bytes 786440 | tf_op jit(solution)/shard_map/ppermute | solution.py:459
  56.9 11.2 %collective-permute-start.7 = (bf16[32,2,128,128]{3,2,1,0:T(8,128)(2,1)S(1)}, bf16[32,2,128,128]{3,2,1,0:T(8,128)(2,1)S(1)}, u32[]{:S(2)}, u32[]{:S(2)}) collective-permute-start(bf16[32,2,128,128]{3,2,1,0:T(8,128)(2,1)S(1)} %constant_dynamic-update-slice_fusion.7.own), channel_id=1, source_target_pairs={{0,8},{8,0},{16,24},{24,16},{32,40},{40,32},{48,56},{56,48},{64,72... | collective-permute-start | bytes 6291464 | tf_op jit(solution)/shard_map/ppermute | solution.py:465
  68.7 15.0 %collective-permute-start.8 = (bf16[2,128,128]{2,1,0:T(8,128)(2,1)S(1)}, bf16[2,128,128]{2,1,0:T(8,128)(2,1)S(1)}, u32[]{:S(2)}, u32[]{:S(2)}) collective-permute-start(bf16[2,128,128]{2,1,0:T(8,128)(2,1)S(1)} %get-tuple-element.32), channel_id=1, source_target_pairs={{0,4},{1,5},{2,6},{3,7},{4,0},{5,1},{6,2},{7,3},{8,12},{9,13},{10,... | collective-permute-start | bytes 196616 | tf_op jit(solution)/shard_map/ppermute | solution.py:468
  83.8 9.4 %collective-permute-start.10 = (bf16[2,2,128,128]{3,2,1,0:T(8,128)(2,1)S(1)}, bf16[2,2,128,128]{3,2,1,0:T(8,128)(2,1)S(1)}, u32[]{:S(2)}, u32[]{:S(2)}) collective-permute-start(bf16[2,2,128,128]{3,2,1,0:T(8,128)(2,1)S(1)} %bitcast_dynamic-update-slice_fusion.near), channel_id=1, source_target_pairs={{0,3},{1,0},{2,1},{3,2},{4,7},{5,4},{6,5},{7,6},{8,11},{9,8},{10,9... | collective-permute-start | bytes 393224 | tf_op jit(solution)/shard_map/ppermute | solution.py:473
  88.2 7.9 %collective-permute-start.11 = (bf16[2,2,128,128]{3,2,1,0:T(8,128)(2,1)S(1)}, bf16[2,2,128,128]{3,2,1,0:T(8,128)(2,1)S(1)}, u32[]{:S(2)}, u32[]{:S(2)}) collective-permute-start(bf16[2,2,128,128]{3,2,1,0:T(8,128)(2,1)S(1)} %bitcast_dynamic-update-slice_fusion.near), channel_id=1, source_target_pairs={{0,2},{1,3},{2,0},{3,1},{4,6},{5,7},{6,4},{7,5},{8,10},{9,11},{10,... | collective-permute-start | bytes 393224 | tf_op jit(solution)/shard_map/ppermute | solution.py:474
  90.6 8.7 %collective-permute-start.9 = (bf16[2,2,128,128]{3,2,1,0:T(8,128)(2,1)S(1)}, bf16[2,2,128,128]{3,2,1,0:T(8,128)(2,1)S(1)}, u32[]{:S(2)}, u32[]{:S(2)}) collective-permute-start(bf16[2,2,128,128]{3,2,1,0:T(8,128)(2,1)S(1)} %bitcast_dynamic-update-slice_fusion.near), channel_id=1, source_target_pairs={{0,1},{1,2},{2,3},{3,0},{4,5},{5,6},{6,7},{7,4},{8,9},{9,10},{10,1... | collective-permute-start | bytes 393224 | tf_op jit(solution)/shard_map/ppermute | solution.py:472

commit v3 on v2

v3 whole, which is shorter than its diff:
```python
import functools
import math

import jax
import jax.numpy as jnp
import numpy as np
from jax import lax
from jax.experimental import pallas as pl
from jax.experimental.pallas import tpu as pltpu
from jax.sharding import PartitionSpec as P

KVH = 8
HD = 128
PAGE = 128
HALF = 64
ROWS = 128
N_CP = 64
N_Z = 4
N_Y = 8
N_TP = 8
N_X = 4
SRC = N_CP // 2
LANES = 128
RUNS = 2 * N_CP
BIG = 1e30

THETA = 500000.0
FREQ = np.concatenate([THETA ** (-np.arange(HALF) * 2.0 / HD)] * 2).astype(np.float32)[None, :]
OFFSETS = (0, -1, 1, -2, 2, -3, 3, 4)
EARLY = 20
LATE = SRC - EARLY
FIRST = 28
REST = N_CP - FIRST
BIG_GRANT = 24 * 2**20


def cp_index(z, y, core):
    return ((z % N_Z) * N_Y + y % N_Y) * 2 + core


def y_pairs(step):
    return [
        (cp_index(z, y, c), cp_index(z, y + step, c))
        for z in range(N_Z)
        for y in range(N_Y)
        for c in range(2)
    ]


Z_GROUPS = [[cp_index(z, y, c) for z in range(N_Z)] for y in range(N_Y) for c in range(2)]
X_GROUPS = [[hi * N_X + x for x in range(N_X)] for hi in range(2)]
CORE_PAIRS = [(i, i ^ 1) for i in range(N_CP)]
ZHI_PAIRS = [(i, (i + N_X) % N_TP) for i in range(N_TP)]


def angles_of(freq, first_run, second_run, rows):
    row = lax.broadcasted_iota(jnp.int32, (rows, HD), 0)
    pos = jnp.where(row < HALF, first_run * HALF + row, second_run * HALF + row - HALF)
    angles = pos.astype(jnp.float32) * freq
    low = lax.broadcasted_iota(jnp.int32, (rows, HD), 1) < HALF
    sin = jnp.sin(angles)
    return jnp.cos(angles), jnp.where(low, -sin, sin)


def turned(x, cos, sin):
    return x * cos + pltpu.roll(x, HALF, 1) * sin


SMEM = pl.BlockSpec(memory_space=pltpu.SMEM)
VMEM = pl.BlockSpec(memory_space=pltpu.VMEM)
ANY = pl.BlockSpec(memory_space=pl.ANY)


def coordinates():
    me = lax.axis_index("cp")
    return me, lax.div(me, 2 * N_Y), lax.rem(lax.div(me, 2), N_Y), lax.rem(me, 2)


def pack_kernel(positions, keys, values, freq, out):
    first = lax.div(positions[lax.axis_index("cp") * ROWS], HALF)
    cos, sin = angles_of(freq[...], first, RUNS - 1 - first, ROWS)
    k_rot = turned(keys[...].astype(jnp.float32), cos, sin).astype(jnp.bfloat16)
    v = values[...]
    for i in range(N_Z):
        out[i, 0] = k_rot
        out[i, 1] = v


def pack(positions, keys, values):
    return pl.pallas_call(
        pack_kernel,
        out_shape=jax.ShapeDtypeStruct((N_Z, 2, ROWS, HD), jnp.bfloat16),
        in_specs=[SMEM, VMEM, VMEM, VMEM],
        out_specs=VMEM,
        cost_estimate=pl.CostEstimate(flops=1_000_000, bytes_accessed=400_000, transcendentals=0),
        name="pack",
    )(positions, keys, values, jnp.asarray(FREQ))


def turn_kernel(positions, queries, freq, after, q_rot, runs):
    del after
    for s in range(N_CP):
        runs[s] = lax.shift_right_logical(positions[s * ROWS], 6)
    my_run = runs[lax.axis_index("cp")]
    cos, sin = angles_of(freq[...], my_run, RUNS - 1 - my_run, ROWS)
    for h in range(KVH):
        q = turned(queries[:, h * HD : (h + 1) * HD].astype(jnp.float32), cos, sin)
        q = q.astype(jnp.bfloat16)
        q_rot[0, h * HALF : (h + 1) * HALF, :] = q[:HALF]
        q_rot[1, h * HALF : (h + 1) * HALF, :] = q[HALF:]


def turn(positions, queries, after):
    return pl.pallas_call(
        turn_kernel,
        out_shape=(
            jax.ShapeDtypeStruct((2, KVH * HALF, HD), jnp.bfloat16),
            jax.ShapeDtypeStruct((N_CP,), jnp.int32),
        ),
        in_specs=[SMEM, VMEM, VMEM, ANY],
        out_specs=(VMEM, SMEM),
        compiler_params=pltpu.CompilerParams(vmem_limit_bytes=BIG_GRANT),
        cost_estimate=pl.CostEstimate(flops=2_000_000, bytes_accessed=600_000, transcendentals=0),
        name="turn",
    )(positions, queries, jnp.asarray(FREQ), after)


LIST_ROWS = ((0, 1), (2, 3))
MISC = 4
AT_COUNT, AT_RUN, AT_PICK = 0, 4, 8


def clip_valid(counts, run):
    return jnp.clip(counts[lax.shift_right_logical(run, 1)] - (run & 1) * HALF, 0, HALF)


def page_of(owner_row, head, me):
    page = jnp.int32(0)
    for p in range(N_CP):
        page = jnp.where(owner_row[head, p] == me, p, page)
    return page


def lists_kernel(runs, counts, owner_row, after, table):
    del after
    me, z_me, y_me, core = coordinates()
    my_run = runs[me]

    for part in range(2):
        if part == 0:
            blocks = [(0, b) for b in range(FIRST)]
        else:
            blocks = [(0, b) for b in range(FIRST, SRC)] + [(1, b) for b in range(SRC)]
        n_low, n_high = jnp.int32(0), jnp.int32(0)
        low, high = LIST_ROWS[part]
        for b, (side, at) in enumerate(blocks):
            src_y = (y_me + OFFSETS[at // N_Z]) & (N_Y - 1)
            src_core = core if side == 0 else 1 - core
            run = runs[((at % N_Z)) * 2 * N_Y + src_y * 2 + src_core]
            first = b * 256 + clip_valid(counts, run)
            second = b * 256 + 128 + clip_valid(counts, RUNS - 1 - run)
            table[high, n_high] = first
            n_high = n_high + 1
            table[high, n_high] = second
            n_high = n_high + (run > my_run).astype(jnp.int32)
            table[low, n_low] = first
            n_low = n_low + (run < my_run).astype(jnp.int32)
        for r in range(16):
            table[low, n_low + r] = 0
            table[high, n_high + r] = 0
        table[MISC, AT_COUNT + low] = n_low
        table[MISC, AT_COUNT + high] = n_high
    table[MISC, AT_RUN] = my_run

    page = page_of(owner_row, lax.axis_index("tp"), me)
    for half in range(2):
        run = page * 2 + half
        second = run >= N_CP
        j = jnp.where(second, RUNS - 1 - run, run)
        src = jnp.int32(0)
        for s in range(N_CP):
            src = jnp.where(runs[s] == j, s, src)
        src_core = src & 1
        off = (lax.shift_right_logical(src, 1) - y_me) & (N_Y - 1)
        order = jnp.where(off < N_Y // 2, 2 * off, 2 * (N_Y - off) - 1)
        at = AT_PICK + 4 * half
        table[MISC, at] = (src_core != core).astype(jnp.int32)
        table[MISC, at + 1] = order * N_Z + (lax.shift_right_logical(src, 4))
        table[MISC, at + 2] = second.astype(jnp.int32)
        table[MISC, at + 3] = clip_valid(counts, run)


def lists(runs, counts, owner_row, after):
    return pl.pallas_call(
        lists_kernel,
        out_shape=jax.ShapeDtypeStruct((8, LANES), jnp.int32),
        in_specs=[SMEM, SMEM, SMEM, ANY],
        out_specs=SMEM,
        compiler_params=pltpu.CompilerParams(vmem_limit_bytes=BIG_GRANT),
        cost_estimate=pl.CostEstimate(flops=2_000_000, bytes_accessed=300_000, transcendentals=0),
        name="lists",
    )(runs, counts, owner_row, after)


def route_kernel(owner_row, owner_col, owner_slot, after, table):
    del after
    me = lax.axis_index("cp")
    tp = lax.axis_index("tp")
    for i in range(N_X):
        for d in range(2):
            head = i + ((tp & N_X) ^ (d * N_X))
            p = page_of(owner_row, head, me)
            mine = owner_col[head, p] == tp
            table[i * 2 + d] = jnp.where(mine, owner_slot[head, p], -1)


def route(owner_row, owner_col, owner_slot, after):
    return pl.pallas_call(
        route_kernel,
        out_shape=jax.ShapeDtypeStruct((8,), jnp.int32),
        in_specs=[SMEM, SMEM, SMEM, ANY],
        out_specs=SMEM,
        compiler_params=pltpu.CompilerParams(vmem_limit_bytes=BIG_GRANT),
        cost_estimate=pl.CostEstimate(flops=2_000_000, bytes_accessed=300_000, transcendentals=0),
        name="route",
    )(owner_row, owner_col, owner_slot, after)


COLS = KVH * HALF
SCALE = math.log2(math.e) / math.sqrt(HD)
dot = functools.partial(lax.dot_general, preferred_element_type=jnp.float32)


def fold(q, keys, vals, bias, allowed, state):
    top, total, acc = state
    s = dot(keys, q, (((1,), (1,)), ((), ()))) * SCALE
    s = s + jnp.concatenate([bias] * (COLS // HD), axis=1)
    if allowed is not None:
        s = jnp.where(allowed, s, -BIG)
    new_top = jnp.maximum(top, jnp.max(s, axis=0, keepdims=True))
    factor = jnp.exp2(top - new_top)
    w = jnp.exp2(s - new_top)
    total = total * factor + jnp.sum(w, axis=0, keepdims=True)
    acc = acc * factor + dot(vals, w.astype(jnp.bfloat16), (((0,), (0,)), ((), ())))
    return new_top, total, acc


def bias_of(valid):
    return jnp.where(lax.broadcasted_iota(jnp.int32, (HALF, HD), 0) < valid, 0.0, -BIG)


def fold_list(table, row, q, kv, state):
    def chunk(size, start, state):
        ks, vs, biases = [], [], []
        for r in range(size):
            code = table[row, start + r]
            b = lax.shift_right_logical(code, 8)
            rows = pl.ds(pl.multiple_of(lax.shift_right_logical(code & 128, 1), HALF), HALF)
            ks.append(kv[b, 0, rows, :])
            vs.append(kv[b, 1, rows, :])
            biases.append(bias_of(code & 127))
        return fold(
            q,
            jnp.concatenate(ks, axis=0),
            jnp.concatenate(vs, axis=0),
            jnp.concatenate(biases, axis=0),
            None,
            state,
        )

    count = table[MISC, AT_COUNT + row]
    wide = lax.shift_right_logical(count + 7, 4)
    state = lax.fori_loop(0, wide, lambda i, st: chunk(16, i * 16, st), state)
    narrow = (count > wide * 16).astype(jnp.int32)
    return lax.fori_loop(0, narrow, lambda i, st: chunk(8, wide * 16, st), state)


def copy_blocks(pieces, kv, sems):
    copies, at = [], 0
    for i, piece in enumerate(pieces):
        size = piece.shape[0]
        copies.append(pltpu.make_async_copy(piece, kv.at[pl.ds(at, size)], sems.at[i]))
        at += size
    for copy in copies:
        copy.start()
    for copy in copies:
        copy.wait()


def first_kernel(table, counts, q_rot, early, f3, b3, tops, totals, accs, kv, sems):
    copy_blocks((early, f3, b3), kv, sems)
    _, z_me, _, _ = coordinates()
    my_run = table[MISC, AT_RUN]
    key = lax.broadcasted_iota(jnp.int32, (HALF, COLS), 0)
    row = lax.broadcasted_iota(jnp.int32, (HALF, COLS), 1) & (HALF - 1)
    for part in range(2):
        q = q_rot[part]
        state = (
            jnp.full((1, COLS), -BIG, jnp.float32),
            jnp.zeros((1, COLS), jnp.float32),
            jnp.zeros((HD, COLS), jnp.float32),
        )
        run = my_run if part == 0 else RUNS - 1 - my_run
        page = lax.shift_right_logical(run, 1)
        valid = jnp.clip(counts[page] - (run & 1) * HALF, 0, HALF)
        rows = slice(part * HALF, (part + 1) * HALF)
        state = fold(q, kv[z_me, 0, rows], kv[z_me, 1, rows], bias_of(valid), key <= row, state)
        state = fold_list(table, LIST_ROWS[0][part], q, kv, state)
        tops[part], totals[part], accs[part] = state


STATE = (
    jax.ShapeDtypeStruct((2, 1, COLS), jnp.float32),
    jax.ShapeDtypeStruct((2, 1, COLS), jnp.float32),
    jax.ShapeDtypeStruct((2, HD, COLS), jnp.float32),
)


def attend_first(table, counts, q_rot, early, f3, b3):
    return pl.pallas_call(
        first_kernel,
        out_shape=STATE,
        in_specs=[SMEM, SMEM, VMEM, ANY, ANY, ANY],
        out_specs=(VMEM, VMEM, VMEM),
        scratch_shapes=[
            pltpu.VMEM((FIRST, 2, ROWS, HD), jnp.bfloat16),
            pltpu.SemaphoreType.DMA((3,)),
        ],
        compiler_params=pltpu.CompilerParams(vmem_limit_bytes=BIG_GRANT),
        cost_estimate=pl.CostEstimate(
            flops=6_000_000_000, bytes_accessed=3_000_000, transcendentals=2_000_000
        ),
        name="attend_first",
    )(table, counts, q_rot, early, f3, b3)


def rest_kernel(table, q_rot, tops, totals, accs, f4, early, late, out, kv, sems):
    copy_blocks((f4, early, late), kv, sems)
    for part in range(2):
        state = tops[part], totals[part], accs[part]
        _, total, acc = fold_list(table, LIST_ROWS[1][part], q_rot[part], kv, state)
        res = jnp.transpose(acc / total).astype(jnp.bfloat16)
        for h in range(KVH):
            out[part * HALF : (part + 1) * HALF, h * HD : (h + 1) * HD] = res[
                h * HALF : (h + 1) * HALF
            ]


def attend_rest(table, q_rot, state, f4, early, late):
    return pl.pallas_call(
        rest_kernel,
        out_shape=jax.ShapeDtypeStruct((ROWS, KVH * HD), jnp.bfloat16),
        in_specs=[SMEM, VMEM, VMEM, VMEM, VMEM, ANY, ANY, ANY],
        out_specs=VMEM,
        scratch_shapes=[
            pltpu.VMEM((REST, 2, ROWS, HD), jnp.bfloat16),
            pltpu.SemaphoreType.DMA((3,)),
        ],
        compiler_params=pltpu.CompilerParams(vmem_limit_bytes=BIG_GRANT),
        cost_estimate=pl.CostEstimate(
            flops=8_000_000_000, bytes_accessed=4_000_000, transcendentals=2_000_000
        ),
        name="attend_rest",
    )(table, q_rot, *state, f4, early, late)


def pick_kernel(table, own_early, own_late, other_early, other_late, out, held, sems):
    for half in range(2):
        at = AT_PICK + 4 * half
        side, index, second = (table[MISC, at + i] for i in range(3))
        rows = pl.ds(pl.multiple_of(second * HALF, HALF), HALF)
        for is_other, early, late in ((0, own_early, own_late), (1, other_early, other_late)):

            @pl.when((side == is_other) & (index < EARLY))
            def _(early=early, half=half, index=index, rows=rows):
                pltpu.make_async_copy(
                    early.at[index, :, rows], held.at[half], sems.at[half]
                ).start()

            @pl.when((side == is_other) & (index >= EARLY))
            def _(late=late, half=half, index=index, rows=rows):
                pltpu.make_async_copy(
                    late.at[index - EARLY, :, rows], held.at[half], sems.at[half]
                ).start()

    row = lax.broadcasted_iota(jnp.int32, (HALF, HD), 0)
    for half in range(2):
        pltpu.make_async_copy(own_late.at[0, :, pl.ds(0, HALF)], held.at[half], sems.at[half]).wait()
        keep = row < table[MISC, AT_PICK + 4 * half + 3]
        for i in range(2):
            block = jnp.where(keep, held[half, i].astype(jnp.float32), 0.0).astype(jnp.bfloat16)
            out[i, half * HALF : (half + 1) * HALF, :] = block


def pick(table, own_early, own_late, other_early, other_late):
    return pl.pallas_call(
        pick_kernel,
        out_shape=jax.ShapeDtypeStruct((2, PAGE, HD), jnp.bfloat16),
        in_specs=[SMEM, ANY, ANY, ANY, ANY],
        out_specs=VMEM,
        scratch_shapes=[
            pltpu.VMEM((2, 2, HALF, HD), jnp.bfloat16),
            pltpu.SemaphoreType.DMA((2,)),
        ],
        compiler_params=pltpu.CompilerParams(vmem_limit_bytes=BIG_GRANT),
        cost_estimate=pl.CostEstimate(flops=100_000, bytes_accessed=300_000, transcendentals=0),
        name="pick",
    )(table, own_early, own_late, other_early, other_late)


def place_kernel(table, pages, pool_k, pool_v, sems):
    for slot in range(2):
        empty = True
        for i in range(N_X):
            for hi in range(2):
                hit = table[i * 2 + hi] == slot
                empty = jnp.logical_and(empty, jnp.logical_not(hit))

                @pl.when(hit)
                def _(i=i, hi=hi, slot=slot):
                    pltpu.make_async_copy(pages.at[i, hi, 0], pool_k.at[slot], sems.at[slot, 0]).start()
                    pltpu.make_async_copy(pages.at[i, hi, 1], pool_v.at[slot], sems.at[slot, 1]).start()

        @pl.when(empty)
        def _(slot=slot):
            pool_k[slot] = jnp.zeros((PAGE, HD), jnp.bfloat16)
            pool_v[slot] = jnp.zeros((PAGE, HD), jnp.bfloat16)

        @pl.when(jnp.logical_not(empty))
        def _(slot=slot):
            pltpu.make_async_copy(pages.at[0, 0, 0], pool_k.at[slot], sems.at[slot, 0]).wait()
            pltpu.make_async_copy(pages.at[0, 0, 1], pool_v.at[slot], sems.at[slot, 1]).wait()


def place(table, pages):
    shape = jax.ShapeDtypeStruct((2, PAGE, HD), jnp.bfloat16)
    return pl.pallas_call(
        place_kernel,
        out_shape=(shape, shape),
        in_specs=[SMEM, ANY],
        out_specs=(VMEM, VMEM),
        scratch_shapes=[pltpu.SemaphoreType.DMA((2, 2))],
        compiler_params=pltpu.CompilerParams(vmem_limit_bytes=BIG_GRANT),
        cost_estimate=pl.CostEstimate(flops=100_000, bytes_accessed=800_000, transcendentals=0),
        name="place",
    )(table, pages)


def shards(queries, keys, values, positions, counts, owner_row, owner_col, owner_slot):
    tie = lax.optimization_barrier
    spread = pack(positions, keys, values)
    unit = lax.all_to_all(spread, "cp", 0, 0, axis_index_groups=Z_GROUPS)

    ahead, back = y_pairs(1), y_pairs(-1)
    f1 = lax.ppermute(unit, "cp", ahead)
    b1 = lax.ppermute(unit, "cp", back)
    f1, q_rot, runs = tie((f1, *turn(positions, queries, unit)))
    f2 = lax.ppermute(f1, "cp", ahead)
    b2 = lax.ppermute(b1, "cp", back)
    f2, table = tie((f2, lists(runs, counts, owner_row, f1)))
    f3 = lax.ppermute(f2, "cp", ahead)
    b3 = lax.ppermute(b2, "cp", back)
    own_early = jnp.concatenate([unit, f1, b1, f2, b2], axis=0)
    other_early = lax.ppermute(own_early, "cp", CORE_PAIRS)
    f4 = lax.ppermute(f3, "cp", ahead)
    state = attend_first(table, counts, q_rot, own_early, f3, b3)
    f4, state = tie((f4, state))
    own_late = jnp.concatenate([f3, b3, f4], axis=0)
    other_late = lax.ppermute(own_late, "cp", CORE_PAIRS)
    other_late, routes = tie((other_late, route(owner_row, owner_col, owner_slot, f4)))

    picked = pick(table, own_early, own_late, other_early, other_late)
    across = lax.ppermute(picked, "tp", ZHI_PAIRS)
    attended = attend_rest(table, q_rot, state, f4, other_early, other_late)
    across, attended = tie((across, attended))
    near = jnp.broadcast_to(jnp.stack([picked, across]), (N_X, 2, 2, PAGE, HD))
    pages = lax.all_to_all(near, "tp", 0, 0, axis_index_groups=X_GROUPS)
    pool_keys, pool_values = place(routes, pages)
    return attended, pool_keys, pool_values


def solution(mesh):
    return jax.shard_map(
        shards,
        mesh=mesh,
        in_specs=(P("cp", "tp"), P("cp", "tp"), P("cp", "tp"), P(), P(), P(), P(), P()),
        out_specs=(P("cp", "tp"), P(("cp", "tp"), None, None), P(("cp", "tp"), None, None)),
        check_vma=False,
    )
```

time: 102 us -> 96.7 us (0.948)
  blocking collectives: 13.8 us -> 25.6 us
  waiting for transfers between devices: 9.96 us -> 2.56 us
  starting transfers between devices: 47.4 us -> 40 us
  local copies, waits for them, and re-layouts: 4.18 us -> 2.73 us
  Pallas kernels: 24.4 us -> 23.2 us
    all_to_all x0 -> x1, blocking collectives: none -> 11.7 us  [shards(): pages = lax.all_to_all(near, 'tp', 0, 0, axis_index_groups=X_GROUPS)]
    ppermute x4 -> x2, waiting for transfers between devices: 9.93 us -> 0.01 us  [the longest x1 0.01 us: shards(): other_early = lax.ppermute(own_early, 'cp', CORE_PAIRS)]
    ppermute x4 -> x2, starting transfers between devices: 16.7 us -> 9.31 us  [the longest x1 6.25 us: shards(): other_early = lax.ppermute(own_early, 'cp', CORE_PAIRS)]
    ppermute x1, waiting for transfers between devices: 0.01 us -> 2.54 us  [shards(): f4 = lax.ppermute(f3, 'cp', ahead)]
  transfers between devices with their start and end apart: 12 -> 10, of which waited for: 3 -> 1; matrix products, arithmetic and copies ran while one was open for 1% -> 0% of each run, Pallas kernels for 20% -> 20%
where the time goes in v3:
time: 96.7 us; the launch traced here: 95.1 us
  starting transfers between devices  40 us (41%)
  blocking collectives  25.6 us (26%)
  Pallas kernels  23.2 us (24%)
  local copies, waits for them, and re-layouts  2.73 us (3%)
  waiting for transfers between devices  2.56 us (3%)
  between operations  0.98 us (1%)
    all_to_all x1, blocking collectives, shards(): unit = lax.all_to_all(spread, 'cp', 0, 0, axis_index_groups=Z_GROUPS)  13.8 us
    all_to_all x1, blocking collectives, shards(): pages = lax.all_to_all(near, 'tp', 0, 0, axis_index_groups=X_GROUPS)  11.7 us
    ppermute x1, starting transfers between devices, shards(): across = lax.ppermute(picked, 'tp', ZHI_PAIRS)  7.94 us
    pallas_call x1, Pallas kernels, attend_rest(): pl.pallas_call(rest_kernel, out_shape=jax.ShapeDtypeStruct((ROWS, KVH * H...  6.39 us
    ppermute x1, starting transfers between devices, shards(): other_early = lax.ppermute(own_early, 'cp', CORE_PAIRS)  6.25 us
    pallas_call x1, Pallas kernels, attend_first(): pl.pallas_call(first_kernel, out_shape=STATE, in_specs=[SMEM, SMEM, VMEM,...  6.09 us
    ppermute x1, starting transfers between devices, shards(): b2 = lax.ppermute(b1, 'cp', back)  4.57 us
    ppermute x1, starting transfers between devices, shards(): b3 = lax.ppermute(b2, 'cp', back)  4.57 us
  transfers between devices with their start and end apart: 10, of which 1 were waited for; matrix products, arithmetic and copies ran while one was open for 0% of the time, Pallas kernels for 20%

profile of v3, /device:TPU:1, one launch (start us, length us, event | category | flops | bytes accessed | tf_op | source)
XLA Modules:
  0.0 95.1 jit_solution(14771416972548596467)
XLA Ops:
  0.6 0.0 copy-start.6
  0.6 0.0 copy-start.2
  0.7 2.3 %pack.1 = bf16[4,2,128,128]{3,2,1,0:T(8,128)(2,1)} custom-call(s32[8192]{0:T(1024)} %positions.3, bf16[128,128]{1,0:T(8,128)(2,1)} %keys.1, bf16[128,128]{1,0:T(8,128)(2,1)} %values.1, f32[1,128]{1,0:T(1,128)} %constant.2.clone.freq), custom_call_target="tpu_custom_call" | custom-call | flops 1000000 | bytes 400000 | tf_op jit(solution)/shard_map/pack/pallas_call | solution.py:90
  3.0 13.8 %all_to_all.10.after = bf16[4,2,128,128]{3,2,1,0:T(8,128)(2,1)S(1)} all-to-all(bf16[4,2,128,128]{3,2,1,0:T(8,128)(2,1)} %pack.1), channel_id=1, replica_groups={{0,128,256,384},{8,136,264,392},{16,144,272,400},{24,152,280,408},{32,1..., dimensions={0} | all-to-all | bytes 524288 | tf_op jit(solution)/shard_map/all_to_all | solution.py:452
  16.8 4.0 %collective-permute-start = (bf16[4,2,128,128]{3,2,1,0:T(8,128)(2,1)S(1)}, bf16[4,2,128,128]{3,2,1,0:T(8,128)(2,1)S(1)}, u32[]{:S(2)}, u32[]{:S(2)}) collective-permute-start(bf16[4,2,128,128]{3,2,1,0:T(8,128)(2,1)S(1)} %all_to_all.10.after), channel_id=1, source_target_pairs={{0,16},{8,24},{16,32},{24,40},{32,48},{40,56},{48,64},{56,72},{64,... | collective-permute-start | bytes 786440 | tf_op jit(solution)/shard_map/ppermute | solution.py:455
  20.9 3.8 %collective-permute-start.2 = (bf16[4,2,128,128]{3,2,1,0:T(8,128)(2,1)S(1)}, bf16[4,2,128,128]{3,2,1,0:T(8,128)(2,1)S(1)}, u32[]{:S(2)}, u32[]{:S(2)}) collective-permute-start(bf16[4,2,128,128]{3,2,1,0:T(8,128)(2,1)S(1)} %all_to_all.10.after), channel_id=1, source_target_pairs={{0,112},{8,120},{16,0},{24,8},{32,16},{40,24},{48,32},{56,40},{64,... | collective-permute-start | bytes 786440 | tf_op jit(solution)/shard_map/ppermute | solution.py:456
  24.7 0.0 copy-start
  24.7 0.9 copy-done
  25.6 0.0 copy-start.1
  25.6 0.8 copy-done.1
  26.4 0.0 copy-start.5
  26.4 0.7 copy-done.5
  27.1 1.8 %turn.1 = (bf16[2,512,128]{2,1,0:T(8,128)(2,1)S(1)}, s32[64]{0:T(128)S(1)}) custom-call(s32[8192]{0:T(1024)S(1)} %copy-done.1, bf16[128,1024]{1,0:T(8,128)(2,1)S(1)} %copy-done, f32[1,128]{1,0:T(1,128)S(1)} %copy-done.5, bf16[4,2,128,128]{3,2,1,0:T(8,128)(2,1)S(1)} %all_to_all.10.after), custom_call_target="tpu_custom_call" | custom-call | flops 2000000 | bytes 600000 | tf_op jit(solution)/shard_map/turn/pallas_call | solution.py:114
  28.8 0.0 collective-permute-done.after
  28.9 1.9 %collective-permute-start.1 = (bf16[4,2,128,128]{3,2,1,0:T(8,128)(2,1)S(1)}, bf16[4,2,128,128]{3,2,1,0:T(8,128)(2,1)S(1)}, u32[]{:S(2)}, u32[]{:S(2)}) collective-permute-start(bf16[4,2,128,128]{3,2,1,0:T(8,128)(2,1)S(1)} %collective-permute-done.after), channel_id=1, source_target_pairs={{0,16},{8,24},{16,32},{24,40},{32,48},{40,56},{48,64},{56,72},{64,... | collective-permute-start | bytes 786440 | tf_op jit(solution)/shard_map/ppermute | solution.py:458
  30.8 0.0 collective-permute-done.2
  30.8 4.6 %collective-permute-start.3 = (bf16[4,2,128,128]{3,2,1,0:T(8,128)(2,1)S(1)}, bf16[4,2,128,128]{3,2,1,0:T(8,128)(2,1)S(1)}, u32[]{:S(2)}, u32[]{:S(2)}) collective-permute-start(bf16[4,2,128,128]{3,2,1,0:T(8,128)(2,1)S(1)} %collective-permute-done.2), channel_id=1, source_target_pairs={{0,112},{8,120},{16,0},{24,8},{32,16},{40,24},{48,32},{56,40},{64,... | collective-permute-start | bytes 786440 | tf_op jit(solution)/shard_map/ppermute | solution.py:459
  35.4 0.0 copy-done.6
  35.4 0.0 copy-done.2
  35.4 2.5 %lists.1.table = s32[8,128]{1,0:T(8,128)S(1)} custom-call(s32[64]{0:T(128)S(1)} %get-tuple-element.26.runs, s32[64]{0:T(128)S(1)} %copy-done.6, s32[8,64]{1,0:T(8,128)S(1)} %copy-done.2, bf16[4,2,128,128]{3,2,1,0:T(8,128)(2,1)S(1)} %collective-permute-done.after), custom_call_target="tpu_custom_call" | custom-call | flops 2000000 | bytes 300000 | tf_op jit(solution)/shard_map/lists/pallas_call | solution.py:194
  37.9 0.0 collective-permute-done.1
  37.9 1.9 %collective-permute-start.4 = (bf16[4,2,128,128]{3,2,1,0:T(8,128)(2,1)S(1)}, bf16[4,2,128,128]{3,2,1,0:T(8,128)(2,1)S(1)}, u32[]{:S(2)}, u32[]{:S(2)}) collective-permute-start(bf16[4,2,128,128]{3,2,1,0:T(8,128)(2,1)S(1)} %collective-permute-done.1), channel_id=1, source_target_pairs={{0,16},{8,24},{16,32},{24,40},{32,48},{40,56},{48,64},{56,72},{64,... | collective-permute-start | bytes 786440 | tf_op jit(solution)/shard_map/ppermute | solution.py:461
  39.9 0.0 collective-permute-done.3
  39.9 4.6 %collective-permute-start.5 = (bf16[4,2,128,128]{3,2,1,0:T(8,128)(2,1)S(1)}, bf16[4,2,128,128]{3,2,1,0:T(8,128)(2,1)S(1)}, u32[]{:S(2)}, u32[]{:S(2)}) collective-permute-start(bf16[4,2,128,128]{3,2,1,0:T(8,128)(2,1)S(1)} %collective-permute-done.3), channel_id=1, source_target_pairs={{0,112},{8,120},{16,0},{24,8},{32,16},{40,24},{48,32},{56,40},{64,... | collective-permute-start | bytes 786440 | tf_op jit(solution)/shard_map/ppermute | solution.py:462
  44.6 6.3 %collective-permute-start.7 = (bf16[20,2,128,128]{3,2,1,0:T(8,128)(2,1)S(1)}, bf16[20,2,128,128]{3,2,1,0:T(8,128)(2,1)S(1)}, u32[]{:S(2)}, u32[]{:S(2)}) collective-permute-start(bf16[20,2,128,128]{3,2,1,0:T(8,128)(2,1)S(1)} %constant_dynamic-update-slice_fusion.early.own_early), channel_id=1, source_target_pairs={{0,8},{8,0},{16,24},{24,16},{32,40},{40,32},{48,56},{56,48},{64,72... | collective-permute-start | bytes 3932168 | tf_op jit(solution)/shard_map/ppermute | solution.py:464
  50.9 0.0 collective-permute-done.4.f3
  50.9 1.9 %collective-permute-start.6 = (bf16[4,2,128,128]{3,2,1,0:T(8,128)(2,1)S(1)}, bf16[4,2,128,128]{3,2,1,0:T(8,128)(2,1)S(1)}, u32[]{:S(2)}, u32[]{:S(2)}) collective-permute-start(bf16[4,2,128,128]{3,2,1,0:T(8,128)(2,1)S(1)} %collective-permute-done.4.f3), channel_id=1, source_target_pairs={{0,16},{8,24},{16,32},{24,40},{32,48},{40,56},{48,64},{56,72},{64,... | collective-permute-start | bytes 786440 | tf_op jit(solution)/shard_map/ppermute | solution.py:465
  52.8 0.0 collective-permute-done.5.b3
  52.8 6.1 %attend_first.1 = (f32[2,1,512]{2,1,0:T(1,128)S(1)}, f32[2,1,512]{2,1,0:T(1,128)S(1)}, f32[2,128,512]{2,1,0:T(8,128)S(1)}) custom-call(s32[8,128]{1,0:T(8,128)S(1)} %lists.1.table, s32[64]{0:T(128)S(1)} %copy-done.6, bf16[2,512,128]{2,1,0:T(8,128)(2,1)S(1)} %get-tuple-element.29.q_rot, ...), custom_call_target="tpu_custom_call" | custom-call | flops 6000000000 | bytes 3000000 | tf_op jit(solution)/shard_map/attend_first/pallas_call | solution.py:320
  58.9 0.0 copy-start.3
  58.9 0.0 copy-start.4
  59.0 2.5 %collective-permute-done.6.after.f4 = bf16[4,2,128,128]{3,2,1,0:T(8,128)(2,1)S(1)} collective-permute-done((bf16[4,2,128,128]{3,2,1,0:T(8,128)(2,1)S(1)}, bf16[4,2,128,128]{3,2,1,0:T(8,128)(2,1)S(1)}, u32[]{:S(2)}, u32[]{:S(2)}) %collective-permute-start.6) | collective-permute-done | bytes 262176 | tf_op jit(solution)/shard_map/ppermute | solution.py:465
  61.6 3.1 %collective-permute-start.8 = (bf16[12,2,128,128]{3,2,1,0:T(8,128)(2,1)S(1)}, bf16[12,2,128,128]{3,2,1,0:T(8,128)(2,1)S(1)}, u32[]{:S(2)}, u32[]{:S(2)}) collective-permute-start(bf16[12,2,128,128]{3,2,1,0:T(8,128)(2,1)S(1)} %constant_dynamic-update-slice_fusion.5.own_late), channel_id=1, source_target_pairs={{0,8},{8,0},{16,24},{24,16},{32,40},{40,32},{48,56},{56,48},{64,72... | collective-permute-start | bytes 2359304 | tf_op jit(solution)/shard_map/ppermute | solution.py:469
  64.6 0.0 copy-done.3
  64.7 0.0 copy-done.4
  64.7 1.9 %route.1.table = s32[8]{0:T(128)S(1)} custom-call(s32[8,64]{1,0:T(8,128)S(1)} %copy-done.2, s32[8,64]{1,0:T(8,128)S(1)} %copy-done.3, s32[8,64]{1,0:T(8,128)S(1)} %copy-done.4, bf16[4,2,128,128]{3,2,1,0:T(8,128)(2,1)S(1)} %collective-permute-done.6.after.f4), custom_call_target="tpu_custom_call" | custom-call | flops 2000000 | bytes 300000 | tf_op jit(solution)/shard_map/route/pallas_call | solution.py:218
  66.6 0.0 collective-permute-done.8.other_late.late
  66.6 0.0 collective-permute-done.7.other_early.early
  66.6 0.7 pick.1
  67.3 7.9 %collective-permute-start.9 = (bf16[2,128,128]{2,1,0:T(8,128)(2,1)S(1)}, bf16[2,128,128]{2,1,0:T(8,128)(2,1)S(1)}, u32[]{:S(2)}, u32[]{:S(2)}) collective-permute-start(bf16[2,128,128]{2,1,0:T(8,128)(2,1)S(1)} %pick.1), channel_id=1, source_target_pairs={{0,4},{1,5},{2,6},{3,7},{4,0},{5,1},{6,2},{7,3},{8,12},{9,13},{10,... | collective-permute-start | bytes 196616 | tf_op jit(solution)/shard_map/ppermute | solution.py:473
  75.3 6.4 %attend_rest.1 = bf16[128,1024]{1,0:T(8,128)(2,1)} custom-call(s32[8,128]{1,0:T(8,128)S(1)} %lists.1.table, bf16[2,512,128]{2,1,0:T(8,128)(2,1)S(1)} %get-tuple-element.29.q_rot, f32[2,1,512]{2,1,0:T(1,128)S(1)} %get-tuple-element.35.tops, f32[2,1,512]{2,1,0:T(1,128)S(1)} %get-tuple-element.36.totals, f32[2,128,512]{2,1,0:T(8,128)S(1)} %get-tuple-element.37.accs, ...), custom_call_target="tpu_custom_call" | custom-call | flops 8000000000 | bytes 4000000 | tf_op jit(solution)/shard_map/attend_rest/pallas_call | solution.py:350
  81.7 0.0 collective-permute-done.9
  81.7 0.1 broadcast_in_dim.3
  81.8 11.7 %all_to_all.11.pages = bf16[4,2,2,128,128]{4,3,2,1,0:T(8,128)(2,1)S(1)} all-to-all(bf16[4,2,2,128,128]{4,3,2,1,0:T(8,128)(2,1)S(1)} %broadcast_in_dim.3), channel_id=1, replica_groups={{0,1,2,3},{4,5,6,7},{8,9,10,11},{12,13,14,15},{16,17,18,19},{20,21,22,2..., dimensions={0} | all-to-all | bytes 1048576 | tf_op jit(solution)/shard_map/all_to_all | solution.py:477
  93.5 1.5 %place.1 = (bf16[2,128,128]{2,1,0:T(8,128)(2,1)}, bf16[2,128,128]{2,1,0:T(8,128)(2,1)}) custom-call(s32[8]{0:T(128)S(1)} %route.1.table, bf16[4,2,2,128,128]{4,3,2,1,0:T(8,128)(2,1)S(1)} %all_to_all.11.pages), custom_call_target="tpu_custom_call" | custom-call | flops 100000 | bytes 800000 | tf_op jit(solution)/shard_map/place/pallas_call | solution.py:437
  (9 shorter events, 0.3 us)
Async XLA Ops:
  0.6 34.8 %copy-start.6 = (s32[64]{0:T(128)S(1)}, s32[64]{0:T(128)}, u32[]{:S(2)}) copy-start(s32[64]{0:T(128)} %counts.3) | copy-start | bytes 772
  0.6 34.8 %copy-start.2 = (s32[8,64]{1,0:T(8,128)S(1)}, s32[8,64]{1,0:T(8,128)}, u32[]{:S(2)}) copy-start(s32[8,64]{1,0:T(8,128)} %owner_row.3) | copy-start | bytes 6148
  16.8 12.0 %collective-permute-start = (bf16[4,2,128,128]{3,2,1,0:T(8,128)(2,1)S(1)}, bf16[4,2,128,128]{3,2,1,0:T(8,128)(2,1)S(1)}, u32[]{:S(2)}, u32[]{:S(2)}) collective-permute-start(bf16[4,2,128,128]{3,2,1,0:T(8,128)(2,1)S(1)} %all_to_all.10.after), channel_id=1, source_target_pairs={{0,16},{8,24},{16,32},{24,40},{32,48},{40,56},{48,64},{56,72},{64,... | collective-permute-start | bytes 786440 | tf_op jit(solution)/shard_map/ppermute | solution.py:455
  20.9 9.9 %collective-permute-start.2 = (bf16[4,2,128,128]{3,2,1,0:T(8,128)(2,1)S(1)}, bf16[4,2,128,128]{3,2,1,0:T(8,128)(2,1)S(1)}, u32[]{:S(2)}, u32[]{:S(2)}) collective-permute-start(bf16[4,2,128,128]{3,2,1,0:T(8,128)(2,1)S(1)} %all_to_all.10.after), channel_id=1, source_target_pairs={{0,112},{8,120},{16,0},{24,8},{32,16},{40,24},{48,32},{56,40},{64,... | collective-permute-start | bytes 786440 | tf_op jit(solution)/shard_map/ppermute | solution.py:456
  24.7 1.0 %copy-start = (bf16[128,1024]{1,0:T(8,128)(2,1)S(1)}, bf16[128,1024]{1,0:T(8,128)(2,1)}, u32[]{:S(2)}) copy-start(bf16[128,1024]{1,0:T(8,128)(2,1)} %queries.1) | copy-start | bytes 786436
  25.6 0.8 copy-start.1
  26.4 0.7 copy-start.5
  28.9 9.1 %collective-permute-start.1 = (bf16[4,2,128,128]{3,2,1,0:T(8,128)(2,1)S(1)}, bf16[4,2,128,128]{3,2,1,0:T(8,128)(2,1)S(1)}, u32[]{:S(2)}, u32[]{:S(2)}) collective-permute-start(bf16[4,2,128,128]{3,2,1,0:T(8,128)(2,1)S(1)} %collective-permute-done.after), channel_id=1, source_target_pairs={{0,16},{8,24},{16,32},{24,40},{32,48},{40,56},{48,64},{56,72},{64,... | collective-permute-start | bytes 786440 | tf_op jit(solution)/shard_map/ppermute | solution.py:458
  30.8 9.1 %collective-permute-start.3 = (bf16[4,2,128,128]{3,2,1,0:T(8,128)(2,1)S(1)}, bf16[4,2,128,128]{3,2,1,0:T(8,128)(2,1)S(1)}, u32[]{:S(2)}, u32[]{:S(2)}) collective-permute-start(bf16[4,2,128,128]{3,2,1,0:T(8,128)(2,1)S(1)} %collective-permute-done.2), channel_id=1, source_target_pairs={{0,112},{8,120},{16,0},{24,8},{32,16},{40,24},{48,32},{56,40},{64,... | collective-permute-start | bytes 786440 | tf_op jit(solution)/shard_map/ppermute | solution.py:459
  37.9 12.9 %collective-permute-start.4 = (bf16[4,2,128,128]{3,2,1,0:T(8,128)(2,1)S(1)}, bf16[4,2,128,128]{3,2,1,0:T(8,128)(2,1)S(1)}, u32[]{:S(2)}, u32[]{:S(2)}) collective-permute-start(bf16[4,2,128,128]{3,2,1,0:T(8,128)(2,1)S(1)} %collective-permute-done.1), channel_id=1, source_target_pairs={{0,16},{8,24},{16,32},{24,40},{32,48},{40,56},{48,64},{56,72},{64,... | collective-permute-start | bytes 786440 | tf_op jit(solution)/shard_map/ppermute | solution.py:461
  39.9 12.9 %collective-permute-start.5 = (bf16[4,2,128,128]{3,2,1,0:T(8,128)(2,1)S(1)}, bf16[4,2,128,128]{3,2,1,0:T(8,128)(2,1)S(1)}, u32[]{:S(2)}, u32[]{:S(2)}) collective-permute-start(bf16[4,2,128,128]{3,2,1,0:T(8,128)(2,1)S(1)} %collective-permute-done.3), channel_id=1, source_target_pairs={{0,112},{8,120},{16,0},{24,8},{32,16},{40,24},{48,32},{56,40},{64,... | collective-permute-start | bytes 786440 | tf_op jit(solution)/shard_map/ppermute | solution.py:462
  44.6 22.0 %collective-permute-start.7 = (bf16[20,2,128,128]{3,2,1,0:T(8,128)(2,1)S(1)}, bf16[20,2,128,128]{3,2,1,0:T(8,128)(2,1)S(1)}, u32[]{:S(2)}, u32[]{:S(2)}) collective-permute-start(bf16[20,2,128,128]{3,2,1,0:T(8,128)(2,1)S(1)} %constant_dynamic-update-slice_fusion.early.own_early), channel_id=1, source_target_pairs={{0,8},{8,0},{16,24},{24,16},{32,40},{40,32},{48,56},{56,48},{64,72... | collective-permute-start | bytes 3932168 | tf_op jit(solution)/shard_map/ppermute | solution.py:464
  50.9 10.7 %collective-permute-start.6 = (bf16[4,2,128,128]{3,2,1,0:T(8,128)(2,1)S(1)}, bf16[4,2,128,128]{3,2,1,0:T(8,128)(2,1)S(1)}, u32[]{:S(2)}, u32[]{:S(2)}) collective-permute-start(bf16[4,2,128,128]{3,2,1,0:T(8,128)(2,1)S(1)} %collective-permute-done.4.f3), channel_id=1, source_target_pairs={{0,16},{8,24},{16,32},{24,40},{32,48},{40,56},{48,64},{56,72},{64,... | collective-permute-start | bytes 786440 | tf_op jit(solution)/shard_map/ppermute | solution.py:465
  58.9 5.7 %copy-start.3 = (s32[8,64]{1,0:T(8,128)S(1)}, s32[8,64]{1,0:T(8,128)}, u32[]{:S(2)}) copy-start(s32[8,64]{1,0:T(8,128)} %owner_col.1) | copy-start | bytes 6148
  58.9 5.7 %copy-start.4 = (s32[8,64]{1,0:T(8,128)S(1)}, s32[8,64]{1,0:T(8,128)}, u32[]{:S(2)}) copy-start(s32[8,64]{1,0:T(8,128)} %owner_slot.1) | copy-start | bytes 6148
  61.6 5.0 %collective-permute-start.8 = (bf16[12,2,128,128]{3,2,1,0:T(8,128)(2,1)S(1)}, bf16[12,2,128,128]{3,2,1,0:T(8,128)(2,1)S(1)}, u32[]{:S(2)}, u32[]{:S(2)}) collective-permute-start(bf16[12,2,128,128]{3,2,1,0:T(8,128)(2,1)S(1)} %constant_dynamic-update-slice_fusion.5.own_late), channel_id=1, source_target_pairs={{0,8},{8,0},{16,24},{24,16},{32,40},{40,32},{48,56},{56,48},{64,72... | collective-permute-start | bytes 2359304 | tf_op jit(solution)/shard_map/ppermute | solution.py:469
  67.3 14.3 %collective-permute-start.9 = (bf16[2,128,128]{2,1,0:T(8,128)(2,1)S(1)}, bf16[2,128,128]{2,1,0:T(8,128)(2,1)S(1)}, u32[]{:S(2)}, u32[]{:S(2)}) collective-permute-start(bf16[2,128,128]{2,1,0:T(8,128)(2,1)S(1)} %pick.1), channel_id=1, source_target_pairs={{0,4},{1,5},{2,6},{3,7},{4,0},{5,1},{6,2},{7,3},{8,12},{9,13},{10,... | collective-permute-start | bytes 196616 | tf_op jit(solution)/shard_map/ppermute | solution.py:473

commit v4 on v3

--- a/solution.py
+++ b/solution.py
@@ -25,12 +25,24 @@
 BIG = 1e30
 
 THETA = 500000.0
-FREQ = np.concatenate([THETA ** (-np.arange(HALF) * 2.0 / HD)] * 2).astype(np.float32)[None, :]
+RATES = THETA ** (-np.arange(HALF) * 2.0 / HD)
+
+
+def cos_sin(positions):
+    angles = np.asarray(positions)[:, None] * np.concatenate([RATES, RATES])[None, :]
+    return np.stack([np.cos(angles), np.sin(angles)]).astype(np.float32)
+
+
+RUN_TABLE = cos_sin(np.arange(RUNS) * HALF)
+STEP_TABLE = cos_sin(np.arange(HALF))
+
+
 OFFSETS = (0, -1, 1, -2, 2, -3, 3, 4)
 EARLY = 20
 LATE = SRC - EARLY
 FIRST = 28
-REST = N_CP - FIRST
+MIDDLE = 8
+REST = N_CP - FIRST - MIDDLE
 BIG_GRANT = 24 * 2**20
 
 
@@ -50,16 +62,24 @@
 Z_GROUPS = [[cp_index(z, y, c) for z in range(N_Z)] for y in range(N_Y) for c in range(2)]
 X_GROUPS = [[hi * N_X + x for x in range(N_X)] for hi in range(2)]
 CORE_PAIRS = [(i, i ^ 1) for i in range(N_CP)]
-ZHI_PAIRS = [(i, (i + N_X) % N_TP) for i in range(N_TP)]
-
-
-def angles_of(freq, first_run, second_run, rows):
-    row = lax.broadcasted_iota(jnp.int32, (rows, HD), 0)
-    pos = jnp.where(row < HALF, first_run * HALF + row, second_run * HALF + row - HALF)
-    angles = pos.astype(jnp.float32) * freq
-    low = lax.broadcasted_iota(jnp.int32, (rows, HD), 1) < HALF
-    sin = jnp.sin(angles)
-    return jnp.cos(angles), jnp.where(low, -sin, sin)
+MIRROR_PAIRS = [
+    (cp_index(z, y, c) * N_TP + tp, cp_index(N_Z - 1 - z, y, c) * N_TP + (tp ^ N_X))
+    for z in range(N_Z)
+    for y in range(N_Y)
+    for c in range(2)
+    for tp in range(N_TP)
+]
+
+
+def angles_of(run_table, step_table, first_run):
+    low = lax.broadcasted_iota(jnp.int32, (HALF, HD), 1) < HALF
+    cos, sin = [], []
+    for run in (first_run, RUNS - 1 - first_run):
+        run_cos, run_sin = run_table[0, pl.ds(run, 1), :], run_table[1, pl.ds(run, 1), :]
+        cos.append(run_cos * step_table[0] - run_sin * step_table[1])
+        part = run_sin * step_table[0] + run_cos * step_table[1]
+        sin.append(jnp.where(low, -part, part))
+    return jnp.concatenate(cos, axis=0), jnp.concatenate(sin, axis=0)
 
 
 def turned(x, cos, sin):
@@ -76,9 +96,9 @@
     return me, lax.div(me, 2 * N_Y), lax.rem(lax.div(me, 2), N_Y), lax.rem(me, 2)
 
 
-def pack_kernel(positions, keys, values, freq, out):
-    first = lax.div(positions[lax.axis_index("cp") * ROWS], HALF)
-    cos, sin = angles_of(freq[...], first, RUNS - 1 - first, ROWS)
+def pack_kernel(positions, keys, values, run_table, step_table, out):
+    first = lax.shift_right_logical(positions[lax.axis_index("cp") & 7, 0], 6)
+    cos, sin = angles_of(run_table, step_table, first)
     k_rot = turned(keys[...].astype(jnp.float32), cos, sin).astype(jnp.bfloat16)
     v = values[...]
     for i in range(N_Z):
@@ -87,22 +107,35 @@
 
 
 def pack(positions, keys, values):
+    def whole(*shape):
+        return pl.BlockSpec(shape, lambda i: (0,) * len(shape))
+
     return pl.pallas_call(
         pack_kernel,
+        grid=(1,),
         out_shape=jax.ShapeDtypeStruct((N_Z, 2, ROWS, HD), jnp.bfloat16),
-        in_specs=[SMEM, VMEM, VMEM, VMEM],
-        out_specs=VMEM,
+        in_specs=[
+            pl.BlockSpec(
+                (8, ROWS),
+                lambda i: (lax.div(lax.axis_index("cp"), 8), 0),
+                memory_space=pltpu.SMEM,
+            ),
+            whole(ROWS, HD),
+            whole(ROWS, HD),
+            whole(2, RUNS, HD),
+            whole(2, HALF, HD),
+        ],
+        out_specs=whole(N_Z, 2, ROWS, HD),
         cost_estimate=pl.CostEstimate(flops=1_000_000, bytes_accessed=400_000, transcendentals=0),
         name="pack",
-    )(positions, keys, values, jnp.asarray(FREQ))
-
-
-def turn_kernel(positions, queries, freq, after, q_rot, runs):
-    del after
+    )(positions.reshape(N_CP, ROWS), keys, values, jnp.asarray(RUN_TABLE), jnp.asarray(STEP_TABLE))
+
+
+def turn_kernel(positions, queries, run_table, step_table, q_rot, runs):
     for s in range(N_CP):
         runs[s] = lax.shift_right_logical(positions[s * ROWS], 6)
     my_run = runs[lax.axis_index("cp")]
-    cos, sin = angles_of(freq[...], my_run, RUNS - 1 - my_run, ROWS)
+    cos, sin = angles_of(run_table, step_table, my_run)
     for h in range(KVH):
         q = turned(queries[:, h * HD : (h + 1) * HD].astype(jnp.float32), cos, sin)
         q = q.astype(jnp.bfloat16)
@@ -110,53 +143,49 @@
         q_rot[1, h * HALF : (h + 1) * HALF, :] = q[HALF:]
 
 
-def turn(positions, queries, after):
+def turn(positions, queries):
     return pl.pallas_call(
         turn_kernel,
         out_shape=(
             jax.ShapeDtypeStruct((2, KVH * HALF, HD), jnp.bfloat16),
             jax.ShapeDtypeStruct((N_CP,), jnp.int32),
         ),
-        in_specs=[SMEM, VMEM, VMEM, ANY],
+        in_specs=[SMEM, VMEM, VMEM, VMEM],
         out_specs=(VMEM, SMEM),
         compiler_params=pltpu.CompilerParams(vmem_limit_bytes=BIG_GRANT),
         cost_estimate=pl.CostEstimate(flops=2_000_000, bytes_accessed=600_000, transcendentals=0),
         name="turn",
-    )(positions, queries, jnp.asarray(FREQ), after)
-
-
-LIST_ROWS = ((0, 1), (2, 3))
-MISC = 4
-AT_COUNT, AT_RUN, AT_PICK = 0, 4, 8
+    )(positions, queries, jnp.asarray(RUN_TABLE), jnp.asarray(STEP_TABLE))
+
+
+LIST_ROWS = ((0, 1), (2, 3), (4, 5))
+MISC = 6
+AT_COUNT, AT_RUN = 0, 8
+BLOCKS = 7
 
 
 def clip_valid(counts, run):
     return jnp.clip(counts[lax.shift_right_logical(run, 1)] - (run & 1) * HALF, 0, HALF)
 
 
-def page_of(owner_row, head, me):
-    page = jnp.int32(0)
-    for p in range(N_CP):
-        page = jnp.where(owner_row[head, p] == me, p, page)
-    return page
-
-
-def lists_kernel(runs, counts, owner_row, after, table):
-    del after
-    me, z_me, y_me, core = coordinates()
+def lists_kernel(runs, counts, table):
+    me, _, y_me, core = coordinates()
     my_run = runs[me]
 
-    for part in range(2):
+    for part in range(3):
         if part == 0:
             blocks = [(0, b) for b in range(FIRST)]
+        elif part == 1:
+            blocks = [(1, b) for b in range(MIDDLE)]
         else:
-            blocks = [(0, b) for b in range(FIRST, SRC)] + [(1, b) for b in range(SRC)]
+            blocks = [(0, b) for b in range(FIRST, SRC)] + [(1, b) for b in range(MIDDLE, SRC)]
         n_low, n_high = jnp.int32(0), jnp.int32(0)
         low, high = LIST_ROWS[part]
         for b, (side, at) in enumerate(blocks):
             src_y = (y_me + OFFSETS[at // N_Z]) & (N_Y - 1)
             src_core = core if side == 0 else 1 - core
-            run = runs[((at % N_Z)) * 2 * N_Y + src_y * 2 + src_core]
+            run = runs[(at % N_Z) * 2 * N_Y + src_y * 2 + src_core]
+            table[BLOCKS, run] = side * SRC + at
             first = b * 256 + clip_valid(counts, run)
             second = b * 256 + 128 + clip_valid(counts, RUNS - 1 - run)
             table[high, n_high] = first
@@ -172,39 +201,31 @@
         table[MISC, AT_COUNT + high] = n_high
     table[MISC, AT_RUN] = my_run
 
-    page = page_of(owner_row, lax.axis_index("tp"), me)
-    for half in range(2):
-        run = page * 2 + half
-        second = run >= N_CP
-        j = jnp.where(second, RUNS - 1 - run, run)
-        src = jnp.int32(0)
-        for s in range(N_CP):
-            src = jnp.where(runs[s] == j, s, src)
-        src_core = src & 1
-        off = (lax.shift_right_logical(src, 1) - y_me) & (N_Y - 1)
-        order = jnp.where(off < N_Y // 2, 2 * off, 2 * (N_Y - off) - 1)
-        at = AT_PICK + 4 * half
-        table[MISC, at] = (src_core != core).astype(jnp.int32)
-        table[MISC, at + 1] = order * N_Z + (lax.shift_right_logical(src, 4))
-        table[MISC, at + 2] = second.astype(jnp.int32)
-        table[MISC, at + 3] = clip_valid(counts, run)
-
-
-def lists(runs, counts, owner_row, after):
+
+def lists(runs, counts):
     return pl.pallas_call(
         lists_kernel,
         out_shape=jax.ShapeDtypeStruct((8, LANES), jnp.int32),
-        in_specs=[SMEM, SMEM, SMEM, ANY],
+        in_specs=[SMEM, SMEM],
         out_specs=SMEM,
         compiler_params=pltpu.CompilerParams(vmem_limit_bytes=BIG_GRANT),
         cost_estimate=pl.CostEstimate(flops=2_000_000, bytes_accessed=300_000, transcendentals=0),
         name="lists",
-    )(runs, counts, owner_row, after)
-
-
-def route_kernel(owner_row, owner_col, owner_slot, after, table):
-    del after
-    me = lax.axis_index("cp")
+    )(runs, counts)
+
+
+AT_PLACE, AT_PICK = 0, 8
+
+
+def page_of(owner_row, head, me):
+    page = jnp.int32(0)
+    for p in range(N_CP):
+        page = jnp.where(owner_row[head, p] == me, p, page)
+    return page
+
+
+def route_kernel(lists, counts, owner_row, owner_col, owner_slot, table):
+    me, z_me, _, _ = coordinates()
     tp = lax.axis_index("tp")
     for i in range(N_X):
         for d in range(2):
@@ -213,17 +234,30 @@
             mine = owner_col[head, p] == tp
             table[i * 2 + d] = jnp.where(mine, owner_slot[head, p], -1)
 
-
-def route(owner_row, owner_col, owner_slot, after):
+    for k in range(4):
+        row = me if k < 2 else me + (N_Z - 1 - 2 * z_me) * 2 * N_Y
+        if k % 2 == 0:
+            page = page_of(owner_row, tp, row)
+        run = page * 2 + k % 2
+        second = run >= N_CP
+        block = lists[BLOCKS, jnp.where(second, RUNS - 1 - run, run)]
+        at = AT_PICK + 4 * k
+        table[at] = lax.shift_right_logical(block, 5)
+        table[at + 1] = block & (SRC - 1)
+        table[at + 2] = second.astype(jnp.int32)
+        table[at + 3] = clip_valid(counts, run)
+
+
+def route(lists, counts, owner_row, owner_col, owner_slot):
     return pl.pallas_call(
         route_kernel,
-        out_shape=jax.ShapeDtypeStruct((8,), jnp.int32),
-        in_specs=[SMEM, SMEM, SMEM, ANY],
+        out_shape=jax.ShapeDtypeStruct((LANES,), jnp.int32),
+        in_specs=[SMEM] * 5,
         out_specs=SMEM,
         compiler_params=pltpu.CompilerParams(vmem_limit_bytes=BIG_GRANT),
         cost_estimate=pl.CostEstimate(flops=2_000_000, bytes_accessed=300_000, transcendentals=0),
         name="route",
-    )(owner_row, owner_col, owner_slot, after)
+    )(lists, counts, owner_row, owner_col, owner_slot)
 
 
 COLS = KVH * HALF
@@ -277,9 +311,12 @@
 
 def copy_blocks(pieces, kv, sems):
     copies, at = [], 0
-    for i, piece in enumerate(pieces):
-        size = piece.shape[0]
-        copies.append(pltpu.make_async_copy(piece, kv.at[pl.ds(at, size)], sems.at[i]))
+    for i, (piece, start, size) in enumerate(pieces):
+        copies.append(
+            pltpu.make_async_copy(
+                piece.at[pl.ds(start, size)], kv.at[pl.ds(at, size)], sems.at[i]
+            )
+        )
         at += size
     for copy in copies:
         copy.start()
@@ -288,7 +325,7 @@
 
 
 def first_kernel(table, counts, q_rot, early, f3, b3, tops, totals, accs, kv, sems):
-    copy_blocks((early, f3, b3), kv, sems)
+    copy_blocks(((early, 0, EARLY), (f3, 0, N_Z), (b3, 0, N_Z)), kv, sems)
     _, z_me, _, _ = coordinates()
     my_run = table[MISC, AT_RUN]
     key = lax.broadcasted_iota(jnp.int32, (HALF, COLS), 0)
@@ -334,11 +371,39 @@
     )(table, counts, q_rot, early, f3, b3)
 
 
-def rest_kernel(table, q_rot, tops, totals, accs, f4, early, late, out, kv, sems):
-    copy_blocks((f4, early, late), kv, sems)
+def middle_kernel(table, q_rot, tops, totals, accs, other, new_tops, new_totals, new_accs, kv, sem):
+    copy = pltpu.make_async_copy(other.at[pl.ds(0, MIDDLE)], kv, sem)
+    copy.start()
+    copy.wait()
     for part in range(2):
         state = tops[part], totals[part], accs[part]
-        _, total, acc = fold_list(table, LIST_ROWS[1][part], q_rot[part], kv, state)
+        state = fold_list(table, LIST_ROWS[1][part], q_rot[part], kv, state)
+        new_tops[part], new_totals[part], new_accs[part] = state
+
+
+def attend_middle(table, q_rot, state, other):
+    return pl.pallas_call(
+        middle_kernel,
+        out_shape=STATE,
+        in_specs=[SMEM, VMEM, VMEM, VMEM, VMEM, ANY],
+        out_specs=(VMEM, VMEM, VMEM),
+        scratch_shapes=[
+            pltpu.VMEM((MIDDLE, 2, ROWS, HD), jnp.bfloat16),
+            pltpu.SemaphoreType.DMA,
+        ],
+        compiler_params=pltpu.CompilerParams(vmem_limit_bytes=BIG_GRANT),
+        cost_estimate=pl.CostEstimate(
+            flops=2_000_000_000, bytes_accessed=2_000_000, transcendentals=1_000_000
+        ),
+        name="attend_middle",
+    )(table, q_rot, *state, other)
+
+
+def rest_kernel(table, q_rot, tops, totals, accs, f4, early, late, out, kv, sems):
+    copy_blocks(((f4, 0, N_Z), (early, MIDDLE, EARLY - MIDDLE), (late, 0, LATE)), kv, sems)
+    for part in range(2):
+        state = tops[part], totals[part], accs[part]
+        _, total, acc = fold_list(table, LIST_ROWS[2][part], q_rot[part], kv, state)
         res = jnp.transpose(acc / total).astype(jnp.bfloat16)
         for h in range(KVH):
             out[part * HALF : (part + 1) * HALF, h * HD : (h + 1) * HD] = res[
@@ -364,43 +429,45 @@
     )(table, q_rot, *state, f4, early, late)
 
 
-def pick_kernel(table, own_early, own_late, other_early, other_late, out, held, sems):
-    for half in range(2):
-        at = AT_PICK + 4 * half
-        side, index, second = (table[MISC, at + i] for i in range(3))
+def pick_kernel(table, own_early, own_late, other_early, other_late, mine, sent, held, sems):
+    for k in range(4):
+        at = AT_PICK + 4 * k
+        side, index, second = (table[at + i] for i in range(3))
         rows = pl.ds(pl.multiple_of(second * HALF, HALF), HALF)
         for is_other, early, late in ((0, own_early, own_late), (1, other_early, other_late)):
 
             @pl.when((side == is_other) & (index < EARLY))
-            def _(early=early, half=half, index=index, rows=rows):
+            def _(early=early, k=k, index=index, rows=rows):
+                pltpu.make_async_copy(early.at[index, :, rows], held.at[k], sems.at[k]).start()
+
+            @pl.when((side == is_other) & (index >= EARLY))
+            def _(late=late, k=k, index=index, rows=rows):
                 pltpu.make_async_copy(
-                    early.at[index, :, rows], held.at[half], sems.at[half]
+                    late.at[index - EARLY, :, rows], held.at[k], sems.at[k]
                 ).start()
 
-            @pl.when((side == is_other) & (index >= EARLY))
-            def _(late=late, half=half, index=index, rows=rows):
-                pltpu.make_async_copy(
-                    late.at[index - EARLY, :, rows], held.at[half], sems.at[half]
-                ).start()
-
     row = lax.broadcasted_iota(jnp.int32, (HALF, HD), 0)
-    for half in range(2):
-        pltpu.make_async_copy(own_late.at[0, :, pl.ds(0, HALF)], held.at[half], sems.at[half]).wait()
-        keep = row < table[MISC, AT_PICK + 4 * half + 3]
+    for k in range(4):
+        pltpu.make_async_copy(own_late.at[0, :, pl.ds(0, HALF)], held.at[k], sems.at[k]).wait()
+        keep = row < table[AT_PICK + 4 * k + 3]
+        out = mine if k < 2 else sent
+        rows = slice(k % 2 * HALF, (k % 2 + 1) * HALF)
         for i in range(2):
-            block = jnp.where(keep, held[half, i].astype(jnp.float32), 0.0).astype(jnp.bfloat16)
-            out[i, half * HALF : (half + 1) * HALF, :] = block
+            out[i, rows, :] = jnp.where(keep, held[k, i].astype(jnp.float32), 0.0).astype(
+                jnp.bfloat16
+            )
 
 
 def pick(table, own_early, own_late, other_early, other_late):
+    page = jax.ShapeDtypeStruct((2, PAGE, HD), jnp.bfloat16)
     return pl.pallas_call(
         pick_kernel,
-        out_shape=jax.ShapeDtypeStruct((2, PAGE, HD), jnp.bfloat16),
+        out_shape=(page, page),
         in_specs=[SMEM, ANY, ANY, ANY, ANY],
-        out_specs=VMEM,
+        out_specs=(VMEM, VMEM),
         scratch_shapes=[
-            pltpu.VMEM((2, 2, HALF, HD), jnp.bfloat16),
-            pltpu.SemaphoreType.DMA((2,)),
+            pltpu.VMEM((4, 2, HALF, HD), jnp.bfloat16),
+            pltpu.SemaphoreType.DMA((4,)),
         ],
         compiler_params=pltpu.CompilerParams(vmem_limit_bytes=BIG_GRANT),
         cost_estimate=pl.CostEstimate(flops=100_000, bytes_accessed=300_000, transcendentals=0),
@@ -449,31 +516,34 @@
 def shards(queries, keys, values, positions, counts, owner_row, owner_col, owner_slot):
     tie = lax.optimization_barrier
     spread = pack(positions, keys, values)
+    spread, later_positions = tie((spread, positions))
     unit = lax.all_to_all(spread, "cp", 0, 0, axis_index_groups=Z_GROUPS)
+    unit, q_rot, runs = tie((unit, *turn(later_positions, queries)))
 
     ahead, back = y_pairs(1), y_pairs(-1)
     f1 = lax.ppermute(unit, "cp", ahead)
     b1 = lax.ppermute(unit, "cp", back)
-    f1, q_rot, runs = tie((f1, *turn(positions, queries, unit)))
+    f1, table = tie((f1, lists(runs, counts)))
     f2 = lax.ppermute(f1, "cp", ahead)
     b2 = lax.ppermute(b1, "cp", back)
-    f2, table = tie((f2, lists(runs, counts, owner_row, f1)))
     f3 = lax.ppermute(f2, "cp", ahead)
     b3 = lax.ppermute(b2, "cp", back)
     own_early = jnp.concatenate([unit, f1, b1, f2, b2], axis=0)
     other_early = lax.ppermute(own_early, "cp", CORE_PAIRS)
+    f3, owner_row = tie((f3, owner_row))
     f4 = lax.ppermute(f3, "cp", ahead)
     state = attend_first(table, counts, q_rot, own_early, f3, b3)
-    f4, state = tie((f4, state))
+    routes = route(table, counts, owner_row, owner_col, owner_slot)
+    f4, state, routes = tie((f4, state, routes))
     own_late = jnp.concatenate([f3, b3, f4], axis=0)
     other_late = lax.ppermute(own_late, "cp", CORE_PAIRS)
-    other_late, routes = tie((other_late, route(owner_row, owner_col, owner_slot, f4)))
-
-    picked = pick(table, own_early, own_late, other_early, other_late)
-    across = lax.ppermute(picked, "tp", ZHI_PAIRS)
+    other_late, state = tie((other_late, attend_middle(table, q_rot, state, other_early)))
+
+    mine, sent = pick(routes, own_early, own_late, other_early, other_late)
+    across = lax.ppermute(sent, ("cp", "tp"), MIRROR_PAIRS)
     attended = attend_rest(table, q_rot, state, f4, other_early, other_late)
     across, attended = tie((across, attended))
-    near = jnp.broadcast_to(jnp.stack([picked, across]), (N_X, 2, 2, PAGE, HD))
+    near = jnp.broadcast_to(jnp.stack([mine, across]), (N_X, 2, 2, PAGE, HD))
     pages = lax.all_to_all(near, "tp", 0, 0, axis_index_groups=X_GROUPS)
     pool_keys, pool_values = place(routes, pages)
     return attended, pool_keys, pool_values

time: 96.7 us -> 94.4 us (0.976)
  blocking collectives: 25.6 us -> 12.4 us
  starting transfers between devices: 40 us -> 49 us
  local copies, waits for them, and re-layouts: 2.73 us -> 3.82 us
    all_to_all x1 -> x0, blocking collectives: 13.8 us -> none  [shards(): unit = lax.all_to_all(spread, 'cp', 0, 0, axis_index_groups=Z_GROUPS)]
    all_to_all x0 -> x1, starting transfers between devices: none -> 7.81 us  [shards(): unit = lax.all_to_all(spread, 'cp', 0, 0, axis_index_groups=Z_GROUPS)]
    ppermute x1, waiting for transfers between devices: 0.01 us -> 1.74 us  [shards(): f2 = lax.ppermute(f1, 'cp', ahead)]
    pallas_call x3 -> x4, Pallas kernels: 4.95 us -> 6.51 us  [the longest x1 2.13 us: route(): pl.pallas_call(route_kernel, out_shape=jax.ShapeDtypeStruct((LANES,), jnp...]
    ppermute x1, waiting for transfers between devices: 2.54 us -> 1.29 us  [shards(): f4 = lax.ppermute(f3, 'cp', ahead)]
    unnamed x20 -> x22, local copies, waits for them, and re-layouts: 2.56 us -> 3.66 us
    ppermute x1, starting transfers between devices: 4.05 us -> 5.13 us  [shards(): f1 = lax.ppermute(unit, 'cp', ahead)]
    pallas_call x1, Pallas kernels: 6.39 us -> 5.4 us  [attend_rest(): pl.pallas_call(rest_kernel, out_shape=jax.ShapeDtypeStruct((ROWS, KVH * H...]
  transfers between devices with their start and end apart: 10 -> 11, of which waited for: 1 -> 3; matrix products, arithmetic and copies ran while one was open for 0% -> 0% of each run, Pallas kernels for 20% -> 20%
where the time goes in v4:
time: 94.4 us; the launch traced here: 92.7 us
  starting transfers between devices  49 us (52%)
  Pallas kernels  23 us (24%)
  blocking collectives  12.4 us (13%)
  local copies, waits for them, and re-layouts  3.82 us (4%)
  waiting for transfers between devices  3.52 us (4%)
  between operations  0.96 us (1%)
    all_to_all x1, blocking collectives, shards(): pages = lax.all_to_all(near, 'tp', 0, 0, axis_index_groups=X_GROUPS)  12.4 us
    ppermute x1, starting transfers between devices, shards(): across = lax.ppermute(sent, ('cp', 'tp'), MIRROR_PAIRS)  7.88 us
    all_to_all x1, starting transfers between devices, shards(): unit = lax.all_to_all(spread, 'cp', 0, 0, axis_index_groups=Z_GROUPS)  7.81 us
    ppermute x1, starting transfers between devices, shards(): other_early = lax.ppermute(own_early, 'cp', CORE_PAIRS)  6.63 us
    pallas_call x1, Pallas kernels, attend_rest(): pl.pallas_call(rest_kernel, out_shape=jax.ShapeDtypeStruct((ROWS, KVH * H...  5.4 us
    pallas_call x1, Pallas kernels, attend_first(): pl.pallas_call(first_kernel, out_shape=STATE, in_specs=[SMEM, SMEM, VMEM,...  5.39 us
    ppermute x1, starting transfers between devices, shards(): f1 = lax.ppermute(unit, 'cp', ahead)  5.13 us
    ppermute x1, starting transfers between devices, shards(): b3 = lax.ppermute(b2, 'cp', back)  4.57 us
  transfers between devices with their start and end apart: 11, of which 3 were waited for; matrix products, arithmetic and copies ran while one was open for 0% of the time, Pallas kernels for 20%

profile of v4, /device:TPU:1, one launch (start us, length us, event | category | flops | bytes accessed | tf_op | source)
XLA Modules:
  0.0 92.7 jit_solution(11239318096283043119)
XLA Ops:
  0.6 0.0 copy-start.7
  0.6 1.7 %pack.1 = bf16[4,2,128,128]{3,2,1,0:T(8,128)(2,1)} custom-call(s32[64,128]{1,0:T(8,128)} %bitcast.3, bf16[128,128]{1,0:T(8,128)(2,1)} %keys.1, bf16[128,128]{1,0:T(8,128)(2,1)} %values.1, f32[2,128,128]{2,1,0:T(8,128)} %constant.4.clone.run_table, f32[2,64,128]{2,1,0:T(8,128)} %constant.5.clone.step_table), custom_call_target="tpu_custom_call" | custom-call | flops 1000000 | bytes 400000 | tf_op jit(solution)/shard_map/pack/pallas_call | solution.py:113
  2.4 7.8 %all-to-all-start = ((bf16[4,2,128,128]{3,2,1,0:T(8,128)(2,1)}), bf16[4,2,128,128]{3,2,1,0:T(8,128)(2,1)S(1)}, u32[]{:S(2)}, u32[]{:S(2)}) async-start(bf16[4,2,128,128]{3,2,1,0:T(8,128)(2,1)} %pack.1), calls=%async_computation | async-start | bytes 524288 | tf_op jit(solution)/shard_map/all_to_all | solution.py:520
  10.2 0.0 copy-start
  10.2 0.9 copy-done
  11.1 0.0 copy-start.1
  11.1 0.8 copy-done.1
  11.9 0.0 copy-start.2
  11.9 0.9 %copy-done.2 = bf16[128,1024]{1,0:T(8,128)(2,1)S(1)} copy-done((bf16[128,1024]{1,0:T(8,128)(2,1)S(1)}, bf16[128,1024]{1,0:T(8,128)(2,1)}, u32[]{:S(2)}) %copy-start.2) | copy-done | bytes 262168
  12.9 0.0 copy-start.3
  12.9 0.8 copy-done.3
  13.6 1.7 %turn.1 = (bf16[2,512,128]{2,1,0:T(8,128)(2,1)S(1)}, s32[64]{0:T(128)S(1)}) custom-call(s32[8192]{0:T(1024)S(1)} %copy-done.3, bf16[128,1024]{1,0:T(8,128)(2,1)S(1)} %copy-done.2, f32[2,128,128]{2,1,0:T(8,128)S(1)} %copy-done, f32[2,64,128]{2,1,0:T(8,128)S(1)} %copy-done.1), custom_call_target="tpu_custom_call" | custom-call | flops 2000000 | bytes 600000 | tf_op jit(solution)/shard_map/turn/pallas_call | solution.py:147
  15.4 0.4 all-to-all-done
  15.8 5.1 %collective-permute-start = (bf16[4,2,128,128]{3,2,1,0:T(8,128)(2,1)S(1)}, bf16[4,2,128,128]{3,2,1,0:T(8,128)(2,1)S(1)}, u32[]{:S(2)}, u32[]{:S(2)}) collective-permute-start(bf16[4,2,128,128]{3,2,1,0:T(8,128)(2,1)S(1)} %all-to-all-done), channel_id=1, source_target_pairs={{0,16},{8,24},{16,32},{24,40},{32,48},{40,56},{48,64},{56,72},{64,... | collective-permute-start | bytes 786440 | tf_op jit(solution)/shard_map/ppermute | solution.py:524
  21.0 3.8 %collective-permute-start.4 = (bf16[4,2,128,128]{3,2,1,0:T(8,128)(2,1)S(1)}, bf16[4,2,128,128]{3,2,1,0:T(8,128)(2,1)S(1)}, u32[]{:S(2)}, u32[]{:S(2)}) collective-permute-start(bf16[4,2,128,128]{3,2,1,0:T(8,128)(2,1)S(1)} %all-to-all-done), channel_id=1, source_target_pairs={{0,112},{8,120},{16,0},{24,8},{32,16},{40,24},{48,32},{56,40},{64,... | collective-permute-start | bytes 786440 | tf_op jit(solution)/shard_map/ppermute | solution.py:525
  24.8 0.0 copy-done.7
  24.8 2.4 %lists.1.table = s32[8,128]{1,0:T(8,128)S(1)} custom-call(s32[64]{0:T(128)S(1)} %get-tuple-element.40.runs, s32[64]{0:T(128)S(1)} %copy-done.7), custom_call_target="tpu_custom_call" | custom-call | flops 2000000 | bytes 300000 | tf_op jit(solution)/shard_map/lists/pallas_call | solution.py:206
  27.2 0.0 collective-permute-done
  27.2 1.9 %collective-permute-start.1 = (bf16[4,2,128,128]{3,2,1,0:T(8,128)(2,1)S(1)}, bf16[4,2,128,128]{3,2,1,0:T(8,128)(2,1)S(1)}, u32[]{:S(2)}, u32[]{:S(2)}) collective-permute-start(bf16[4,2,128,128]{3,2,1,0:T(8,128)(2,1)S(1)} %collective-permute-done), channel_id=1, source_target_pairs={{0,16},{8,24},{16,32},{24,40},{32,48},{40,56},{48,64},{56,72},{64,... | collective-permute-start | bytes 786440 | tf_op jit(solution)/shard_map/ppermute | solution.py:527
  29.1 0.0 collective-permute-done.4
  29.1 4.6 %collective-permute-start.5 = (bf16[4,2,128,128]{3,2,1,0:T(8,128)(2,1)S(1)}, bf16[4,2,128,128]{3,2,1,0:T(8,128)(2,1)S(1)}, u32[]{:S(2)}, u32[]{:S(2)}) collective-permute-start(bf16[4,2,128,128]{3,2,1,0:T(8,128)(2,1)S(1)} %collective-permute-done.4), channel_id=1, source_target_pairs={{0,112},{8,120},{16,0},{24,8},{32,16},{40,24},{48,32},{56,40},{64,... | collective-permute-start | bytes 786440 | tf_op jit(solution)/shard_map/ppermute | solution.py:528
  33.8 1.7 %collective-permute-done.1 = bf16[4,2,128,128]{3,2,1,0:T(8,128)(2,1)S(1)} collective-permute-done((bf16[4,2,128,128]{3,2,1,0:T(8,128)(2,1)S(1)}, bf16[4,2,128,128]{3,2,1,0:T(8,128)(2,1)S(1)}, u32[]{:S(2)}, u32[]{:S(2)}) %collective-permute-start.1) | collective-permute-done | bytes 262176 | tf_op jit(solution)/shard_map/ppermute | solution.py:527
  35.5 1.9 %collective-permute-start.2 = (bf16[4,2,128,128]{3,2,1,0:T(8,128)(2,1)S(1)}, bf16[4,2,128,128]{3,2,1,0:T(8,128)(2,1)S(1)}, u32[]{:S(2)}, u32[]{:S(2)}) collective-permute-start(bf16[4,2,128,128]{3,2,1,0:T(8,128)(2,1)S(1)} %collective-permute-done.1), channel_id=1, source_target_pairs={{0,16},{8,24},{16,32},{24,40},{32,48},{40,56},{48,64},{56,72},{64,... | collective-permute-start | bytes 786440 | tf_op jit(solution)/shard_map/ppermute | solution.py:529
  37.4 0.0 collective-permute-done.5
  37.5 4.6 %collective-permute-start.6 = (bf16[4,2,128,128]{3,2,1,0:T(8,128)(2,1)S(1)}, bf16[4,2,128,128]{3,2,1,0:T(8,128)(2,1)S(1)}, u32[]{:S(2)}, u32[]{:S(2)}) collective-permute-start(bf16[4,2,128,128]{3,2,1,0:T(8,128)(2,1)S(1)} %collective-permute-done.5), channel_id=1, source_target_pairs={{0,112},{8,120},{16,0},{24,8},{32,16},{40,24},{48,32},{56,40},{64,... | collective-permute-start | bytes 786440 | tf_op jit(solution)/shard_map/ppermute | solution.py:530
  42.2 0.0 copy-start.4
  42.2 0.0 copy-start.5
  42.2 0.0 copy-start.6
  42.2 6.6 %collective-permute-start.7 = (bf16[20,2,128,128]{3,2,1,0:T(8,128)(2,1)S(1)}, bf16[20,2,128,128]{3,2,1,0:T(8,128)(2,1)S(1)}, u32[]{:S(2)}, u32[]{:S(2)}) collective-permute-start(bf16[20,2,128,128]{3,2,1,0:T(8,128)(2,1)S(1)} %constant_dynamic-update-slice_fusion.early.own_early), channel_id=1, source_target_pairs={{0,8},{8,0},{16,24},{24,16},{32,40},{40,32},{48,56},{56,48},{64,72... | collective-permute-start | bytes 3932168 | tf_op jit(solution)/shard_map/ppermute | solution.py:532
  48.8 0.0 collective-permute-done.2.f3
  48.9 1.9 %collective-permute-start.3 = (bf16[4,2,128,128]{3,2,1,0:T(8,128)(2,1)S(1)}, bf16[4,2,128,128]{3,2,1,0:T(8,128)(2,1)S(1)}, u32[]{:S(2)}, u32[]{:S(2)}) collective-permute-start(bf16[4,2,128,128]{3,2,1,0:T(8,128)(2,1)S(1)} %collective-permute-done.2.f3), channel_id=1, source_target_pairs={{0,16},{8,24},{16,32},{24,40},{32,48},{40,56},{48,64},{56,72},{64,... | collective-permute-start | bytes 786440 | tf_op jit(solution)/shard_map/ppermute | solution.py:534
  50.8 0.0 collective-permute-done.6.b3
  50.8 5.4 %attend_first.1 = (f32[2,1,512]{2,1,0:T(1,128)S(1)}, f32[2,1,512]{2,1,0:T(1,128)S(1)}, f32[2,128,512]{2,1,0:T(8,128)S(1)}) custom-call(s32[8,128]{1,0:T(8,128)S(1)} %lists.1.table, s32[64]{0:T(128)S(1)} %copy-done.7, bf16[2,512,128]{2,1,0:T(8,128)(2,1)S(1)} %get-tuple-element.44.q_rot, ...), custom_call_target="tpu_custom_call" | custom-call | flops 6000000000 | bytes 3000000 | tf_op jit(solution)/shard_map/attend_first/pallas_call | solution.py:357
  56.2 0.0 copy-done.4
  56.2 0.0 copy-done.5
  56.2 0.0 copy-done.6
  56.2 2.1 %route.1.table = s32[128]{0:T(128)S(1)} custom-call(s32[8,128]{1,0:T(8,128)S(1)} %lists.1.table, s32[64]{0:T(128)S(1)} %copy-done.7, s32[8,64]{1,0:T(8,128)S(1)} %copy-done.4, s32[8,64]{1,0:T(8,128)S(1)} %copy-done.5, s32[8,64]{1,0:T(8,128)S(1)} %copy-done.6), custom_call_target="tpu_custom_call" | custom-call | flops 2000000 | bytes 300000 | tf_op jit(solution)/shard_map/route/pallas_call | solution.py:252
  58.4 1.3 %collective-permute-done.3.f4 = bf16[4,2,128,128]{3,2,1,0:T(8,128)(2,1)S(1)} collective-permute-done((bf16[4,2,128,128]{3,2,1,0:T(8,128)(2,1)S(1)}, bf16[4,2,128,128]{3,2,1,0:T(8,128)(2,1)S(1)}, u32[]{:S(2)}, u32[]{:S(2)}) %collective-permute-start.3) | collective-permute-done | bytes 262176 | tf_op jit(solution)/shard_map/ppermute | solution.py:534
  59.8 2.9 %collective-permute-start.8 = (bf16[12,2,128,128]{3,2,1,0:T(8,128)(2,1)S(1)}, bf16[12,2,128,128]{3,2,1,0:T(8,128)(2,1)S(1)}, u32[]{:S(2)}, u32[]{:S(2)}) collective-permute-start(bf16[12,2,128,128]{3,2,1,0:T(8,128)(2,1)S(1)} %constant_dynamic-update-slice_fusion.5.own_late), channel_id=1, source_target_pairs={{0,8},{8,0},{16,24},{24,16},{32,40},{40,32},{48,56},{56,48},{64,72... | collective-permute-start | bytes 2359304 | tf_op jit(solution)/shard_map/ppermute | solution.py:539
  62.6 0.0 collective-permute-done.7.other.other_early.early
  62.7 1.8 %attend_middle.1 = (f32[2,1,512]{2,1,0:T(1,128)S(1)}, f32[2,1,512]{2,1,0:T(1,128)S(1)}, f32[2,128,512]{2,1,0:T(8,128)S(1)}) custom-call(s32[8,128]{1,0:T(8,128)S(1)} %lists.1.table, bf16[2,512,128]{2,1,0:T(8,128)(2,1)S(1)} %get-tuple-element.44.q_rot, f32[2,1,512]{2,1,0:T(1,128)S(1)} %get-tuple-element.51.tops, f32[2,1,512]{2,1,0:T(1,128)S(1)} %get-tuple-element.52.totals, ...), custom_call_target="tpu_custom_call" | custom-call | flops 2000000000 | bytes 2000000 | tf_op jit(solution)/shard_map/attend_middle/pallas_call | solution.py:385
  64.5 0.0 collective-permute-done.8.other_late.late
  64.5 0.8 pick.1
  65.3 7.9 %collective-permute-start.9 = (bf16[2,128,128]{2,1,0:T(8,128)(2,1)S(1)}, bf16[2,128,128]{2,1,0:T(8,128)(2,1)S(1)}, u32[]{:S(2)}, u32[]{:S(2)}) collective-permute-start(bf16[2,128,128]{2,1,0:T(8,128)(2,1)S(1)} %get-tuple-element.58), channel_id=1, source_target_pairs={{0,388},{1,389},{2,390},{3,391},{4,384},{5,385},{6,386},{7,387},{8... | collective-permute-start | bytes 196616 | tf_op jit(solution)/shard_map/ppermute | solution.py:543
  73.2 5.4 %attend_rest.1 = bf16[128,1024]{1,0:T(8,128)(2,1)} custom-call(s32[8,128]{1,0:T(8,128)S(1)} %lists.1.table, bf16[2,512,128]{2,1,0:T(8,128)(2,1)S(1)} %get-tuple-element.44.q_rot, f32[2,1,512]{2,1,0:T(1,128)S(1)} %get-tuple-element.59.tops, f32[2,1,512]{2,1,0:T(1,128)S(1)} %get-tuple-element.60.totals, f32[2,128,512]{2,1,0:T(8,128)S(1)} %get-tuple-element.61.accs, ...), custom_call_target="tpu_custom_call" | custom-call | flops 8000000000 | bytes 4000000 | tf_op jit(solution)/shard_map/attend_rest/pallas_call | solution.py:415
  78.6 0.0 collective-permute-done.9
  78.7 0.1 broadcast_in_dim.3
  78.8 12.4 %all_to_all.10.pages = bf16[4,2,2,128,128]{4,3,2,1,0:T(8,128)(2,1)S(1)} all-to-all(bf16[4,2,2,128,128]{4,3,2,1,0:T(8,128)(2,1)S(1)} %broadcast_in_dim.3), channel_id=1, replica_groups={{0,1,2,3},{4,5,6,7},{8,9,10,11},{12,13,14,15},{16,17,18,19},{20,21,22,2..., dimensions={0} | all-to-all | bytes 1048576 | tf_op jit(solution)/shard_map/all_to_all | solution.py:547
  91.2 1.5 %place.1 = (bf16[2,128,128]{2,1,0:T(8,128)(2,1)}, bf16[2,128,128]{2,1,0:T(8,128)(2,1)}) custom-call(s32[128]{0:T(128)S(1)} %route.1.table, bf16[4,2,2,128,128]{4,3,2,1,0:T(8,128)(2,1)S(1)} %all_to_all.10.pages), custom_call_target="tpu_custom_call" | custom-call | flops 100000 | bytes 800000 | tf_op jit(solution)/shard_map/place/pallas_call | solution.py:504
  (9 shorter events, 0.3 us)
Async XLA Ops:
  0.6 24.2 %copy-start.7 = (s32[64]{0:T(128)S(1)}, s32[64]{0:T(128)}, u32[]{:S(2)}) copy-start(s32[64]{0:T(128)} %counts.5) | copy-start | bytes 772
  2.4 13.4 %all-to-all-start = ((bf16[4,2,128,128]{3,2,1,0:T(8,128)(2,1)}), bf16[4,2,128,128]{3,2,1,0:T(8,128)(2,1)S(1)}, u32[]{:S(2)}, u32[]{:S(2)}) async-start(bf16[4,2,128,128]{3,2,1,0:T(8,128)(2,1)} %pack.1), calls=%async_computation | async-start | bytes 524288 | tf_op jit(solution)/shard_map/all_to_all | solution.py:520
  10.2 0.9 copy-start
  11.1 0.8 copy-start.1
  11.9 0.9 %copy-start.2 = (bf16[128,1024]{1,0:T(8,128)(2,1)S(1)}, bf16[128,1024]{1,0:T(8,128)(2,1)}, u32[]{:S(2)}) copy-start(bf16[128,1024]{1,0:T(8,128)(2,1)} %queries.1) | copy-start | bytes 786436
  12.9 0.8 copy-start.3
  15.8 11.4 %collective-permute-start = (bf16[4,2,128,128]{3,2,1,0:T(8,128)(2,1)S(1)}, bf16[4,2,128,128]{3,2,1,0:T(8,128)(2,1)S(1)}, u32[]{:S(2)}, u32[]{:S(2)}) collective-permute-start(bf16[4,2,128,128]{3,2,1,0:T(8,128)(2,1)S(1)} %all-to-all-done), channel_id=1, source_target_pairs={{0,16},{8,24},{16,32},{24,40},{32,48},{40,56},{48,64},{56,72},{64,... | collective-permute-start | bytes 786440 | tf_op jit(solution)/shard_map/ppermute | solution.py:524
  21.0 8.2 %collective-permute-start.4 = (bf16[4,2,128,128]{3,2,1,0:T(8,128)(2,1)S(1)}, bf16[4,2,128,128]{3,2,1,0:T(8,128)(2,1)S(1)}, u32[]{:S(2)}, u32[]{:S(2)}) collective-permute-start(bf16[4,2,128,128]{3,2,1,0:T(8,128)(2,1)S(1)} %all-to-all-done), channel_id=1, source_target_pairs={{0,112},{8,120},{16,0},{24,8},{32,16},{40,24},{48,32},{56,40},{64,... | collective-permute-start | bytes 786440 | tf_op jit(solution)/shard_map/ppermute | solution.py:525
  27.2 8.3 %collective-permute-start.1 = (bf16[4,2,128,128]{3,2,1,0:T(8,128)(2,1)S(1)}, bf16[4,2,128,128]{3,2,1,0:T(8,128)(2,1)S(1)}, u32[]{:S(2)}, u32[]{:S(2)}) collective-permute-start(bf16[4,2,128,128]{3,2,1,0:T(8,128)(2,1)S(1)} %collective-permute-done), channel_id=1, source_target_pairs={{0,16},{8,24},{16,32},{24,40},{32,48},{40,56},{48,64},{56,72},{64,... | collective-permute-start | bytes 786440 | tf_op jit(solution)/shard_map/ppermute | solution.py:527
  29.1 8.3 %collective-permute-start.5 = (bf16[4,2,128,128]{3,2,1,0:T(8,128)(2,1)S(1)}, bf16[4,2,128,128]{3,2,1,0:T(8,128)(2,1)S(1)}, u32[]{:S(2)}, u32[]{:S(2)}) collective-permute-start(bf16[4,2,128,128]{3,2,1,0:T(8,128)(2,1)S(1)} %collective-permute-done.4), channel_id=1, source_target_pairs={{0,112},{8,120},{16,0},{24,8},{32,16},{40,24},{48,32},{56,40},{64,... | collective-permute-start | bytes 786440 | tf_op jit(solution)/shard_map/ppermute | solution.py:528
  35.5 13.3 %collective-permute-start.2 = (bf16[4,2,128,128]{3,2,1,0:T(8,128)(2,1)S(1)}, bf16[4,2,128,128]{3,2,1,0:T(8,128)(2,1)S(1)}, u32[]{:S(2)}, u32[]{:S(2)}) collective-permute-start(bf16[4,2,128,128]{3,2,1,0:T(8,128)(2,1)S(1)} %collective-permute-done.1), channel_id=1, source_target_pairs={{0,16},{8,24},{16,32},{24,40},{32,48},{40,56},{48,64},{56,72},{64,... | collective-permute-start | bytes 786440 | tf_op jit(solution)/shard_map/ppermute | solution.py:529
  37.5 13.3 %collective-permute-start.6 = (bf16[4,2,128,128]{3,2,1,0:T(8,128)(2,1)S(1)}, bf16[4,2,128,128]{3,2,1,0:T(8,128)(2,1)S(1)}, u32[]{:S(2)}, u32[]{:S(2)}) collective-permute-start(bf16[4,2,128,128]{3,2,1,0:T(8,128)(2,1)S(1)} %collective-permute-done.5), channel_id=1, source_target_pairs={{0,112},{8,120},{16,0},{24,8},{32,16},{40,24},{48,32},{56,40},{64,... | collective-permute-start | bytes 786440 | tf_op jit(solution)/shard_map/ppermute | solution.py:530
  42.2 14.0 %copy-start.4 = (s32[8,64]{1,0:T(8,128)S(1)}, s32[8,64]{1,0:T(8,128)}, u32[]{:S(2)}) copy-start(s32[8,64]{1,0:T(8,128)} %owner_row) | copy-start | bytes 6148
  42.2 14.0 %copy-start.5 = (s32[8,64]{1,0:T(8,128)S(1)}, s32[8,64]{1,0:T(8,128)}, u32[]{:S(2)}) copy-start(s32[8,64]{1,0:T(8,128)} %owner_col.1) | copy-start | bytes 6148
  42.2 14.0 %copy-start.6 = (s32[8,64]{1,0:T(8,128)S(1)}, s32[8,64]{1,0:T(8,128)}, u32[]{:S(2)}) copy-start(s32[8,64]{1,0:T(8,128)} %owner_slot.1) | copy-start | bytes 6148
  42.2 20.4 %collective-permute-start.7 = (bf16[20,2,128,128]{3,2,1,0:T(8,128)(2,1)S(1)}, bf16[20,2,128,128]{3,2,1,0:T(8,128)(2,1)S(1)}, u32[]{:S(2)}, u32[]{:S(2)}) collective-permute-start(bf16[20,2,128,128]{3,2,1,0:T(8,128)(2,1)S(1)} %constant_dynamic-update-slice_fusion.early.own_early), channel_id=1, source_target_pairs={{0,8},{8,0},{16,24},{24,16},{32,40},{40,32},{48,56},{56,48},{64,72... | collective-permute-start | bytes 3932168 | tf_op jit(solution)/shard_map/ppermute | solution.py:532
  48.9 10.9 %collective-permute-start.3 = (bf16[4,2,128,128]{3,2,1,0:T(8,128)(2,1)S(1)}, bf16[4,2,128,128]{3,2,1,0:T(8,128)(2,1)S(1)}, u32[]{:S(2)}, u32[]{:S(2)}) collective-permute-start(bf16[4,2,128,128]{3,2,1,0:T(8,128)(2,1)S(1)} %collective-permute-done.2.f3), channel_id=1, source_target_pairs={{0,16},{8,24},{16,32},{24,40},{32,48},{40,56},{48,64},{56,72},{64,... | collective-permute-start | bytes 786440 | tf_op jit(solution)/shard_map/ppermute | solution.py:534
  59.8 4.8 %collective-permute-start.8 = (bf16[12,2,128,128]{3,2,1,0:T(8,128)(2,1)S(1)}, bf16[12,2,128,128]{3,2,1,0:T(8,128)(2,1)S(1)}, u32[]{:S(2)}, u32[]{:S(2)}) collective-permute-start(bf16[12,2,128,128]{3,2,1,0:T(8,128)(2,1)S(1)} %constant_dynamic-update-slice_fusion.5.own_late), channel_id=1, source_target_pairs={{0,8},{8,0},{16,24},{24,16},{32,40},{40,32},{48,56},{56,48},{64,72... | collective-permute-start | bytes 2359304 | tf_op jit(solution)/shard_map/ppermute | solution.py:539
  65.3 13.3 %collective-permute-start.9 = (bf16[2,128,128]{2,1,0:T(8,128)(2,1)S(1)}, bf16[2,128,128]{2,1,0:T(8,128)(2,1)S(1)}, u32[]{:S(2)}, u32[]{:S(2)}) collective-permute-start(bf16[2,128,128]{2,1,0:T(8,128)(2,1)S(1)} %get-tuple-element.58), channel_id=1, source_target_pairs={{0,388},{1,389},{2,390},{3,391},{4,384},{5,385},{6,386},{7,387},{8... | collective-permute-start | bytes 196616 | tf_op jit(solution)/shard_map/ppermute | solution.py:543

commit v5 on v4

--- a/solution.py
+++ b/solution.py
@@ -38,11 +38,9 @@
 
 
 OFFSETS = (0, -1, 1, -2, 2, -3, 3, 4)
-EARLY = 20
-LATE = SRC - EARLY
 FIRST = 28
-MIDDLE = 8
-REST = N_CP - FIRST - MIDDLE
+MIDDLE = SRC - FIRST
+REST = SRC
 BIG_GRANT = 24 * 2**20
 
 
@@ -173,15 +171,11 @@
     my_run = runs[me]
 
     for part in range(3):
-        if part == 0:
-            blocks = [(0, b) for b in range(FIRST)]
-        elif part == 1:
-            blocks = [(1, b) for b in range(MIDDLE)]
-        else:
-            blocks = [(0, b) for b in range(FIRST, SRC)] + [(1, b) for b in range(MIDDLE, SRC)]
+        side = part // 2
+        start, stop = ((0, FIRST), (FIRST, SRC), (0, SRC))[part]
         n_low, n_high = jnp.int32(0), jnp.int32(0)
         low, high = LIST_ROWS[part]
-        for b, (side, at) in enumerate(blocks):
+        for b, at in enumerate(range(start, stop)):
             src_y = (y_me + OFFSETS[at // N_Z]) & (N_Y - 1)
             src_core = core if side == 0 else 1 - core
             run = runs[(at % N_Z) * 2 * N_Y + src_y * 2 + src_core]
@@ -234,18 +228,19 @@
             mine = owner_col[head, p] == tp
             table[i * 2 + d] = jnp.where(mine, owner_slot[head, p], -1)
 
-    for k in range(4):
-        row = me if k < 2 else me + (N_Z - 1 - 2 * z_me) * 2 * N_Y
+    for k in range(8):
+        row = me if k < 4 else me ^ 1
+        if k // 2 % 2 == 1:
+            row = row + (N_Z - 1 - 2 * z_me) * 2 * N_Y
         if k % 2 == 0:
             page = page_of(owner_row, tp, row)
         run = page * 2 + k % 2
         second = run >= N_CP
         block = lists[BLOCKS, jnp.where(second, RUNS - 1 - run, run)]
-        at = AT_PICK + 4 * k
-        table[at] = lax.shift_right_logical(block, 5)
-        table[at + 1] = block & (SRC - 1)
-        table[at + 2] = second.astype(jnp.int32)
-        table[at + 3] = clip_valid(counts, run)
+        at = AT_PICK + 3 * k
+        table[at] = block & (SRC - 1)
+        table[at + 1] = second.astype(jnp.int32)
+        table[at + 2] = jnp.where(block < SRC, clip_valid(counts, run), 0)
 
 
 def route(lists, counts, owner_row, owner_col, owner_slot):
@@ -324,8 +319,9 @@
         copy.wait()
 
 
-def first_kernel(table, counts, q_rot, early, f3, b3, tops, totals, accs, kv, sems):
-    copy_blocks(((early, 0, EARLY), (f3, 0, N_Z), (b3, 0, N_Z)), kv, sems)
+def first_kernel(table, counts, q_rot, *refs):
+    pieces, (tops, totals, accs, kv, sems) = refs[:-5], refs[-5:]
+    copy_blocks([(piece, 0, N_Z) for piece in pieces], kv, sems)
     _, z_me, _, _ = coordinates()
     my_run = table[MISC, AT_RUN]
     key = lax.broadcasted_iota(jnp.int32, (HALF, COLS), 0)
@@ -353,26 +349,26 @@
 )
 
 
-def attend_first(table, counts, q_rot, early, f3, b3):
+def attend_first(table, counts, q_rot, *pieces):
     return pl.pallas_call(
         first_kernel,
         out_shape=STATE,
-        in_specs=[SMEM, SMEM, VMEM, ANY, ANY, ANY],
+        in_specs=[SMEM, SMEM, VMEM] + [ANY] * len(pieces),
         out_specs=(VMEM, VMEM, VMEM),
         scratch_shapes=[
             pltpu.VMEM((FIRST, 2, ROWS, HD), jnp.bfloat16),
-            pltpu.SemaphoreType.DMA((3,)),
+            pltpu.SemaphoreType.DMA((len(pieces),)),
         ],
         compiler_params=pltpu.CompilerParams(vmem_limit_bytes=BIG_GRANT),
         cost_estimate=pl.CostEstimate(
             flops=6_000_000_000, bytes_accessed=3_000_000, transcendentals=2_000_000
         ),
         name="attend_first",
-    )(table, counts, q_rot, early, f3, b3)
+    )(table, counts, q_rot, *pieces)
 
 
 def middle_kernel(table, q_rot, tops, totals, accs, other, new_tops, new_totals, new_accs, kv, sem):
-    copy = pltpu.make_async_copy(other.at[pl.ds(0, MIDDLE)], kv, sem)
+    copy = pltpu.make_async_copy(other, kv, sem)
     copy.start()
     copy.wait()
     for part in range(2):
@@ -399,8 +395,10 @@
     )(table, q_rot, *state, other)
 
 
-def rest_kernel(table, q_rot, tops, totals, accs, f4, early, late, out, kv, sems):
-    copy_blocks(((f4, 0, N_Z), (early, MIDDLE, EARLY - MIDDLE), (late, 0, LATE)), kv, sems)
+def rest_kernel(table, q_rot, tops, totals, accs, other, out, kv, sem):
+    copy = pltpu.make_async_copy(other, kv, sem)
+    copy.start()
+    copy.wait()
     for part in range(2):
         state = tops[part], totals[part], accs[part]
         _, total, acc = fold_list(table, LIST_ROWS[2][part], q_rot[part], kv, state)
@@ -411,68 +409,77 @@
             ]
 
 
-def attend_rest(table, q_rot, state, f4, early, late):
+def attend_rest(table, q_rot, state, other):
     return pl.pallas_call(
         rest_kernel,
         out_shape=jax.ShapeDtypeStruct((ROWS, KVH * HD), jnp.bfloat16),
-        in_specs=[SMEM, VMEM, VMEM, VMEM, VMEM, ANY, ANY, ANY],
+        in_specs=[SMEM, VMEM, VMEM, VMEM, VMEM, ANY],
         out_specs=VMEM,
         scratch_shapes=[
             pltpu.VMEM((REST, 2, ROWS, HD), jnp.bfloat16),
-            pltpu.SemaphoreType.DMA((3,)),
+            pltpu.SemaphoreType.DMA,
         ],
         compiler_params=pltpu.CompilerParams(vmem_limit_bytes=BIG_GRANT),
         cost_estimate=pl.CostEstimate(
             flops=8_000_000_000, bytes_accessed=4_000_000, transcendentals=2_000_000
         ),
         name="attend_rest",
-    )(table, q_rot, *state, f4, early, late)
-
-
-def pick_kernel(table, own_early, own_late, other_early, other_late, mine, sent, held, sems):
-    for k in range(4):
-        at = AT_PICK + 4 * k
-        side, index, second = (table[at + i] for i in range(3))
+    )(table, q_rot, *state, other)
+
+
+def pick_kernel(table, own, mine, theirs, held, sems):
+    copies = []
+    for k in range(8):
+        index, second = table[AT_PICK + 3 * k], table[AT_PICK + 3 * k + 1]
         rows = pl.ds(pl.multiple_of(second * HALF, HALF), HALF)
-        for is_other, early, late in ((0, own_early, own_late), (1, other_early, other_late)):
-
-            @pl.when((side == is_other) & (index < EARLY))
-            def _(early=early, k=k, index=index, rows=rows):
-                pltpu.make_async_copy(early.at[index, :, rows], held.at[k], sems.at[k]).start()
-
-            @pl.when((side == is_other) & (index >= EARLY))
-            def _(late=late, k=k, index=index, rows=rows):
-                pltpu.make_async_copy(
-                    late.at[index - EARLY, :, rows], held.at[k], sems.at[k]
-                ).start()
-
+        copies.append(pltpu.make_async_copy(own.at[index, :, rows], held.at[k], sems.at[k]))
+        copies[-1].start()
     row = lax.broadcasted_iota(jnp.int32, (HALF, HD), 0)
-    for k in range(4):
-        pltpu.make_async_copy(own_late.at[0, :, pl.ds(0, HALF)], held.at[k], sems.at[k]).wait()
-        keep = row < table[AT_PICK + 4 * k + 3]
-        out = mine if k < 2 else sent
+    for k in range(8):
+        copies[k].wait()
+        keep = row < table[AT_PICK + 3 * k + 2]
+        out = mine if k < 4 else theirs
         rows = slice(k % 2 * HALF, (k % 2 + 1) * HALF)
         for i in range(2):
-            out[i, rows, :] = jnp.where(keep, held[k, i].astype(jnp.float32), 0.0).astype(
-                jnp.bfloat16
-            )
-
-
-def pick(table, own_early, own_late, other_early, other_late):
-    page = jax.ShapeDtypeStruct((2, PAGE, HD), jnp.bfloat16)
+            out[k // 2 % 2, i, rows, :] = jnp.where(
+                keep, held[k, i].astype(jnp.float32), 0.0
+            ).astype(jnp.bfloat16)
+
+
+def pick(table, own):
+    pages = jax.ShapeDtypeStruct((2, 2, PAGE, HD), jnp.bfloat16)
     return pl.pallas_call(
         pick_kernel,
-        out_shape=(page, page),
-        in_specs=[SMEM, ANY, ANY, ANY, ANY],
+        out_shape=(pages, pages),
+        in_specs=[SMEM, ANY],
         out_specs=(VMEM, VMEM),
         scratch_shapes=[
-            pltpu.VMEM((4, 2, HALF, HD), jnp.bfloat16),
-            pltpu.SemaphoreType.DMA((4,)),
+            pltpu.VMEM((8, 2, HALF, HD), jnp.bfloat16),
+            pltpu.SemaphoreType.DMA((8,)),
         ],
         compiler_params=pltpu.CompilerParams(vmem_limit_bytes=BIG_GRANT),
         cost_estimate=pl.CostEstimate(flops=100_000, bytes_accessed=300_000, transcendentals=0),
         name="pick",
-    )(table, own_early, own_late, other_early, other_late)
+    )(table, own)
+
+
+def spread_kernel(mine, across, out):
+    for i in range(N_X):
+        out[i, 0] = mine[0]
+        out[i, 1] = across[...]
+
+
+def spread(mine, across):
+    return pl.pallas_call(
+        spread_kernel,
+        out_shape=jax.ShapeDtypeStruct((N_X, 2, 2, PAGE, HD), jnp.bfloat16),
+        in_specs=[VMEM, VMEM],
+        out_specs=VMEM,
+        cost_estimate=pl.CostEstimate(
+            flops=100_000_000_000, bytes_accessed=700_000, transcendentals=0
+        ),
+        name="spread",
+    )(mine, across)
 
 
 def place_kernel(table, pages, pool_k, pool_v, sems):
@@ -515,9 +522,8 @@
 
 def shards(queries, keys, values, positions, counts, owner_row, owner_col, owner_slot):
     tie = lax.optimization_barrier
-    spread = pack(positions, keys, values)
-    spread, later_positions = tie((spread, positions))
-    unit = lax.all_to_all(spread, "cp", 0, 0, axis_index_groups=Z_GROUPS)
+    packed, later_positions = tie((pack(positions, keys, values), positions))
+    unit = lax.all_to_all(packed, "cp", 0, 0, axis_index_groups=Z_GROUPS)
     unit, q_rot, runs = tie((unit, *turn(later_positions, queries)))
 
     ahead, back = y_pairs(1), y_pairs(-1)
@@ -528,23 +534,22 @@
     b2 = lax.ppermute(b1, "cp", back)
     f3 = lax.ppermute(f2, "cp", ahead)
     b3 = lax.ppermute(b2, "cp", back)
-    own_early = jnp.concatenate([unit, f1, b1, f2, b2], axis=0)
-    other_early = lax.ppermute(own_early, "cp", CORE_PAIRS)
-    f3, owner_row = tie((f3, owner_row))
     f4 = lax.ppermute(f3, "cp", ahead)
-    state = attend_first(table, counts, q_rot, own_early, f3, b3)
+    state = attend_first(table, counts, q_rot, unit, f1, b1, f2, b2, f3, b3)
     routes = route(table, counts, owner_row, owner_col, owner_slot)
     f4, state, routes = tie((f4, state, routes))
-    own_late = jnp.concatenate([f3, b3, f4], axis=0)
-    other_late = lax.ppermute(own_late, "cp", CORE_PAIRS)
-    other_late, state = tie((other_late, attend_middle(table, q_rot, state, other_early)))
-
-    mine, sent = pick(routes, own_early, own_late, other_early, other_late)
-    across = lax.ppermute(sent, ("cp", "tp"), MIRROR_PAIRS)
-    attended = attend_rest(table, q_rot, state, f4, other_early, other_late)
-    across, attended = tie((across, attended))
-    near = jnp.broadcast_to(jnp.stack([mine, across]), (N_X, 2, 2, PAGE, HD))
-    pages = lax.all_to_all(near, "tp", 0, 0, axis_index_groups=X_GROUPS)
+    own = jnp.concatenate([unit, f1, b1, f2, b2, f3, b3, f4], axis=0)
+
+    mine, theirs = pick(routes, own)
+    pages = mine + lax.ppermute(theirs, "cp", CORE_PAIRS)
+    across = lax.ppermute(pages[1], ("cp", "tp"), MIRROR_PAIRS)
+    pages, state = tie((pages, state))
+    state = attend_middle(table, q_rot, state, f4)
+    own, state = tie((own, state))
+    other = lax.ppermute(own, "cp", CORE_PAIRS)
+    across, state = tie((across, state))
+    pages = lax.all_to_all(spread(pages, across), "tp", 0, 0, axis_index_groups=X_GROUPS)
+    pages, attended = tie((pages, attend_rest(table, q_rot, state, other)))
     pool_keys, pool_values = place(routes, pages)
     return attended, pool_keys, pool_values
 

time: 94.4 us -> 92.3 us (0.978)
  blocking collectives: 12.4 us -> 0 us
  Pallas kernels: 23 us -> 28.6 us
  starting transfers between devices: 49 us -> 51.8 us
  local copies, waits for them, and re-layouts: 3.82 us -> 5.02 us
    all_to_all x1 -> x0, blocking collectives: 12.4 us -> none  [shards(): pages = lax.all_to_all(near, 'tp', 0, 0, axis_index_groups=X_GROUPS)]
    all_to_all x1 -> x2, starting transfers between devices: 7.81 us -> 11.8 us  [the longest x1 7.81 us: shards(): unit = lax.all_to_all(packed, 'cp', 0, 0, axis_index_groups=Z_GROUPS)]
    pallas_call x2 -> x3, Pallas kernels: 6.19 us -> 8.84 us  [the longest x1 6.15 us: attend_first(): pl.pallas_call(first_kernel, out_shape=STATE, in_specs=[SMEM, SMEM, VMEM]...]
    pallas_call x1, Pallas kernels: 5.4 us -> 7.82 us  [attend_rest(): pl.pallas_call(rest_kernel, out_shape=jax.ShapeDtypeStruct((ROWS, KVH * H...]
    unnamed x22 -> x27, local copies, waits for them, and re-layouts: 3.66 us -> 4.98 us
    ppermute x3, starting transfers between devices: 17.4 us -> 16.2 us  [the longest x1 7.35 us: shards(): pages = mine + lax.ppermute(theirs, 'cp', CORE_PAIRS)]
    ppermute x1, waiting for transfers between devices: 1.29 us -> 0.14 us  [shards(): f4 = lax.ppermute(f3, 'cp', ahead)]
  transfers between devices with their start and end apart: 11 -> 12, of which waited for: 3 -> 5; matrix products, arithmetic and copies ran while one was open for 0% -> 0% of each run, Pallas kernels for 20% -> 27%
where the time goes in v5:
time: 92.3 us; the launch traced here: 90.6 us
  starting transfers between devices  51.8 us (56%)
  Pallas kernels  28.6 us (31%)
  local copies, waits for them, and re-layouts  5.02 us (5%)
  waiting for transfers between devices  4.23 us (5%)
  between operations  0.97 us (1%)
    pallas_call x1, Pallas kernels, attend_rest(): pl.pallas_call(rest_kernel, out_shape=jax.ShapeDtypeStruct((ROWS, KVH * H...  7.82 us
    all_to_all x1, starting transfers between devices, shards(): unit = lax.all_to_all(packed, 'cp', 0, 0, axis_index_groups=Z_GROUPS)  7.81 us
    ppermute x1, starting transfers between devices, shards(): pages = mine + lax.ppermute(theirs, 'cp', CORE_PAIRS)  7.35 us
    ppermute x1, starting transfers between devices, shards(): across = lax.ppermute(pages[1], ('cp', 'tp'), MIRROR_PAIRS)  6.88 us
    pallas_call x1, Pallas kernels, attend_first(): pl.pallas_call(first_kernel, out_shape=STATE, in_specs=[SMEM, SMEM, VMEM]...  6.15 us
    ppermute x1, starting transfers between devices, shards(): f1 = lax.ppermute(unit, 'cp', ahead)  5.13 us
    unnamed x27, local copies, waits for them, and re-layouts  4.98 us
    ppermute x1, starting transfers between devices, shards(): b3 = lax.ppermute(b2, 'cp', back)  4.57 us
  transfers between devices with their start and end apart: 12, of which 5 were waited for; matrix products, arithmetic and copies ran while one was open for 0% of the time, Pallas kernels for 27%

profile of v5, /device:TPU:1, one launch (start us, length us, event | category | flops | bytes accessed | tf_op | source)
XLA Modules:
  0.0 90.6 jit_solution(8092778565873023654)
XLA Ops:
  0.6 0.0 copy-start.4
  0.6 0.0 copy-start.5
  0.7 0.0 copy-start.6
  0.7 1.8 %pack.1 = bf16[4,2,128,128]{3,2,1,0:T(8,128)(2,1)} custom-call(s32[64,128]{1,0:T(8,128)} %bitcast.3, bf16[128,128]{1,0:T(8,128)(2,1)} %keys.1, bf16[128,128]{1,0:T(8,128)(2,1)} %values.1, f32[2,128,128]{2,1,0:T(8,128)} %constant.4.clone.run_table, f32[2,64,128]{2,1,0:T(8,128)} %constant.5.clone.step_table), custom_call_target="tpu_custom_call" | custom-call | flops 1000000 | bytes 400000 | tf_op jit(solution)/shard_map/pack/pallas_call | solution.py:111
  2.4 7.8 %all-to-all-start = ((bf16[4,2,128,128]{3,2,1,0:T(8,128)(2,1)}), bf16[4,2,128,128]{3,2,1,0:T(8,128)(2,1)S(1)}, u32[]{:S(2)}, u32[]{:S(2)}) async-start(bf16[4,2,128,128]{3,2,1,0:T(8,128)(2,1)} %pack.1), calls=%async_computation | async-start | bytes 524288 | tf_op jit(solution)/shard_map/all_to_all | solution.py:526
  10.2 0.0 copy-start
  10.2 0.9 copy-done
  11.1 0.0 copy-start.1
  11.1 0.8 copy-done.1
  12.0 0.0 copy-start.2
  12.0 0.9 %copy-done.2 = bf16[128,1024]{1,0:T(8,128)(2,1)S(1)} copy-done((bf16[128,1024]{1,0:T(8,128)(2,1)S(1)}, bf16[128,1024]{1,0:T(8,128)(2,1)}, u32[]{:S(2)}) %copy-start.2) | copy-done | bytes 262168
  12.9 0.0 copy-start.3
  12.9 0.8 copy-done.3
  13.7 1.7 %turn.1 = (bf16[2,512,128]{2,1,0:T(8,128)(2,1)S(1)}, s32[64]{0:T(128)S(1)}) custom-call(s32[8192]{0:T(1024)S(1)} %copy-done.3, bf16[128,1024]{1,0:T(8,128)(2,1)S(1)} %copy-done.2, f32[2,128,128]{2,1,0:T(8,128)S(1)} %copy-done, f32[2,64,128]{2,1,0:T(8,128)S(1)} %copy-done.1), custom_call_target="tpu_custom_call" | custom-call | flops 2000000 | bytes 600000 | tf_op jit(solution)/shard_map/turn/pallas_call | solution.py:145
  15.4 0.4 all-to-all-done.refs_0_
  15.9 5.1 %collective-permute-start = (bf16[4,2,128,128]{3,2,1,0:T(8,128)(2,1)S(1)}, bf16[4,2,128,128]{3,2,1,0:T(8,128)(2,1)S(1)}, u32[]{:S(2)}, u32[]{:S(2)}) collective-permute-start(bf16[4,2,128,128]{3,2,1,0:T(8,128)(2,1)S(1)} %all-to-all-done.refs_0_), channel_id=1, source_target_pairs={{0,16},{8,24},{16,32},{24,40},{32,48},{40,56},{48,64},{56,72},{64,... | collective-permute-start | bytes 786440 | tf_op jit(solution)/shard_map/ppermute | solution.py:530
  21.0 3.8 %collective-permute-start.4 = (bf16[4,2,128,128]{3,2,1,0:T(8,128)(2,1)S(1)}, bf16[4,2,128,128]{3,2,1,0:T(8,128)(2,1)S(1)}, u32[]{:S(2)}, u32[]{:S(2)}) collective-permute-start(bf16[4,2,128,128]{3,2,1,0:T(8,128)(2,1)S(1)} %all-to-all-done.refs_0_), channel_id=1, source_target_pairs={{0,112},{8,120},{16,0},{24,8},{32,16},{40,24},{48,32},{56,40},{64,... | collective-permute-start | bytes 786440 | tf_op jit(solution)/shard_map/ppermute | solution.py:531
  24.8 0.0 copy-start.7
  24.8 0.6 copy-done.7
  25.5 2.4 %lists.1.table = s32[8,128]{1,0:T(8,128)S(1)} custom-call(s32[64]{0:T(128)S(1)} %get-tuple-element.46.runs, s32[64]{0:T(128)S(1)} %copy-done.7), custom_call_target="tpu_custom_call" | custom-call | flops 2000000 | bytes 300000 | tf_op jit(solution)/shard_map/lists/pallas_call | solution.py:200
  27.9 0.0 collective-permute-done.refs_1_
  27.9 1.9 %collective-permute-start.1 = (bf16[4,2,128,128]{3,2,1,0:T(8,128)(2,1)S(1)}, bf16[4,2,128,128]{3,2,1,0:T(8,128)(2,1)S(1)}, u32[]{:S(2)}, u32[]{:S(2)}) collective-permute-start(bf16[4,2,128,128]{3,2,1,0:T(8,128)(2,1)S(1)} %collective-permute-done.refs_1_), channel_id=1, source_target_pairs={{0,16},{8,24},{16,32},{24,40},{32,48},{40,56},{48,64},{56,72},{64,... | collective-permute-start | bytes 786440 | tf_op jit(solution)/shard_map/ppermute | solution.py:533
  29.8 0.0 collective-permute-done.4.refs_2_
  29.8 4.6 %collective-permute-start.5 = (bf16[4,2,128,128]{3,2,1,0:T(8,128)(2,1)S(1)}, bf16[4,2,128,128]{3,2,1,0:T(8,128)(2,1)S(1)}, u32[]{:S(2)}, u32[]{:S(2)}) collective-permute-start(bf16[4,2,128,128]{3,2,1,0:T(8,128)(2,1)S(1)} %collective-permute-done.4.refs_2_), channel_id=1, source_target_pairs={{0,112},{8,120},{16,0},{24,8},{32,16},{40,24},{48,32},{56,40},{64,... | collective-permute-start | bytes 786440 | tf_op jit(solution)/shard_map/ppermute | solution.py:534
  34.5 1.7 %collective-permute-done.1.refs_3_ = bf16[4,2,128,128]{3,2,1,0:T(8,128)(2,1)S(1)} collective-permute-done((bf16[4,2,128,128]{3,2,1,0:T(8,128)(2,1)S(1)}, bf16[4,2,128,128]{3,2,1,0:T(8,128)(2,1)S(1)}, u32[]{:S(2)}, u32[]{:S(2)}) %collective-permute-start.1) | collective-permute-done | bytes 262176 | tf_op jit(solution)/shard_map/ppermute | solution.py:533
  36.2 1.9 %collective-permute-start.2 = (bf16[4,2,128,128]{3,2,1,0:T(8,128)(2,1)S(1)}, bf16[4,2,128,128]{3,2,1,0:T(8,128)(2,1)S(1)}, u32[]{:S(2)}, u32[]{:S(2)}) collective-permute-start(bf16[4,2,128,128]{3,2,1,0:T(8,128)(2,1)S(1)} %collective-permute-done.1.refs_3_), channel_id=1, source_target_pairs={{0,16},{8,24},{16,32},{24,40},{32,48},{40,56},{48,64},{56,72},{64,... | collective-permute-start | bytes 786440 | tf_op jit(solution)/shard_map/ppermute | solution.py:535
  38.1 0.0 collective-permute-done.5.refs_4_
  38.1 4.6 %collective-permute-start.6 = (bf16[4,2,128,128]{3,2,1,0:T(8,128)(2,1)S(1)}, bf16[4,2,128,128]{3,2,1,0:T(8,128)(2,1)S(1)}, u32[]{:S(2)}, u32[]{:S(2)}) collective-permute-start(bf16[4,2,128,128]{3,2,1,0:T(8,128)(2,1)S(1)} %collective-permute-done.5.refs_4_), channel_id=1, source_target_pairs={{0,112},{8,120},{16,0},{24,8},{32,16},{40,24},{48,32},{56,40},{64,... | collective-permute-start | bytes 786440 | tf_op jit(solution)/shard_map/ppermute | solution.py:536
  42.8 0.0 copy-done.4
  42.8 0.0 copy-done.5
  42.8 0.0 copy-done.6
  42.8 2.3 %route.1.table = s32[128]{0:T(128)S(1)} custom-call(s32[8,128]{1,0:T(8,128)S(1)} %lists.1.table, s32[64]{0:T(128)S(1)} %copy-done.7, s32[8,64]{1,0:T(8,128)S(1)} %copy-done.4, s32[8,64]{1,0:T(8,128)S(1)} %copy-done.5, s32[8,64]{1,0:T(8,128)S(1)} %copy-done.6), custom_call_target="tpu_custom_call" | custom-call | flops 2000000 | bytes 300000 | tf_op jit(solution)/shard_map/route/pallas_call | solution.py:247
  45.2 0.0 collective-permute-done.2.refs_5_
  45.2 1.9 %collective-permute-start.3 = (bf16[4,2,128,128]{3,2,1,0:T(8,128)(2,1)S(1)}, bf16[4,2,128,128]{3,2,1,0:T(8,128)(2,1)S(1)}, u32[]{:S(2)}, u32[]{:S(2)}) collective-permute-start(bf16[4,2,128,128]{3,2,1,0:T(8,128)(2,1)S(1)} %collective-permute-done.2.refs_5_), channel_id=1, source_target_pairs={{0,16},{8,24},{16,32},{24,40},{32,48},{40,56},{48,64},{56,72},{64,... | collective-permute-start | bytes 786440 | tf_op jit(solution)/shard_map/ppermute | solution.py:537
  47.1 0.0 collective-permute-done.6.refs_6_
  47.1 6.2 %attend_first.1 = (f32[2,1,512]{2,1,0:T(1,128)S(1)}, f32[2,1,512]{2,1,0:T(1,128)S(1)}, f32[2,128,512]{2,1,0:T(8,128)S(1)}) custom-call(s32[8,128]{1,0:T(8,128)S(1)} %lists.1.table, s32[64]{0:T(128)S(1)} %copy-done.7, bf16[2,512,128]{2,1,0:T(8,128)(2,1)S(1)} %get-tuple-element.49.q_rot, bf16[4,2,128,128]{3,2,1,0:T(8,128)(2,1)S(1)} %all-to-all-done.refs_0_, ...), custom_call_target="tpu_custom_call" | custom-call | flops 6000000000 | bytes 3000000 | tf_op jit(solution)/shard_map/attend_first/pallas_call | solution.py:353
  53.4 0.1 collective-permute-done.3.other
  53.6 0.9 %pick.1 = (bf16[2,2,128,128]{3,2,1,0:T(8,128)(2,1)S(1)}, bf16[2,2,128,128]{3,2,1,0:T(8,128)(2,1)S(1)}) custom-call(s32[128]{0:T(128)S(1)} %route.1.table, bf16[32,2,128,128]{3,2,1,0:T(8,128)(2,1)S(1)} %constant_dynamic-update-slice_fusion.own), custom_call_target="tpu_custom_call" | custom-call | flops 100000 | bytes 300000 | tf_op jit(solution)/shard_map/pick/pallas_call | solution.py:451
  54.5 7.4 %collective-permute-start.7 = (bf16[2,2,128,128]{3,2,1,0:T(8,128)(2,1)S(1)}, bf16[2,2,128,128]{3,2,1,0:T(8,128)(2,1)S(1)}, u32[]{:S(2)}, u32[]{:S(2)}) collective-permute-start(bf16[2,2,128,128]{3,2,1,0:T(8,128)(2,1)S(1)} %get-tuple-element.56), channel_id=1, source_target_pairs={{0,8},{8,0},{16,24},{24,16},{32,40},{40,32},{48,56},{56,48},{64,72... | collective-permute-start | bytes 393224 | tf_op jit(solution)/shard_map/ppermute | solution.py:544
  61.8 1.0 %collective-permute-done.7 = bf16[2,2,128,128]{3,2,1,0:T(8,128)(2,1)S(1)} collective-permute-done((bf16[2,2,128,128]{3,2,1,0:T(8,128)(2,1)S(1)}, bf16[2,2,128,128]{3,2,1,0:T(8,128)(2,1)S(1)}, u32[]{:S(2)}, u32[]{:S(2)}) %collective-permute-start.7) | collective-permute-done | bytes 131104 | tf_op jit(solution)/shard_map/ppermute | solution.py:544
  62.9 0.0 copy-start.8
  62.9 6.9 %collective-permute-start.8 = (bf16[2,128,128]{2,1,0:T(8,128)(2,1)S(1)}, bf16[2,128,128]{2,1,0:T(8,128)(2,1)S(1)}, u32[]{:S(2)}, u32[]{:S(2)}) collective-permute-start(bf16[2,128,128]{2,1,0:T(8,128)(2,1)S(1)} %slice_bitcast_fusion), channel_id=1, source_target_pairs={{0,388},{1,389},{2,390},{3,391},{4,384},{5,385},{6,386},{7,387},{8... | collective-permute-start | bytes 196616 | tf_op jit(solution)/shard_map/ppermute | solution.py:545
  69.8 2.2 %attend_middle.1 = (f32[2,1,512]{2,1,0:T(1,128)S(1)}, f32[2,1,512]{2,1,0:T(1,128)S(1)}, f32[2,128,512]{2,1,0:T(8,128)S(1)}) custom-call(s32[8,128]{1,0:T(8,128)S(1)} %lists.1.table, bf16[2,512,128]{2,1,0:T(8,128)(2,1)S(1)} %get-tuple-element.49.q_rot, f32[2,1,512]{2,1,0:T(1,128)S(1)} %get-tuple-element.61.tops, f32[2,1,512]{2,1,0:T(1,128)S(1)} %get-tuple-element.62.totals, ...), custom_call_target="tpu_custom_call" | custom-call | flops 2000000000 | bytes 2000000 | tf_op jit(solution)/shard_map/attend_middle/pallas_call | solution.py:381
  72.0 0.0 copy-done.8
  72.0 1.9 %collective-permute-start.9 = (bf16[32,2,128,128]{3,2,1,0:T(8,128)(2,1)S(1)}, bf16[32,2,128,128]{3,2,1,0:T(8,128)(2,1)}, u32[]{:S(2)}, u32[]{:S(2)}) collective-permute-start(bf16[32,2,128,128]{3,2,1,0:T(8,128)(2,1)S(1)} %constant_dynamic-update-slice_fusion.own), channel_id=1, source_target_pairs={{0,8},{8,0},{16,24},{24,16},{32,40},{40,32},{48,56},{56,48},{64,72... | collective-permute-start | bytes 6291464 | tf_op jit(solution)/shard_map/ppermute | solution.py:549
  73.9 0.0 collective-permute-done.8.across
  73.9 0.0 copy-start.9
  73.9 0.6 copy-done.9
  74.5 1.8 %spread.1 = bf16[4,2,2,128,128]{4,3,2,1,0:T(8,128)(2,1)} custom-call(bf16[2,2,128,128]{3,2,1,0:T(8,128)(2,1)} %copy-done.8, bf16[2,128,128]{2,1,0:T(8,128)(2,1)} %copy-done.9), custom_call_target="tpu_custom_call" | custom-call | flops 99999997952 | bytes 700000 | tf_op jit(solution)/shard_map/spread/pallas_call | solution.py:473
  76.3 4.0 %all-to-all-start.1 = ((bf16[4,2,2,128,128]{4,3,2,1,0:T(8,128)(2,1)}), bf16[4,2,2,128,128]{4,3,2,1,0:T(8,128)(2,1)S(1)}, u32[]{:S(2)}, u32[]{:S(2)}) async-start(bf16[4,2,2,128,128]{4,3,2,1,0:T(8,128)(2,1)} %spread.1), calls=%async_computation.1 | async-start | bytes 1048576 | tf_op jit(solution)/shard_map/all_to_all | solution.py:551
  80.3 0.0 collective-permute-done.9.other
  80.3 7.8 %attend_rest.1 = bf16[128,1024]{1,0:T(8,128)(2,1)} custom-call(s32[8,128]{1,0:T(8,128)S(1)} %lists.1.table, bf16[2,512,128]{2,1,0:T(8,128)(2,1)S(1)} %get-tuple-element.49.q_rot, f32[2,1,512]{2,1,0:T(1,128)S(1)} %get-tuple-element.71.tops, f32[2,1,512]{2,1,0:T(1,128)S(1)} %get-tuple-element.72.totals, f32[2,128,512]{2,1,0:T(8,128)S(1)} %get-tuple-element.73.accs, ...), custom_call_target="tpu_custom_call" | custom-call | flops 8000000000 | bytes 4000000 | tf_op jit(solution)/shard_map/attend_rest/pallas_call | solution.py:413
  88.2 0.9 %all-to-all-done.1.pages = bf16[4,2,2,128,128]{4,3,2,1,0:T(8,128)(2,1)S(1)} async-done(((bf16[4,2,2,128,128]{4,3,2,1,0:T(8,128)(2,1)}), bf16[4,2,2,128,128]{4,3,2,1,0:T(8,128)(2,1)S(1)}, u32[]{:S(2)}, u32[]{:S(2)}) %all-to-all-start.1) | async-done | bytes 524320 | tf_op jit(solution)/shard_map/all_to_all | solution.py:551
  89.1 1.5 %place.1 = (bf16[2,128,128]{2,1,0:T(8,128)(2,1)}, bf16[2,128,128]{2,1,0:T(8,128)(2,1)}) custom-call(s32[128]{0:T(128)S(1)} %route.1.table, bf16[4,2,2,128,128]{4,3,2,1,0:T(8,128)(2,1)S(1)} %all-to-all-done.1.pages), custom_call_target="tpu_custom_call" | custom-call | flops 100000 | bytes 800000 | tf_op jit(solution)/shard_map/place/pallas_call | solution.py:511
  (10 shorter events, 0.3 us)
Async XLA Ops:
  0.6 42.1 %copy-start.4 = (s32[8,64]{1,0:T(8,128)S(1)}, s32[8,64]{1,0:T(8,128)}, u32[]{:S(2)}) copy-start(s32[8,64]{1,0:T(8,128)} %owner_row.1) | copy-start | bytes 6148
  0.6 42.1 %copy-start.5 = (s32[8,64]{1,0:T(8,128)S(1)}, s32[8,64]{1,0:T(8,128)}, u32[]{:S(2)}) copy-start(s32[8,64]{1,0:T(8,128)} %owner_col.1) | copy-start | bytes 6148
  0.7 42.1 %copy-start.6 = (s32[8,64]{1,0:T(8,128)S(1)}, s32[8,64]{1,0:T(8,128)}, u32[]{:S(2)}) copy-start(s32[8,64]{1,0:T(8,128)} %owner_slot.1) | copy-start | bytes 6148
  2.4 13.4 %all-to-all-start = ((bf16[4,2,128,128]{3,2,1,0:T(8,128)(2,1)}), bf16[4,2,128,128]{3,2,1,0:T(8,128)(2,1)S(1)}, u32[]{:S(2)}, u32[]{:S(2)}) async-start(bf16[4,2,128,128]{3,2,1,0:T(8,128)(2,1)} %pack.1), calls=%async_computation | async-start | bytes 524288 | tf_op jit(solution)/shard_map/all_to_all | solution.py:526
  10.2 0.9 copy-start
  11.1 0.8 copy-start.1
  12.0 0.9 %copy-start.2 = (bf16[128,1024]{1,0:T(8,128)(2,1)S(1)}, bf16[128,1024]{1,0:T(8,128)(2,1)}, u32[]{:S(2)}) copy-start(bf16[128,1024]{1,0:T(8,128)(2,1)} %queries.1) | copy-start | bytes 786436
  12.9 0.8 copy-start.3
  15.9 12.0 %collective-permute-start = (bf16[4,2,128,128]{3,2,1,0:T(8,128)(2,1)S(1)}, bf16[4,2,128,128]{3,2,1,0:T(8,128)(2,1)S(1)}, u32[]{:S(2)}, u32[]{:S(2)}) collective-permute-start(bf16[4,2,128,128]{3,2,1,0:T(8,128)(2,1)S(1)} %all-to-all-done.refs_0_), channel_id=1, source_target_pairs={{0,16},{8,24},{16,32},{24,40},{32,48},{40,56},{48,64},{56,72},{64,... | collective-permute-start | bytes 786440 | tf_op jit(solution)/shard_map/ppermute | solution.py:530
  21.0 8.8 %collective-permute-start.4 = (bf16[4,2,128,128]{3,2,1,0:T(8,128)(2,1)S(1)}, bf16[4,2,128,128]{3,2,1,0:T(8,128)(2,1)S(1)}, u32[]{:S(2)}, u32[]{:S(2)}) collective-permute-start(bf16[4,2,128,128]{3,2,1,0:T(8,128)(2,1)S(1)} %all-to-all-done.refs_0_), channel_id=1, source_target_pairs={{0,112},{8,120},{16,0},{24,8},{32,16},{40,24},{48,32},{56,40},{64,... | collective-permute-start | bytes 786440 | tf_op jit(solution)/shard_map/ppermute | solution.py:531
  24.8 0.7 copy-start.7
  27.9 8.3 %collective-permute-start.1 = (bf16[4,2,128,128]{3,2,1,0:T(8,128)(2,1)S(1)}, bf16[4,2,128,128]{3,2,1,0:T(8,128)(2,1)S(1)}, u32[]{:S(2)}, u32[]{:S(2)}) collective-permute-start(bf16[4,2,128,128]{3,2,1,0:T(8,128)(2,1)S(1)} %collective-permute-done.refs_1_), channel_id=1, source_target_pairs={{0,16},{8,24},{16,32},{24,40},{32,48},{40,56},{48,64},{56,72},{64,... | collective-permute-start | bytes 786440 | tf_op jit(solution)/shard_map/ppermute | solution.py:533
  29.8 8.3 %collective-permute-start.5 = (bf16[4,2,128,128]{3,2,1,0:T(8,128)(2,1)S(1)}, bf16[4,2,128,128]{3,2,1,0:T(8,128)(2,1)S(1)}, u32[]{:S(2)}, u32[]{:S(2)}) collective-permute-start(bf16[4,2,128,128]{3,2,1,0:T(8,128)(2,1)S(1)} %collective-permute-done.4.refs_2_), channel_id=1, source_target_pairs={{0,112},{8,120},{16,0},{24,8},{32,16},{40,24},{48,32},{56,40},{64,... | collective-permute-start | bytes 786440 | tf_op jit(solution)/shard_map/ppermute | solution.py:534
  36.2 9.0 %collective-permute-start.2 = (bf16[4,2,128,128]{3,2,1,0:T(8,128)(2,1)S(1)}, bf16[4,2,128,128]{3,2,1,0:T(8,128)(2,1)S(1)}, u32[]{:S(2)}, u32[]{:S(2)}) collective-permute-start(bf16[4,2,128,128]{3,2,1,0:T(8,128)(2,1)S(1)} %collective-permute-done.1.refs_3_), channel_id=1, source_target_pairs={{0,16},{8,24},{16,32},{24,40},{32,48},{40,56},{48,64},{56,72},{64,... | collective-permute-start | bytes 786440 | tf_op jit(solution)/shard_map/ppermute | solution.py:535
  38.1 9.0 %collective-permute-start.6 = (bf16[4,2,128,128]{3,2,1,0:T(8,128)(2,1)S(1)}, bf16[4,2,128,128]{3,2,1,0:T(8,128)(2,1)S(1)}, u32[]{:S(2)}, u32[]{:S(2)}) collective-permute-start(bf16[4,2,128,128]{3,2,1,0:T(8,128)(2,1)S(1)} %collective-permute-done.5.refs_4_), channel_id=1, source_target_pairs={{0,112},{8,120},{16,0},{24,8},{32,16},{40,24},{48,32},{56,40},{64,... | collective-permute-start | bytes 786440 | tf_op jit(solution)/shard_map/ppermute | solution.py:536
  45.2 8.3 %collective-permute-start.3 = (bf16[4,2,128,128]{3,2,1,0:T(8,128)(2,1)S(1)}, bf16[4,2,128,128]{3,2,1,0:T(8,128)(2,1)S(1)}, u32[]{:S(2)}, u32[]{:S(2)}) collective-permute-start(bf16[4,2,128,128]{3,2,1,0:T(8,128)(2,1)S(1)} %collective-permute-done.2.refs_5_), channel_id=1, source_target_pairs={{0,16},{8,24},{16,32},{24,40},{32,48},{40,56},{48,64},{56,72},{64,... | collective-permute-start | bytes 786440 | tf_op jit(solution)/shard_map/ppermute | solution.py:537
  54.5 8.3 %collective-permute-start.7 = (bf16[2,2,128,128]{3,2,1,0:T(8,128)(2,1)S(1)}, bf16[2,2,128,128]{3,2,1,0:T(8,128)(2,1)S(1)}, u32[]{:S(2)}, u32[]{:S(2)}) collective-permute-start(bf16[2,2,128,128]{3,2,1,0:T(8,128)(2,1)S(1)} %get-tuple-element.56), channel_id=1, source_target_pairs={{0,8},{8,0},{16,24},{24,16},{32,40},{40,32},{48,56},{56,48},{64,72... | collective-permute-start | bytes 393224 | tf_op jit(solution)/shard_map/ppermute | solution.py:544
  62.9 9.1 %copy-start.8 = (bf16[2,2,128,128]{3,2,1,0:T(8,128)(2,1)}, bf16[2,2,128,128]{3,2,1,0:T(8,128)(2,1)S(1)}, u32[]{:S(2)}) copy-start(bf16[2,2,128,128]{3,2,1,0:T(8,128)(2,1)S(1)} %add.3.mine) | copy-start | bytes 393220
  62.9 11.0 %collective-permute-start.8 = (bf16[2,128,128]{2,1,0:T(8,128)(2,1)S(1)}, bf16[2,128,128]{2,1,0:T(8,128)(2,1)S(1)}, u32[]{:S(2)}, u32[]{:S(2)}) collective-permute-start(bf16[2,128,128]{2,1,0:T(8,128)(2,1)S(1)} %slice_bitcast_fusion), channel_id=1, source_target_pairs={{0,388},{1,389},{2,390},{3,391},{4,384},{5,385},{6,386},{7,387},{8... | collective-permute-start | bytes 196616 | tf_op jit(solution)/shard_map/ppermute | solution.py:545
  72.0 8.4 %collective-permute-start.9 = (bf16[32,2,128,128]{3,2,1,0:T(8,128)(2,1)S(1)}, bf16[32,2,128,128]{3,2,1,0:T(8,128)(2,1)}, u32[]{:S(2)}, u32[]{:S(2)}) collective-permute-start(bf16[32,2,128,128]{3,2,1,0:T(8,128)(2,1)S(1)} %constant_dynamic-update-slice_fusion.own), channel_id=1, source_target_pairs={{0,8},{8,0},{16,24},{24,16},{32,40},{40,32},{48,56},{56,48},{64,72... | collective-permute-start | bytes 6291464 | tf_op jit(solution)/shard_map/ppermute | solution.py:549
  73.9 0.6 copy-start.9
  76.3 12.8 %all-to-all-start.1 = ((bf16[4,2,2,128,128]{4,3,2,1,0:T(8,128)(2,1)}), bf16[4,2,2,128,128]{4,3,2,1,0:T(8,128)(2,1)S(1)}, u32[]{:S(2)}, u32[]{:S(2)}) async-start(bf16[4,2,2,128,128]{4,3,2,1,0:T(8,128)(2,1)} %spread.1), calls=%async_computation.1 | async-start | bytes 1048576 | tf_op jit(solution)/shard_map/all_to_all | solution.py:551

commit v6 on v5

--- a/solution.py
+++ b/solution.py
@@ -150,7 +150,6 @@
         ),
         in_specs=[SMEM, VMEM, VMEM, VMEM],
         out_specs=(VMEM, SMEM),
-        compiler_params=pltpu.CompilerParams(vmem_limit_bytes=BIG_GRANT),
         cost_estimate=pl.CostEstimate(flops=2_000_000, bytes_accessed=600_000, transcendentals=0),
         name="turn",
     )(positions, queries, jnp.asarray(RUN_TABLE), jnp.asarray(STEP_TABLE))
@@ -166,7 +165,7 @@
     return jnp.clip(counts[lax.shift_right_logical(run, 1)] - (run & 1) * HALF, 0, HALF)
 
 
-def lists_kernel(runs, counts, table):
+def lists_kernel(runs, counts, owner_row, owner_col, owner_slot, table, routes):
     me, _, y_me, core = coordinates()
     my_run = runs[me]
 
@@ -194,18 +193,7 @@
         table[MISC, AT_COUNT + low] = n_low
         table[MISC, AT_COUNT + high] = n_high
     table[MISC, AT_RUN] = my_run
-
-
-def lists(runs, counts):
-    return pl.pallas_call(
-        lists_kernel,
-        out_shape=jax.ShapeDtypeStruct((8, LANES), jnp.int32),
-        in_specs=[SMEM, SMEM],
-        out_specs=SMEM,
-        compiler_params=pltpu.CompilerParams(vmem_limit_bytes=BIG_GRANT),
-        cost_estimate=pl.CostEstimate(flops=2_000_000, bytes_accessed=300_000, transcendentals=0),
-        name="lists",
-    )(runs, counts)
+    route_entries(table, counts, owner_row, owner_col, owner_slot, routes)
 
 
 AT_PLACE, AT_PICK = 0, 8
@@ -218,7 +206,7 @@
     return page
 
 
-def route_kernel(lists, counts, owner_row, owner_col, owner_slot, table):
+def route_entries(lists, counts, owner_row, owner_col, owner_slot, table):
     me, z_me, _, _ = coordinates()
     tp = lax.axis_index("tp")
     for i in range(N_X):
@@ -243,16 +231,18 @@
         table[at + 2] = jnp.where(block < SRC, clip_valid(counts, run), 0)
 
 
-def route(lists, counts, owner_row, owner_col, owner_slot):
-    return pl.pallas_call(
-        route_kernel,
-        out_shape=jax.ShapeDtypeStruct((LANES,), jnp.int32),
+def lists(runs, counts, owner_row, owner_col, owner_slot):
+    return pl.pallas_call(
+        lists_kernel,
+        out_shape=(
+            jax.ShapeDtypeStruct((8, LANES), jnp.int32),
+            jax.ShapeDtypeStruct((LANES,), jnp.int32),
+        ),
         in_specs=[SMEM] * 5,
-        out_specs=SMEM,
-        compiler_params=pltpu.CompilerParams(vmem_limit_bytes=BIG_GRANT),
+        out_specs=(SMEM, SMEM),
         cost_estimate=pl.CostEstimate(flops=2_000_000, bytes_accessed=300_000, transcendentals=0),
-        name="route",
-    )(lists, counts, owner_row, owner_col, owner_slot)
+        name="lists",
+    )(runs, counts, owner_row, owner_col, owner_slot)
 
 
 COLS = KVH * HALF
@@ -472,9 +462,14 @@
 def spread(mine, across):
     return pl.pallas_call(
         spread_kernel,
+        grid=(1,),
         out_shape=jax.ShapeDtypeStruct((N_X, 2, 2, PAGE, HD), jnp.bfloat16),
-        in_specs=[VMEM, VMEM],
-        out_specs=VMEM,
+        in_specs=[
+            pl.BlockSpec((1, 2, PAGE, HD), lambda i: (0, 0, 0, 0)),
+            pl.BlockSpec((2, PAGE, HD), lambda i: (0, 0, 0)),
+        ],
+        out_specs=pl.BlockSpec((N_X, 2, 2, PAGE, HD), lambda i: (0, 0, 0, 0, 0)),
+        compiler_params=pltpu.CompilerParams(vmem_limit_bytes=BIG_GRANT),
         cost_estimate=pl.CostEstimate(
             flops=100_000_000_000, bytes_accessed=700_000, transcendentals=0
         ),
@@ -524,20 +519,20 @@
     tie = lax.optimization_barrier
     packed, later_positions = tie((pack(positions, keys, values), positions))
     unit = lax.all_to_all(packed, "cp", 0, 0, axis_index_groups=Z_GROUPS)
-    unit, q_rot, runs = tie((unit, *turn(later_positions, queries)))
+    q_rot, runs = turn(later_positions, queries)
+    table, routes = lists(runs, counts, owner_row, owner_col, owner_slot)
+    unit, q_rot, table, routes = tie((unit, q_rot, table, routes))
 
     ahead, back = y_pairs(1), y_pairs(-1)
     f1 = lax.ppermute(unit, "cp", ahead)
     b1 = lax.ppermute(unit, "cp", back)
-    f1, table = tie((f1, lists(runs, counts)))
     f2 = lax.ppermute(f1, "cp", ahead)
     b2 = lax.ppermute(b1, "cp", back)
     f3 = lax.ppermute(f2, "cp", ahead)
     b3 = lax.ppermute(b2, "cp", back)
     f4 = lax.ppermute(f3, "cp", ahead)
     state = attend_first(table, counts, q_rot, unit, f1, b1, f2, b2, f3, b3)
-    routes = route(table, counts, owner_row, owner_col, owner_slot)
-    f4, state, routes = tie((f4, state, routes))
+    f4, state = tie((f4, state))
     own = jnp.concatenate([unit, f1, b1, f2, b2, f3, b3, f4], axis=0)
 
     mine, theirs = pick(routes, own)

time: 92.3 us -> 90.4 us (0.979)
  local copies, waits for them, and re-layouts: 5.02 us -> 0.3 us
  waiting for transfers between devices: 4.23 us -> 8.09 us
  Pallas kernels: 28.6 us -> 26.7 us
  starting transfers between devices: 51.8 us -> 52.8 us
    unnamed x27 -> x15, local copies, waits for them, and re-layouts: 4.98 us -> 0.26 us
    ppermute x1, waiting for transfers between devices: 0.01 us -> 2.37 us  [shards(): f1 = lax.ppermute(unit, 'cp', ahead)]
    pallas_call x3 -> x2, Pallas kernels: 6.48 us -> 4.48 us  [the longest x1 3.63 us: lists(): pl.pallas_call(lists_kernel, out_shape=(jax.ShapeDtypeStruct((8, LANES),...]
    ppermute x1, waiting for transfers between devices: 0.01 us -> 1.66 us  [shards(): f3 = lax.ppermute(f2, 'cp', ahead)]
    ppermute x1, starting transfers between devices: 7.35 us -> 8.3 us  [shards(): pages = mine + lax.ppermute(theirs, 'cp', CORE_PAIRS)]
  transfers between devices with their start and end apart: 12 -> 12, of which waited for: 5 -> 6; matrix products, arithmetic and copies ran while one was open for 0% -> 0% of each run, Pallas kernels for 27% -> 25%
where the time goes in v6:
time: 90.4 us; the launch traced here: 88.8 us
  starting transfers between devices  52.8 us (58%)
  Pallas kernels  26.7 us (30%)
  waiting for transfers between devices  8.09 us (9%)
  between operations  0.94 us (1%)
    ppermute x1, starting transfers between devices, shards(): pages = mine + lax.ppermute(theirs, 'cp', CORE_PAIRS)  8.3 us
    pallas_call x1, Pallas kernels, attend_rest(): pl.pallas_call(rest_kernel, out_shape=jax.ShapeDtypeStruct((ROWS, KVH * H...  7.86 us
    all_to_all x1, starting transfers between devices, shards(): unit = lax.all_to_all(packed, 'cp', 0, 0, axis_index_groups=Z_GROUPS)  7.81 us
    ppermute x1, starting transfers between devices, shards(): across = lax.ppermute(pages[1], ('cp', 'tp'), MIRROR_PAIRS)  7.23 us
    pallas_call x1, Pallas kernels, attend_first(): pl.pallas_call(first_kernel, out_shape=STATE, in_specs=[SMEM, SMEM, VMEM]...  5.81 us
    ppermute x1, starting transfers between devices, shards(): f1 = lax.ppermute(unit, 'cp', ahead)  4.86 us
    ppermute x1, starting transfers between devices, shards(): b2 = lax.ppermute(b1, 'cp', back)  4.57 us
    ppermute x1, starting transfers between devices, shards(): b3 = lax.ppermute(b2, 'cp', back)  4.57 us
  transfers between devices with their start and end apart: 12, of which 6 were waited for; matrix products, arithmetic and copies ran while one was open for 0% of the time, Pallas kernels for 25%

profile of v6, /device:TPU:1, one launch (start us, length us, event | category | flops | bytes accessed | tf_op | source)
XLA Modules:
  0.0 88.8 jit_solution(12895709621735412592)
XLA Ops:
  0.6 0.0 copy-start.1
  0.6 1.7 %pack.1 = bf16[4,2,128,128]{3,2,1,0:T(8,128)(2,1)} custom-call(s32[64,128]{1,0:T(8,128)} %bitcast.3, bf16[128,128]{1,0:T(8,128)(2,1)} %keys.1, bf16[128,128]{1,0:T(8,128)(2,1)} %values.1, f32[2,128,128]{2,1,0:T(8,128)} %constant.4.clone.run_table, f32[2,64,128]{2,1,0:T(8,128)} %constant.5.clone.step_table), custom_call_target="tpu_custom_call" | custom-call | flops 1000000 | bytes 400000 | tf_op jit(solution)/shard_map/pack/pallas_call | solution.py:111
  2.4 7.8 %all-to-all-start = ((bf16[4,2,128,128]{3,2,1,0:T(8,128)(2,1)}), bf16[4,2,128,128]{3,2,1,0:T(8,128)(2,1)S(1)}, u32[]{:S(2)}, u32[]{:S(2)}) async-start(bf16[4,2,128,128]{3,2,1,0:T(8,128)(2,1)} %pack.1), calls=%async_computation | async-start | bytes 524288 | tf_op jit(solution)/shard_map/all_to_all | solution.py:521
  10.2 2.2 %turn.1 = (bf16[2,512,128]{2,1,0:T(8,128)(2,1)}, s32[64]{0:T(128)}) custom-call(s32[8192]{0:T(1024)} %positions, bf16[128,1024]{1,0:T(8,128)(2,1)} %queries.1, f32[2,128,128]{2,1,0:T(8,128)} %constant.4.clone.run_table, f32[2,64,128]{2,1,0:T(8,128)} %constant.5.clone.step_table), custom_call_target="tpu_custom_call" | custom-call | flops 2000000 | bytes 600000 | tf_op jit(solution)/shard_map/turn/pallas_call | solution.py:145
  12.4 0.0 copy-start.2
  12.4 3.6 %lists.1 = (s32[8,128]{1,0:T(8,128)}, s32[128]{0:T(128)}) custom-call(s32[64]{0:T(128)} %get-tuple-element.44.runs, s32[64]{0:T(128)} %counts.3, s32[8,64]{1,0:T(8,128)} %owner_row.1, s32[8,64]{1,0:T(8,128)} %owner_col.1, s32[8,64]{1,0:T(8,128)} %owner_slot.1), custom_call_target="tpu_custom_call" | custom-call | flops 2000000 | bytes 300000 | tf_op jit(solution)/shard_map/lists/pallas_call | solution.py:235
  16.1 0.0 copy-start.3
  16.1 0.0 all-to-all-done.refs_0_
  16.1 4.9 %collective-permute-start = (bf16[4,2,128,128]{3,2,1,0:T(8,128)(2,1)S(1)}, bf16[4,2,128,128]{3,2,1,0:T(8,128)(2,1)S(1)}, u32[]{:S(2)}, u32[]{:S(2)}) collective-permute-start(bf16[4,2,128,128]{3,2,1,0:T(8,128)(2,1)S(1)} %all-to-all-done.refs_0_), channel_id=1, source_target_pairs={{0,16},{8,24},{16,32},{24,40},{32,48},{40,56},{48,64},{56,72},{64,... | collective-permute-start | bytes 786440 | tf_op jit(solution)/shard_map/ppermute | solution.py:527
  21.0 3.8 %collective-permute-start.1 = (bf16[4,2,128,128]{3,2,1,0:T(8,128)(2,1)S(1)}, bf16[4,2,128,128]{3,2,1,0:T(8,128)(2,1)S(1)}, u32[]{:S(2)}, u32[]{:S(2)}) collective-permute-start(bf16[4,2,128,128]{3,2,1,0:T(8,128)(2,1)S(1)} %all-to-all-done.refs_0_), channel_id=1, source_target_pairs={{0,112},{8,120},{16,0},{24,8},{32,16},{40,24},{48,32},{56,40},{64,... | collective-permute-start | bytes 786440 | tf_op jit(solution)/shard_map/ppermute | solution.py:528
  24.8 2.4 %collective-permute-done.refs_1_ = bf16[4,2,128,128]{3,2,1,0:T(8,128)(2,1)S(1)} collective-permute-done((bf16[4,2,128,128]{3,2,1,0:T(8,128)(2,1)S(1)}, bf16[4,2,128,128]{3,2,1,0:T(8,128)(2,1)S(1)}, u32[]{:S(2)}, u32[]{:S(2)}) %collective-permute-start) | collective-permute-done | bytes 262176 | tf_op jit(solution)/shard_map/ppermute | solution.py:527
  27.1 1.9 %collective-permute-start.2 = (bf16[4,2,128,128]{3,2,1,0:T(8,128)(2,1)S(1)}, bf16[4,2,128,128]{3,2,1,0:T(8,128)(2,1)S(1)}, u32[]{:S(2)}, u32[]{:S(2)}) collective-permute-start(bf16[4,2,128,128]{3,2,1,0:T(8,128)(2,1)S(1)} %collective-permute-done.refs_1_), channel_id=1, source_target_pairs={{0,16},{8,24},{16,32},{24,40},{32,48},{40,56},{48,64},{56,72},{64,... | collective-permute-start | bytes 786440 | tf_op jit(solution)/shard_map/ppermute | solution.py:529
  29.1 0.0 collective-permute-done.1.refs_2_
  29.1 4.6 %collective-permute-start.3 = (bf16[4,2,128,128]{3,2,1,0:T(8,128)(2,1)S(1)}, bf16[4,2,128,128]{3,2,1,0:T(8,128)(2,1)S(1)}, u32[]{:S(2)}, u32[]{:S(2)}) collective-permute-start(bf16[4,2,128,128]{3,2,1,0:T(8,128)(2,1)S(1)} %collective-permute-done.1.refs_2_), channel_id=1, source_target_pairs={{0,112},{8,120},{16,0},{24,8},{32,16},{40,24},{48,32},{56,40},{64,... | collective-permute-start | bytes 786440 | tf_op jit(solution)/shard_map/ppermute | solution.py:530
  33.7 1.7 %collective-permute-done.2.refs_3_ = bf16[4,2,128,128]{3,2,1,0:T(8,128)(2,1)S(1)} collective-permute-done((bf16[4,2,128,128]{3,2,1,0:T(8,128)(2,1)S(1)}, bf16[4,2,128,128]{3,2,1,0:T(8,128)(2,1)S(1)}, u32[]{:S(2)}, u32[]{:S(2)}) %collective-permute-start.2) | collective-permute-done | bytes 262176 | tf_op jit(solution)/shard_map/ppermute | solution.py:529
  35.5 1.9 %collective-permute-start.4 = (bf16[4,2,128,128]{3,2,1,0:T(8,128)(2,1)S(1)}, bf16[4,2,128,128]{3,2,1,0:T(8,128)(2,1)S(1)}, u32[]{:S(2)}, u32[]{:S(2)}) collective-permute-start(bf16[4,2,128,128]{3,2,1,0:T(8,128)(2,1)S(1)} %collective-permute-done.2.refs_3_), channel_id=1, source_target_pairs={{0,16},{8,24},{16,32},{24,40},{32,48},{40,56},{48,64},{56,72},{64,... | collective-permute-start | bytes 786440 | tf_op jit(solution)/shard_map/ppermute | solution.py:531
  37.4 0.0 collective-permute-done.3.refs_4_
  37.4 4.6 %collective-permute-start.5 = (bf16[4,2,128,128]{3,2,1,0:T(8,128)(2,1)S(1)}, bf16[4,2,128,128]{3,2,1,0:T(8,128)(2,1)S(1)}, u32[]{:S(2)}, u32[]{:S(2)}) collective-permute-start(bf16[4,2,128,128]{3,2,1,0:T(8,128)(2,1)S(1)} %collective-permute-done.3.refs_4_), channel_id=1, source_target_pairs={{0,112},{8,120},{16,0},{24,8},{32,16},{40,24},{48,32},{56,40},{64,... | collective-permute-start | bytes 786440 | tf_op jit(solution)/shard_map/ppermute | solution.py:532
  42.1 0.0 copy-start
  42.1 1.7 %collective-permute-done.4.refs_5_ = bf16[4,2,128,128]{3,2,1,0:T(8,128)(2,1)S(1)} collective-permute-done((bf16[4,2,128,128]{3,2,1,0:T(8,128)(2,1)S(1)}, bf16[4,2,128,128]{3,2,1,0:T(8,128)(2,1)S(1)}, u32[]{:S(2)}, u32[]{:S(2)}) %collective-permute-start.4) | collective-permute-done | bytes 262176 | tf_op jit(solution)/shard_map/ppermute | solution.py:531
  43.8 1.9 %collective-permute-start.6 = (bf16[4,2,128,128]{3,2,1,0:T(8,128)(2,1)S(1)}, bf16[4,2,128,128]{3,2,1,0:T(8,128)(2,1)S(1)}, u32[]{:S(2)}, u32[]{:S(2)}) collective-permute-start(bf16[4,2,128,128]{3,2,1,0:T(8,128)(2,1)S(1)} %collective-permute-done.4.refs_5_), channel_id=1, source_target_pairs={{0,16},{8,24},{16,32},{24,40},{32,48},{40,56},{48,64},{56,72},{64,... | collective-permute-start | bytes 786440 | tf_op jit(solution)/shard_map/ppermute | solution.py:533
  45.7 0.0 collective-permute-done.5.refs_6_
  45.7 0.0 copy-done.1
  45.7 0.0 copy-done.2
  45.7 0.0 copy-done.3
  45.7 5.8 %attend_first.1 = (f32[2,1,512]{2,1,0:T(1,128)S(1)}, f32[2,1,512]{2,1,0:T(1,128)S(1)}, f32[2,128,512]{2,1,0:T(8,128)S(1)}) custom-call(s32[8,128]{1,0:T(8,128)S(1)} %copy-done.3, s32[64]{0:T(128)S(1)} %copy-done.1, bf16[2,512,128]{2,1,0:T(8,128)(2,1)S(1)} %copy-done.2, bf16[4,2,128,128]{3,2,1,0:T(8,128)(2,1)S(1)} %all-to-all-done.refs_0_, ...), custom_call_target="tpu_custom_call" | custom-call | flops 6000000000 | bytes 3000000 | tf_op jit(solution)/shard_map/attend_first/pallas_call | solution.py:343
  51.6 0.4 collective-permute-done.6.other
  52.1 0.0 copy-done
  52.1 0.9 %pick.1 = (bf16[2,2,128,128]{3,2,1,0:T(8,128)(2,1)S(1)}, bf16[2,2,128,128]{3,2,1,0:T(8,128)(2,1)S(1)}) custom-call(s32[128]{0:T(128)S(1)} %copy-done, bf16[32,2,128,128]{3,2,1,0:T(8,128)(2,1)S(1)} %constant_dynamic-update-slice_fusion.own), custom_call_target="tpu_custom_call" | custom-call | flops 100000 | bytes 300000 | tf_op jit(solution)/shard_map/pick/pallas_call | solution.py:441
  53.1 8.3 %collective-permute-start.7 = (bf16[2,2,128,128]{3,2,1,0:T(8,128)(2,1)S(1)}, bf16[2,2,128,128]{3,2,1,0:T(8,128)(2,1)S(1)}, u32[]{:S(2)}, u32[]{:S(2)}) collective-permute-start(bf16[2,2,128,128]{3,2,1,0:T(8,128)(2,1)S(1)} %get-tuple-element.56), channel_id=1, source_target_pairs={{0,8},{8,0},{16,24},{24,16},{32,40},{40,32},{48,56},{56,48},{64,72... | collective-permute-start | bytes 393224 | tf_op jit(solution)/shard_map/ppermute | solution.py:539
  61.4 1.0 %collective-permute-done.7 = bf16[2,2,128,128]{3,2,1,0:T(8,128)(2,1)S(1)} collective-permute-done((bf16[2,2,128,128]{3,2,1,0:T(8,128)(2,1)S(1)}, bf16[2,2,128,128]{3,2,1,0:T(8,128)(2,1)S(1)}, u32[]{:S(2)}, u32[]{:S(2)}) %collective-permute-start.7) | collective-permute-done | bytes 131104 | tf_op jit(solution)/shard_map/ppermute | solution.py:539
  62.4 7.2 %collective-permute-start.8 = (bf16[2,128,128]{2,1,0:T(8,128)(2,1)S(1)}, bf16[2,128,128]{2,1,0:T(8,128)(2,1)S(1)}, u32[]{:S(2)}, u32[]{:S(2)}) collective-permute-start(bf16[2,128,128]{2,1,0:T(8,128)(2,1)S(1)} %slice_bitcast_fusion), channel_id=1, source_target_pairs={{0,388},{1,389},{2,390},{3,391},{4,384},{5,385},{6,386},{7,387},{8... | collective-permute-start | bytes 196616 | tf_op jit(solution)/shard_map/ppermute | solution.py:540
  69.6 2.2 %attend_middle.1 = (f32[2,1,512]{2,1,0:T(1,128)S(1)}, f32[2,1,512]{2,1,0:T(1,128)S(1)}, f32[2,128,512]{2,1,0:T(8,128)S(1)}) custom-call(s32[8,128]{1,0:T(8,128)S(1)} %copy-done.3, bf16[2,512,128]{2,1,0:T(8,128)(2,1)S(1)} %copy-done.2, f32[2,1,512]{2,1,0:T(1,128)S(1)} %get-tuple-element.61.tops, f32[2,1,512]{2,1,0:T(1,128)S(1)} %get-tuple-element.62.totals, ...), custom_call_target="tpu_custom_call" | custom-call | flops 2000000000 | bytes 2000000 | tf_op jit(solution)/shard_map/attend_middle/pallas_call | solution.py:371
  71.8 1.9 %collective-permute-start.9 = (bf16[32,2,128,128]{3,2,1,0:T(8,128)(2,1)S(1)}, bf16[32,2,128,128]{3,2,1,0:T(8,128)(2,1)}, u32[]{:S(2)}, u32[]{:S(2)}) collective-permute-start(bf16[32,2,128,128]{3,2,1,0:T(8,128)(2,1)S(1)} %constant_dynamic-update-slice_fusion.own), channel_id=1, source_target_pairs={{0,8},{8,0},{16,24},{24,16},{32,40},{40,32},{48,56},{56,48},{64,72... | collective-permute-start | bytes 6291464 | tf_op jit(solution)/shard_map/ppermute | solution.py:544
  73.7 0.0 collective-permute-done.8.across
  73.8 0.9 spread.1
  74.6 4.0 %all-to-all-start.1 = ((bf16[4,2,2,128,128]{4,3,2,1,0:T(8,128)(2,1)}), bf16[4,2,2,128,128]{4,3,2,1,0:T(8,128)(2,1)S(1)}, u32[]{:S(2)}, u32[]{:S(2)}) async-start(bf16[4,2,2,128,128]{4,3,2,1,0:T(8,128)(2,1)} %spread.1), calls=%async_computation.1 | async-start | bytes 1048576 | tf_op jit(solution)/shard_map/all_to_all | solution.py:546
  78.6 0.0 collective-permute-done.9.other
  78.6 7.9 %attend_rest.1 = bf16[128,1024]{1,0:T(8,128)(2,1)} custom-call(s32[8,128]{1,0:T(8,128)S(1)} %copy-done.3, bf16[2,512,128]{2,1,0:T(8,128)(2,1)S(1)} %copy-done.2, f32[2,1,512]{2,1,0:T(1,128)S(1)} %get-tuple-element.71.tops, f32[2,1,512]{2,1,0:T(1,128)S(1)} %get-tuple-element.72.totals, f32[2,128,512]{2,1,0:T(8,128)S(1)} %get-tuple-element.73.accs, ...), custom_call_target="tpu_custom_call" | custom-call | flops 8000000000 | bytes 4000000 | tf_op jit(solution)/shard_map/attend_rest/pallas_call | solution.py:403
  86.5 0.9 %all-to-all-done.1.pages = bf16[4,2,2,128,128]{4,3,2,1,0:T(8,128)(2,1)S(1)} async-done(((bf16[4,2,2,128,128]{4,3,2,1,0:T(8,128)(2,1)}), bf16[4,2,2,128,128]{4,3,2,1,0:T(8,128)(2,1)S(1)}, u32[]{:S(2)}, u32[]{:S(2)}) %all-to-all-start.1) | async-done | bytes 524320 | tf_op jit(solution)/shard_map/all_to_all | solution.py:546
  87.4 1.5 %place.1 = (bf16[2,128,128]{2,1,0:T(8,128)(2,1)}, bf16[2,128,128]{2,1,0:T(8,128)(2,1)}) custom-call(s32[128]{0:T(128)S(1)} %copy-done, bf16[4,2,2,128,128]{4,3,2,1,0:T(8,128)(2,1)S(1)} %all-to-all-done.1.pages), custom_call_target="tpu_custom_call" | custom-call | flops 100000 | bytes 800000 | tf_op jit(solution)/shard_map/place/pallas_call | solution.py:506
  (10 shorter events, 0.3 us)
Async XLA Ops:
  0.6 45.1 %copy-start.1 = (s32[64]{0:T(128)S(1)}, s32[64]{0:T(128)}, u32[]{:S(2)}) copy-start(s32[64]{0:T(128)} %counts.3) | copy-start | bytes 772
  2.4 13.7 %all-to-all-start = ((bf16[4,2,128,128]{3,2,1,0:T(8,128)(2,1)}), bf16[4,2,128,128]{3,2,1,0:T(8,128)(2,1)S(1)}, u32[]{:S(2)}, u32[]{:S(2)}) async-start(bf16[4,2,128,128]{3,2,1,0:T(8,128)(2,1)} %pack.1), calls=%async_computation | async-start | bytes 524288 | tf_op jit(solution)/shard_map/all_to_all | solution.py:521
  12.4 33.3 %copy-start.2 = (bf16[2,512,128]{2,1,0:T(8,128)(2,1)S(1)}, bf16[2,512,128]{2,1,0:T(8,128)(2,1)}, u32[]{:S(2)}) copy-start(bf16[2,512,128]{2,1,0:T(8,128)(2,1)} %get-tuple-element.50.q_rot) | copy-start | bytes 786436
  16.1 29.7 %copy-start.3 = (s32[8,128]{1,0:T(8,128)S(1)}, s32[8,128]{1,0:T(8,128)}, u32[]{:S(2)}) copy-start(s32[8,128]{1,0:T(8,128)} %get-tuple-element.49.table) | copy-start | bytes 12292
  16.1 11.1 %collective-permute-start = (bf16[4,2,128,128]{3,2,1,0:T(8,128)(2,1)S(1)}, bf16[4,2,128,128]{3,2,1,0:T(8,128)(2,1)S(1)}, u32[]{:S(2)}, u32[]{:S(2)}) collective-permute-start(bf16[4,2,128,128]{3,2,1,0:T(8,128)(2,1)S(1)} %all-to-all-done.refs_0_), channel_id=1, source_target_pairs={{0,16},{8,24},{16,32},{24,40},{32,48},{40,56},{48,64},{56,72},{64,... | collective-permute-start | bytes 786440 | tf_op jit(solution)/shard_map/ppermute | solution.py:527
  21.0 8.1 %collective-permute-start.1 = (bf16[4,2,128,128]{3,2,1,0:T(8,128)(2,1)S(1)}, bf16[4,2,128,128]{3,2,1,0:T(8,128)(2,1)S(1)}, u32[]{:S(2)}, u32[]{:S(2)}) collective-permute-start(bf16[4,2,128,128]{3,2,1,0:T(8,128)(2,1)S(1)} %all-to-all-done.refs_0_), channel_id=1, source_target_pairs={{0,112},{8,120},{16,0},{24,8},{32,16},{40,24},{48,32},{56,40},{64,... | collective-permute-start | bytes 786440 | tf_op jit(solution)/shard_map/ppermute | solution.py:528
  27.1 8.3 %collective-permute-start.2 = (bf16[4,2,128,128]{3,2,1,0:T(8,128)(2,1)S(1)}, bf16[4,2,128,128]{3,2,1,0:T(8,128)(2,1)S(1)}, u32[]{:S(2)}, u32[]{:S(2)}) collective-permute-start(bf16[4,2,128,128]{3,2,1,0:T(8,128)(2,1)S(1)} %collective-permute-done.refs_1_), channel_id=1, source_target_pairs={{0,16},{8,24},{16,32},{24,40},{32,48},{40,56},{48,64},{56,72},{64,... | collective-permute-start | bytes 786440 | tf_op jit(solution)/shard_map/ppermute | solution.py:529
  29.1 8.3 %collective-permute-start.3 = (bf16[4,2,128,128]{3,2,1,0:T(8,128)(2,1)S(1)}, bf16[4,2,128,128]{3,2,1,0:T(8,128)(2,1)S(1)}, u32[]{:S(2)}, u32[]{:S(2)}) collective-permute-start(bf16[4,2,128,128]{3,2,1,0:T(8,128)(2,1)S(1)} %collective-permute-done.1.refs_2_), channel_id=1, source_target_pairs={{0,112},{8,120},{16,0},{24,8},{32,16},{40,24},{48,32},{56,40},{64,... | collective-permute-start | bytes 786440 | tf_op jit(solution)/shard_map/ppermute | solution.py:530
  35.5 8.3 %collective-permute-start.4 = (bf16[4,2,128,128]{3,2,1,0:T(8,128)(2,1)S(1)}, bf16[4,2,128,128]{3,2,1,0:T(8,128)(2,1)S(1)}, u32[]{:S(2)}, u32[]{:S(2)}) collective-permute-start(bf16[4,2,128,128]{3,2,1,0:T(8,128)(2,1)S(1)} %collective-permute-done.2.refs_3_), channel_id=1, source_target_pairs={{0,16},{8,24},{16,32},{24,40},{32,48},{40,56},{48,64},{56,72},{64,... | collective-permute-start | bytes 786440 | tf_op jit(solution)/shard_map/ppermute | solution.py:531
  37.4 8.3 %collective-permute-start.5 = (bf16[4,2,128,128]{3,2,1,0:T(8,128)(2,1)S(1)}, bf16[4,2,128,128]{3,2,1,0:T(8,128)(2,1)S(1)}, u32[]{:S(2)}, u32[]{:S(2)}) collective-permute-start(bf16[4,2,128,128]{3,2,1,0:T(8,128)(2,1)S(1)} %collective-permute-done.3.refs_4_), channel_id=1, source_target_pairs={{0,112},{8,120},{16,0},{24,8},{32,16},{40,24},{48,32},{56,40},{64,... | collective-permute-start | bytes 786440 | tf_op jit(solution)/shard_map/ppermute | solution.py:532
  42.1 10.0 %copy-start = (s32[128]{0:T(128)S(1)}, s32[128]{0:T(128)}, u32[]{:S(2)}) copy-start(s32[128]{0:T(128)} %get-tuple-element.47.table) | copy-start | bytes 1540
  43.8 8.3 %collective-permute-start.6 = (bf16[4,2,128,128]{3,2,1,0:T(8,128)(2,1)S(1)}, bf16[4,2,128,128]{3,2,1,0:T(8,128)(2,1)S(1)}, u32[]{:S(2)}, u32[]{:S(2)}) collective-permute-start(bf16[4,2,128,128]{3,2,1,0:T(8,128)(2,1)S(1)} %collective-permute-done.4.refs_5_), channel_id=1, source_target_pairs={{0,16},{8,24},{16,32},{24,40},{32,48},{40,56},{48,64},{56,72},{64,... | collective-permute-start | bytes 786440 | tf_op jit(solution)/shard_map/ppermute | solution.py:533
  53.1 9.3 %collective-permute-start.7 = (bf16[2,2,128,128]{3,2,1,0:T(8,128)(2,1)S(1)}, bf16[2,2,128,128]{3,2,1,0:T(8,128)(2,1)S(1)}, u32[]{:S(2)}, u32[]{:S(2)}) collective-permute-start(bf16[2,2,128,128]{3,2,1,0:T(8,128)(2,1)S(1)} %get-tuple-element.56), channel_id=1, source_target_pairs={{0,8},{8,0},{16,24},{24,16},{32,40},{40,32},{48,56},{56,48},{64,72... | collective-permute-start | bytes 393224 | tf_op jit(solution)/shard_map/ppermute | solution.py:539
  62.4 11.4 %collective-permute-start.8 = (bf16[2,128,128]{2,1,0:T(8,128)(2,1)S(1)}, bf16[2,128,128]{2,1,0:T(8,128)(2,1)S(1)}, u32[]{:S(2)}, u32[]{:S(2)}) collective-permute-start(bf16[2,128,128]{2,1,0:T(8,128)(2,1)S(1)} %slice_bitcast_fusion), channel_id=1, source_target_pairs={{0,388},{1,389},{2,390},{3,391},{4,384},{5,385},{6,386},{7,387},{8... | collective-permute-start | bytes 196616 | tf_op jit(solution)/shard_map/ppermute | solution.py:540
  71.8 6.8 %collective-permute-start.9 = (bf16[32,2,128,128]{3,2,1,0:T(8,128)(2,1)S(1)}, bf16[32,2,128,128]{3,2,1,0:T(8,128)(2,1)}, u32[]{:S(2)}, u32[]{:S(2)}) collective-permute-start(bf16[32,2,128,128]{3,2,1,0:T(8,128)(2,1)S(1)} %constant_dynamic-update-slice_fusion.own), channel_id=1, source_target_pairs={{0,8},{8,0},{16,24},{24,16},{32,40},{40,32},{48,56},{56,48},{64,72... | collective-permute-start | bytes 6291464 | tf_op jit(solution)/shard_map/ppermute | solution.py:544
  74.6 12.8 %all-to-all-start.1 = ((bf16[4,2,2,128,128]{4,3,2,1,0:T(8,128)(2,1)}), bf16[4,2,2,128,128]{4,3,2,1,0:T(8,128)(2,1)S(1)}, u32[]{:S(2)}, u32[]{:S(2)}) async-start(bf16[4,2,2,128,128]{4,3,2,1,0:T(8,128)(2,1)} %spread.1), calls=%async_computation.1 | async-start | bytes 1048576 | tf_op jit(solution)/shard_map/all_to_all | solution.py:546

commit v7 on v6

--- a/solution.py
+++ b/solution.py
@@ -38,7 +38,7 @@
 
 
 OFFSETS = (0, -1, 1, -2, 2, -3, 3, 4)
-FIRST = 28
+FIRST = 24
 MIDDLE = SRC - FIRST
 REST = SRC
 BIG_GRANT = 24 * 2**20
@@ -357,32 +357,30 @@
     )(table, counts, q_rot, *pieces)
 
 
-def middle_kernel(table, q_rot, tops, totals, accs, other, new_tops, new_totals, new_accs, kv, sem):
-    copy = pltpu.make_async_copy(other, kv, sem)
-    copy.start()
-    copy.wait()
+def middle_kernel(table, q_rot, tops, totals, accs, b3, f4, new_tops, new_totals, new_accs, kv, sems):
+    copy_blocks(((b3, 0, N_Z), (f4, 0, N_Z)), kv, sems)
     for part in range(2):
         state = tops[part], totals[part], accs[part]
         state = fold_list(table, LIST_ROWS[1][part], q_rot[part], kv, state)
         new_tops[part], new_totals[part], new_accs[part] = state
 
 
-def attend_middle(table, q_rot, state, other):
+def attend_middle(table, q_rot, state, b3, f4):
     return pl.pallas_call(
         middle_kernel,
         out_shape=STATE,
-        in_specs=[SMEM, VMEM, VMEM, VMEM, VMEM, ANY],
+        in_specs=[SMEM, VMEM, VMEM, VMEM, VMEM, ANY, ANY],
         out_specs=(VMEM, VMEM, VMEM),
         scratch_shapes=[
             pltpu.VMEM((MIDDLE, 2, ROWS, HD), jnp.bfloat16),
-            pltpu.SemaphoreType.DMA,
+            pltpu.SemaphoreType.DMA((2,)),
         ],
         compiler_params=pltpu.CompilerParams(vmem_limit_bytes=BIG_GRANT),
         cost_estimate=pl.CostEstimate(
             flops=2_000_000_000, bytes_accessed=2_000_000, transcendentals=1_000_000
         ),
         name="attend_middle",
-    )(table, q_rot, *state, other)
+    )(table, q_rot, *state, b3, f4)
 
 
 def rest_kernel(table, q_rot, tops, totals, accs, other, out, kv, sem):
@@ -531,7 +529,7 @@
     f3 = lax.ppermute(f2, "cp", ahead)
     b3 = lax.ppermute(b2, "cp", back)
     f4 = lax.ppermute(f3, "cp", ahead)
-    state = attend_first(table, counts, q_rot, unit, f1, b1, f2, b2, f3, b3)
+    state = attend_first(table, counts, q_rot, unit, f1, b1, f2, b2, f3)
     f4, state = tie((f4, state))
     own = jnp.concatenate([unit, f1, b1, f2, b2, f3, b3, f4], axis=0)
 
@@ -539,7 +537,7 @@
     pages = mine + lax.ppermute(theirs, "cp", CORE_PAIRS)
     across = lax.ppermute(pages[1], ("cp", "tp"), MIRROR_PAIRS)
     pages, state = tie((pages, state))
-    state = attend_middle(table, q_rot, state, f4)
+    state = attend_middle(table, q_rot, state, b3, f4)
     own, state = tie((own, state))
     other = lax.ppermute(own, "cp", CORE_PAIRS)
     across, state = tie((across, state))

time: 90.4 us -> 90.9 us (level); the launches traced: 88.8 us -> 90.5 us
  starting transfers between devices: 52.8 us -> 53.8 us
  waiting for transfers between devices: 8.09 us -> 9.06 us
    ppermute x1, starting transfers between devices: 1.92 us -> 2.88 us  [shards(): other = lax.ppermute(own, 'cp', CORE_PAIRS)]
  transfers between devices with their start and end apart: 12 -> 12, of which waited for: 6 -> 6; matrix products, arithmetic and copies ran while one was open for 0% -> 0% of each run, Pallas kernels for 25% -> 24%
where the time goes in v7:
time: 90.9 us; the launch traced here: 90.5 us
  starting transfers between devices  53.8 us (59%)
  Pallas kernels  26.3 us (29%)
  waiting for transfers between devices  9.06 us (10%)
  between operations  0.94 us (1%)
    ppermute x1, starting transfers between devices, shards(): pages = mine + lax.ppermute(theirs, 'cp', CORE_PAIRS)  8.3 us
    pallas_call x1, Pallas kernels, attend_rest(): pl.pallas_call(rest_kernel, out_shape=jax.ShapeDtypeStruct((ROWS, KVH * H...  7.83 us
    all_to_all x1, starting transfers between devices, shards(): unit = lax.all_to_all(packed, 'cp', 0, 0, axis_index_groups=Z_GROUPS)  7.81 us
    ppermute x1, starting transfers between devices, shards(): across = lax.ppermute(pages[1], ('cp', 'tp'), MIRROR_PAIRS)  7.23 us
    pallas_call x1, Pallas kernels, attend_first(): pl.pallas_call(first_kernel, out_shape=STATE, in_specs=[SMEM, SMEM, VMEM]...  5.43 us
    ppermute x1, starting transfers between devices, shards(): f1 = lax.ppermute(unit, 'cp', ahead)  4.86 us
    ppermute x1, starting transfers between devices, shards(): b2 = lax.ppermute(b1, 'cp', back)  4.57 us
    ppermute x1, starting transfers between devices, shards(): b3 = lax.ppermute(b2, 'cp', back)  4.57 us
  transfers between devices with their start and end apart: 12, of which 6 were waited for; matrix products, arithmetic and copies ran while one was open for 0% of the time, Pallas kernels for 24%

profile of v7, /device:TPU:1, one launch (start us, length us, event | category | flops | bytes accessed | tf_op | source)
XLA Modules:
  0.0 90.5 jit_solution(6147271374395707252)
XLA Ops:
  0.6 0.0 copy-start.1
  0.6 1.7 %pack.1 = bf16[4,2,128,128]{3,2,1,0:T(8,128)(2,1)} custom-call(s32[64,128]{1,0:T(8,128)} %bitcast.3, bf16[128,128]{1,0:T(8,128)(2,1)} %keys.1, bf16[128,128]{1,0:T(8,128)(2,1)} %values.1, f32[2,128,128]{2,1,0:T(8,128)} %constant.4.clone.run_table, f32[2,64,128]{2,1,0:T(8,128)} %constant.5.clone.step_table), custom_call_target="tpu_custom_call" | custom-call | flops 1000000 | bytes 400000 | tf_op jit(solution)/shard_map/pack/pallas_call | solution.py:111
  2.4 7.8 %all-to-all-start = ((bf16[4,2,128,128]{3,2,1,0:T(8,128)(2,1)}), bf16[4,2,128,128]{3,2,1,0:T(8,128)(2,1)S(1)}, u32[]{:S(2)}, u32[]{:S(2)}) async-start(bf16[4,2,128,128]{3,2,1,0:T(8,128)(2,1)} %pack.1), calls=%async_computation | async-start | bytes 524288 | tf_op jit(solution)/shard_map/all_to_all | solution.py:519
  10.2 2.2 %turn.1 = (bf16[2,512,128]{2,1,0:T(8,128)(2,1)}, s32[64]{0:T(128)}) custom-call(s32[8192]{0:T(1024)} %positions, bf16[128,1024]{1,0:T(8,128)(2,1)} %queries.1, f32[2,128,128]{2,1,0:T(8,128)} %constant.4.clone.run_table, f32[2,64,128]{2,1,0:T(8,128)} %constant.5.clone.step_table), custom_call_target="tpu_custom_call" | custom-call | flops 2000000 | bytes 600000 | tf_op jit(solution)/shard_map/turn/pallas_call | solution.py:145
  12.4 0.0 copy-start.2
  12.4 3.6 %lists.1 = (s32[8,128]{1,0:T(8,128)}, s32[128]{0:T(128)}) custom-call(s32[64]{0:T(128)} %get-tuple-element.44.runs, s32[64]{0:T(128)} %counts.3, s32[8,64]{1,0:T(8,128)} %owner_row.1, s32[8,64]{1,0:T(8,128)} %owner_col.1, s32[8,64]{1,0:T(8,128)} %owner_slot.1), custom_call_target="tpu_custom_call" | custom-call | flops 2000000 | bytes 300000 | tf_op jit(solution)/shard_map/lists/pallas_call | solution.py:235
  16.1 0.0 copy-start.3
  16.1 0.0 all-to-all-done.refs_0_
  16.1 4.9 %collective-permute-start = (bf16[4,2,128,128]{3,2,1,0:T(8,128)(2,1)S(1)}, bf16[4,2,128,128]{3,2,1,0:T(8,128)(2,1)S(1)}, u32[]{:S(2)}, u32[]{:S(2)}) collective-permute-start(bf16[4,2,128,128]{3,2,1,0:T(8,128)(2,1)S(1)} %all-to-all-done.refs_0_), channel_id=1, source_target_pairs={{0,16},{8,24},{16,32},{24,40},{32,48},{40,56},{48,64},{56,72},{64,... | collective-permute-start | bytes 786440 | tf_op jit(solution)/shard_map/ppermute | solution.py:525
  21.0 3.8 %collective-permute-start.1 = (bf16[4,2,128,128]{3,2,1,0:T(8,128)(2,1)S(1)}, bf16[4,2,128,128]{3,2,1,0:T(8,128)(2,1)S(1)}, u32[]{:S(2)}, u32[]{:S(2)}) collective-permute-start(bf16[4,2,128,128]{3,2,1,0:T(8,128)(2,1)S(1)} %all-to-all-done.refs_0_), channel_id=1, source_target_pairs={{0,112},{8,120},{16,0},{24,8},{32,16},{40,24},{48,32},{56,40},{64,... | collective-permute-start | bytes 786440 | tf_op jit(solution)/shard_map/ppermute | solution.py:526
  24.8 2.4 %collective-permute-done.refs_1_ = bf16[4,2,128,128]{3,2,1,0:T(8,128)(2,1)S(1)} collective-permute-done((bf16[4,2,128,128]{3,2,1,0:T(8,128)(2,1)S(1)}, bf16[4,2,128,128]{3,2,1,0:T(8,128)(2,1)S(1)}, u32[]{:S(2)}, u32[]{:S(2)}) %collective-permute-start) | collective-permute-done | bytes 262176 | tf_op jit(solution)/shard_map/ppermute | solution.py:525
  27.1 1.9 %collective-permute-start.2 = (bf16[4,2,128,128]{3,2,1,0:T(8,128)(2,1)S(1)}, bf16[4,2,128,128]{3,2,1,0:T(8,128)(2,1)S(1)}, u32[]{:S(2)}, u32[]{:S(2)}) collective-permute-start(bf16[4,2,128,128]{3,2,1,0:T(8,128)(2,1)S(1)} %collective-permute-done.refs_1_), channel_id=1, source_target_pairs={{0,16},{8,24},{16,32},{24,40},{32,48},{40,56},{48,64},{56,72},{64,... | collective-permute-start | bytes 786440 | tf_op jit(solution)/shard_map/ppermute | solution.py:527
  29.1 0.0 collective-permute-done.1.refs_2_
  29.1 4.6 %collective-permute-start.3 = (bf16[4,2,128,128]{3,2,1,0:T(8,128)(2,1)S(1)}, bf16[4,2,128,128]{3,2,1,0:T(8,128)(2,1)S(1)}, u32[]{:S(2)}, u32[]{:S(2)}) collective-permute-start(bf16[4,2,128,128]{3,2,1,0:T(8,128)(2,1)S(1)} %collective-permute-done.1.refs_2_), channel_id=1, source_target_pairs={{0,112},{8,120},{16,0},{24,8},{32,16},{40,24},{48,32},{56,40},{64,... | collective-permute-start | bytes 786440 | tf_op jit(solution)/shard_map/ppermute | solution.py:528
  33.7 1.7 %collective-permute-done.2.refs_3_ = bf16[4,2,128,128]{3,2,1,0:T(8,128)(2,1)S(1)} collective-permute-done((bf16[4,2,128,128]{3,2,1,0:T(8,128)(2,1)S(1)}, bf16[4,2,128,128]{3,2,1,0:T(8,128)(2,1)S(1)}, u32[]{:S(2)}, u32[]{:S(2)}) %collective-permute-start.2) | collective-permute-done | bytes 262176 | tf_op jit(solution)/shard_map/ppermute | solution.py:527
  35.5 1.9 %collective-permute-start.4 = (bf16[4,2,128,128]{3,2,1,0:T(8,128)(2,1)S(1)}, bf16[4,2,128,128]{3,2,1,0:T(8,128)(2,1)S(1)}, u32[]{:S(2)}, u32[]{:S(2)}) collective-permute-start(bf16[4,2,128,128]{3,2,1,0:T(8,128)(2,1)S(1)} %collective-permute-done.2.refs_3_), channel_id=1, source_target_pairs={{0,16},{8,24},{16,32},{24,40},{32,48},{40,56},{48,64},{56,72},{64,... | collective-permute-start | bytes 786440 | tf_op jit(solution)/shard_map/ppermute | solution.py:529
  37.4 0.0 collective-permute-done.3.refs_4_
  37.4 4.6 %collective-permute-start.5 = (bf16[4,2,128,128]{3,2,1,0:T(8,128)(2,1)S(1)}, bf16[4,2,128,128]{3,2,1,0:T(8,128)(2,1)S(1)}, u32[]{:S(2)}, u32[]{:S(2)}) collective-permute-start(bf16[4,2,128,128]{3,2,1,0:T(8,128)(2,1)S(1)} %collective-permute-done.3.refs_4_), channel_id=1, source_target_pairs={{0,112},{8,120},{16,0},{24,8},{32,16},{40,24},{48,32},{56,40},{64,... | collective-permute-start | bytes 786440 | tf_op jit(solution)/shard_map/ppermute | solution.py:530
  42.1 0.0 copy-start
  42.1 1.7 %collective-permute-done.4.refs_5_ = bf16[4,2,128,128]{3,2,1,0:T(8,128)(2,1)S(1)} collective-permute-done((bf16[4,2,128,128]{3,2,1,0:T(8,128)(2,1)S(1)}, bf16[4,2,128,128]{3,2,1,0:T(8,128)(2,1)S(1)}, u32[]{:S(2)}, u32[]{:S(2)}) %collective-permute-start.4) | collective-permute-done | bytes 262176 | tf_op jit(solution)/shard_map/ppermute | solution.py:529
  43.8 1.9 %collective-permute-start.6 = (bf16[4,2,128,128]{3,2,1,0:T(8,128)(2,1)S(1)}, bf16[4,2,128,128]{3,2,1,0:T(8,128)(2,1)S(1)}, u32[]{:S(2)}, u32[]{:S(2)}) collective-permute-start(bf16[4,2,128,128]{3,2,1,0:T(8,128)(2,1)S(1)} %collective-permute-done.4.refs_5_), channel_id=1, source_target_pairs={{0,16},{8,24},{16,32},{24,40},{32,48},{40,56},{48,64},{56,72},{64,... | collective-permute-start | bytes 786440 | tf_op jit(solution)/shard_map/ppermute | solution.py:531
  45.7 0.0 copy-done.1
  45.7 0.0 copy-done.2
  45.7 0.0 copy-done.3
  45.7 5.4 %attend_first.1 = (f32[2,1,512]{2,1,0:T(1,128)S(1)}, f32[2,1,512]{2,1,0:T(1,128)S(1)}, f32[2,128,512]{2,1,0:T(8,128)S(1)}) custom-call(s32[8,128]{1,0:T(8,128)S(1)} %copy-done.3, s32[64]{0:T(128)S(1)} %copy-done.1, bf16[2,512,128]{2,1,0:T(8,128)(2,1)S(1)} %copy-done.2, bf16[4,2,128,128]{3,2,1,0:T(8,128)(2,1)S(1)} %all-to-all-done.refs_0_, ...), custom_call_target="tpu_custom_call" | custom-call | flops 6000000000 | bytes 3000000 | tf_op jit(solution)/shard_map/attend_first/pallas_call | solution.py:343
  51.2 0.0 collective-permute-done.5.b3
  51.3 0.8 collective-permute-done.6.f4
  52.1 0.0 copy-done
  52.1 0.9 %pick.1 = (bf16[2,2,128,128]{3,2,1,0:T(8,128)(2,1)S(1)}, bf16[2,2,128,128]{3,2,1,0:T(8,128)(2,1)S(1)}) custom-call(s32[128]{0:T(128)S(1)} %copy-done, bf16[32,2,128,128]{3,2,1,0:T(8,128)(2,1)S(1)} %constant_dynamic-update-slice_fusion.own), custom_call_target="tpu_custom_call" | custom-call | flops 100000 | bytes 300000 | tf_op jit(solution)/shard_map/pick/pallas_call | solution.py:439
  53.1 8.3 %collective-permute-start.7 = (bf16[2,2,128,128]{3,2,1,0:T(8,128)(2,1)S(1)}, bf16[2,2,128,128]{3,2,1,0:T(8,128)(2,1)S(1)}, u32[]{:S(2)}, u32[]{:S(2)}) collective-permute-start(bf16[2,2,128,128]{3,2,1,0:T(8,128)(2,1)S(1)} %get-tuple-element.56), channel_id=1, source_target_pairs={{0,8},{8,0},{16,24},{24,16},{32,40},{40,32},{48,56},{56,48},{64,72... | collective-permute-start | bytes 393224 | tf_op jit(solution)/shard_map/ppermute | solution.py:537
  61.4 1.0 %collective-permute-done.7 = bf16[2,2,128,128]{3,2,1,0:T(8,128)(2,1)S(1)} collective-permute-done((bf16[2,2,128,128]{3,2,1,0:T(8,128)(2,1)S(1)}, bf16[2,2,128,128]{3,2,1,0:T(8,128)(2,1)S(1)}, u32[]{:S(2)}, u32[]{:S(2)}) %collective-permute-start.7) | collective-permute-done | bytes 131104 | tf_op jit(solution)/shard_map/ppermute | solution.py:537
  62.4 7.2 %collective-permute-start.8 = (bf16[2,128,128]{2,1,0:T(8,128)(2,1)S(1)}, bf16[2,128,128]{2,1,0:T(8,128)(2,1)S(1)}, u32[]{:S(2)}, u32[]{:S(2)}) collective-permute-start(bf16[2,128,128]{2,1,0:T(8,128)(2,1)S(1)} %slice_bitcast_fusion), channel_id=1, source_target_pairs={{0,388},{1,389},{2,390},{3,391},{4,384},{5,385},{6,386},{7,387},{8... | collective-permute-start | bytes 196616 | tf_op jit(solution)/shard_map/ppermute | solution.py:538
  69.6 2.2 %attend_middle.1 = (f32[2,1,512]{2,1,0:T(1,128)S(1)}, f32[2,1,512]{2,1,0:T(1,128)S(1)}, f32[2,128,512]{2,1,0:T(8,128)S(1)}) custom-call(s32[8,128]{1,0:T(8,128)S(1)} %copy-done.3, bf16[2,512,128]{2,1,0:T(8,128)(2,1)S(1)} %copy-done.2, f32[2,1,512]{2,1,0:T(1,128)S(1)} %get-tuple-element.61.tops, f32[2,1,512]{2,1,0:T(1,128)S(1)} %get-tuple-element.62.totals, ...), custom_call_target="tpu_custom_call" | custom-call | flops 2000000000 | bytes 2000000 | tf_op jit(solution)/shard_map/attend_middle/pallas_call | solution.py:369
  71.8 2.9 %collective-permute-start.9 = (bf16[32,2,128,128]{3,2,1,0:T(8,128)(2,1)S(1)}, bf16[32,2,128,128]{3,2,1,0:T(8,128)(2,1)}, u32[]{:S(2)}, u32[]{:S(2)}) collective-permute-start(bf16[32,2,128,128]{3,2,1,0:T(8,128)(2,1)S(1)} %constant_dynamic-update-slice_fusion.own), channel_id=1, source_target_pairs={{0,8},{8,0},{16,24},{24,16},{32,40},{40,32},{48,56},{56,48},{64,72... | collective-permute-start | bytes 6291464 | tf_op jit(solution)/shard_map/ppermute | solution.py:542
  74.7 0.0 collective-permute-done.8.across
  74.7 0.9 spread.1
  75.6 4.0 %all-to-all-start.1 = ((bf16[4,2,2,128,128]{4,3,2,1,0:T(8,128)(2,1)}), bf16[4,2,2,128,128]{4,3,2,1,0:T(8,128)(2,1)S(1)}, u32[]{:S(2)}, u32[]{:S(2)}) async-start(bf16[4,2,2,128,128]{4,3,2,1,0:T(8,128)(2,1)} %spread.1), calls=%async_computation.1 | async-start | bytes 1048576 | tf_op jit(solution)/shard_map/all_to_all | solution.py:544
  79.6 0.0 collective-permute-done.9.other
  79.6 7.8 %attend_rest.1 = bf16[128,1024]{1,0:T(8,128)(2,1)} custom-call(s32[8,128]{1,0:T(8,128)S(1)} %copy-done.3, bf16[2,512,128]{2,1,0:T(8,128)(2,1)S(1)} %copy-done.2, f32[2,1,512]{2,1,0:T(1,128)S(1)} %get-tuple-element.71.tops, f32[2,1,512]{2,1,0:T(1,128)S(1)} %get-tuple-element.72.totals, f32[2,128,512]{2,1,0:T(8,128)S(1)} %get-tuple-element.73.accs, ...), custom_call_target="tpu_custom_call" | custom-call | flops 8000000000 | bytes 4000000 | tf_op jit(solution)/shard_map/attend_rest/pallas_call | solution.py:401
  87.4 1.5 %all-to-all-done.1.pages = bf16[4,2,2,128,128]{4,3,2,1,0:T(8,128)(2,1)S(1)} async-done(((bf16[4,2,2,128,128]{4,3,2,1,0:T(8,128)(2,1)}), bf16[4,2,2,128,128]{4,3,2,1,0:T(8,128)(2,1)S(1)}, u32[]{:S(2)}, u32[]{:S(2)}) %all-to-all-start.1) | async-done | bytes 524320 | tf_op jit(solution)/shard_map/all_to_all | solution.py:544
  88.9 1.5 %place.1 = (bf16[2,128,128]{2,1,0:T(8,128)(2,1)}, bf16[2,128,128]{2,1,0:T(8,128)(2,1)}) custom-call(s32[128]{0:T(128)S(1)} %copy-done, bf16[4,2,2,128,128]{4,3,2,1,0:T(8,128)(2,1)S(1)} %all-to-all-done.1.pages), custom_call_target="tpu_custom_call" | custom-call | flops 100000 | bytes 800000 | tf_op jit(solution)/shard_map/place/pallas_call | solution.py:504
  (10 shorter events, 0.3 us)
Async XLA Ops:
  0.6 45.1 %copy-start.1 = (s32[64]{0:T(128)S(1)}, s32[64]{0:T(128)}, u32[]{:S(2)}) copy-start(s32[64]{0:T(128)} %counts.3) | copy-start | bytes 772
  2.4 13.7 %all-to-all-start = ((bf16[4,2,128,128]{3,2,1,0:T(8,128)(2,1)}), bf16[4,2,128,128]{3,2,1,0:T(8,128)(2,1)S(1)}, u32[]{:S(2)}, u32[]{:S(2)}) async-start(bf16[4,2,128,128]{3,2,1,0:T(8,128)(2,1)} %pack.1), calls=%async_computation | async-start | bytes 524288 | tf_op jit(solution)/shard_map/all_to_all | solution.py:519
  12.4 33.3 %copy-start.2 = (bf16[2,512,128]{2,1,0:T(8,128)(2,1)S(1)}, bf16[2,512,128]{2,1,0:T(8,128)(2,1)}, u32[]{:S(2)}) copy-start(bf16[2,512,128]{2,1,0:T(8,128)(2,1)} %get-tuple-element.50.q_rot) | copy-start | bytes 786436
  16.1 29.6 %copy-start.3 = (s32[8,128]{1,0:T(8,128)S(1)}, s32[8,128]{1,0:T(8,128)}, u32[]{:S(2)}) copy-start(s32[8,128]{1,0:T(8,128)} %get-tuple-element.49.table) | copy-start | bytes 12292
  16.1 11.1 %collective-permute-start = (bf16[4,2,128,128]{3,2,1,0:T(8,128)(2,1)S(1)}, bf16[4,2,128,128]{3,2,1,0:T(8,128)(2,1)S(1)}, u32[]{:S(2)}, u32[]{:S(2)}) collective-permute-start(bf16[4,2,128,128]{3,2,1,0:T(8,128)(2,1)S(1)} %all-to-all-done.refs_0_), channel_id=1, source_target_pairs={{0,16},{8,24},{16,32},{24,40},{32,48},{40,56},{48,64},{56,72},{64,... | collective-permute-start | bytes 786440 | tf_op jit(solution)/shard_map/ppermute | solution.py:525
  21.0 8.1 %collective-permute-start.1 = (bf16[4,2,128,128]{3,2,1,0:T(8,128)(2,1)S(1)}, bf16[4,2,128,128]{3,2,1,0:T(8,128)(2,1)S(1)}, u32[]{:S(2)}, u32[]{:S(2)}) collective-permute-start(bf16[4,2,128,128]{3,2,1,0:T(8,128)(2,1)S(1)} %all-to-all-done.refs_0_), channel_id=1, source_target_pairs={{0,112},{8,120},{16,0},{24,8},{32,16},{40,24},{48,32},{56,40},{64,... | collective-permute-start | bytes 786440 | tf_op jit(solution)/shard_map/ppermute | solution.py:526
  27.1 8.3 %collective-permute-start.2 = (bf16[4,2,128,128]{3,2,1,0:T(8,128)(2,1)S(1)}, bf16[4,2,128,128]{3,2,1,0:T(8,128)(2,1)S(1)}, u32[]{:S(2)}, u32[]{:S(2)}) collective-permute-start(bf16[4,2,128,128]{3,2,1,0:T(8,128)(2,1)S(1)} %collective-permute-done.refs_1_), channel_id=1, source_target_pairs={{0,16},{8,24},{16,32},{24,40},{32,48},{40,56},{48,64},{56,72},{64,... | collective-permute-start | bytes 786440 | tf_op jit(solution)/shard_map/ppermute | solution.py:527
  29.1 8.4 %collective-permute-start.3 = (bf16[4,2,128,128]{3,2,1,0:T(8,128)(2,1)S(1)}, bf16[4,2,128,128]{3,2,1,0:T(8,128)(2,1)S(1)}, u32[]{:S(2)}, u32[]{:S(2)}) collective-permute-start(bf16[4,2,128,128]{3,2,1,0:T(8,128)(2,1)S(1)} %collective-permute-done.1.refs_2_), channel_id=1, source_target_pairs={{0,112},{8,120},{16,0},{24,8},{32,16},{40,24},{48,32},{56,40},{64,... | collective-permute-start | bytes 786440 | tf_op jit(solution)/shard_map/ppermute | solution.py:528
  35.5 8.3 %collective-permute-start.4 = (bf16[4,2,128,128]{3,2,1,0:T(8,128)(2,1)S(1)}, bf16[4,2,128,128]{3,2,1,0:T(8,128)(2,1)S(1)}, u32[]{:S(2)}, u32[]{:S(2)}) collective-permute-start(bf16[4,2,128,128]{3,2,1,0:T(8,128)(2,1)S(1)} %collective-permute-done.2.refs_3_), channel_id=1, source_target_pairs={{0,16},{8,24},{16,32},{24,40},{32,48},{40,56},{48,64},{56,72},{64,... | collective-permute-start | bytes 786440 | tf_op jit(solution)/shard_map/ppermute | solution.py:529
  37.4 13.8 %collective-permute-start.5 = (bf16[4,2,128,128]{3,2,1,0:T(8,128)(2,1)S(1)}, bf16[4,2,128,128]{3,2,1,0:T(8,128)(2,1)S(1)}, u32[]{:S(2)}, u32[]{:S(2)}) collective-permute-start(bf16[4,2,128,128]{3,2,1,0:T(8,128)(2,1)S(1)} %collective-permute-done.3.refs_4_), channel_id=1, source_target_pairs={{0,112},{8,120},{16,0},{24,8},{32,16},{40,24},{48,32},{56,40},{64,... | collective-permute-start | bytes 786440 | tf_op jit(solution)/shard_map/ppermute | solution.py:530
  42.1 10.0 %copy-start = (s32[128]{0:T(128)S(1)}, s32[128]{0:T(128)}, u32[]{:S(2)}) copy-start(s32[128]{0:T(128)} %get-tuple-element.47.table) | copy-start | bytes 1540
  43.8 8.3 %collective-permute-start.6 = (bf16[4,2,128,128]{3,2,1,0:T(8,128)(2,1)S(1)}, bf16[4,2,128,128]{3,2,1,0:T(8,128)(2,1)S(1)}, u32[]{:S(2)}, u32[]{:S(2)}) collective-permute-start(bf16[4,2,128,128]{3,2,1,0:T(8,128)(2,1)S(1)} %collective-permute-done.4.refs_5_), channel_id=1, source_target_pairs={{0,16},{8,24},{16,32},{24,40},{32,48},{40,56},{48,64},{56,72},{64,... | collective-permute-start | bytes 786440 | tf_op jit(solution)/shard_map/ppermute | solution.py:531
  53.1 9.3 %collective-permute-start.7 = (bf16[2,2,128,128]{3,2,1,0:T(8,128)(2,1)S(1)}, bf16[2,2,128,128]{3,2,1,0:T(8,128)(2,1)S(1)}, u32[]{:S(2)}, u32[]{:S(2)}) collective-permute-start(bf16[2,2,128,128]{3,2,1,0:T(8,128)(2,1)S(1)} %get-tuple-element.56), channel_id=1, source_target_pairs={{0,8},{8,0},{16,24},{24,16},{32,40},{40,32},{48,56},{56,48},{64,72... | collective-permute-start | bytes 393224 | tf_op jit(solution)/shard_map/ppermute | solution.py:537
  62.4 12.3 %collective-permute-start.8 = (bf16[2,128,128]{2,1,0:T(8,128)(2,1)S(1)}, bf16[2,128,128]{2,1,0:T(8,128)(2,1)S(1)}, u32[]{:S(2)}, u32[]{:S(2)}) collective-permute-start(bf16[2,128,128]{2,1,0:T(8,128)(2,1)S(1)} %slice_bitcast_fusion), channel_id=1, source_target_pairs={{0,388},{1,389},{2,390},{3,391},{4,384},{5,385},{6,386},{7,387},{8... | collective-permute-start | bytes 196616 | tf_op jit(solution)/shard_map/ppermute | solution.py:538
  71.8 7.8 %collective-permute-start.9 = (bf16[32,2,128,128]{3,2,1,0:T(8,128)(2,1)S(1)}, bf16[32,2,128,128]{3,2,1,0:T(8,128)(2,1)}, u32[]{:S(2)}, u32[]{:S(2)}) collective-permute-start(bf16[32,2,128,128]{3,2,1,0:T(8,128)(2,1)S(1)} %constant_dynamic-update-slice_fusion.own), channel_id=1, source_target_pairs={{0,8},{8,0},{16,24},{24,16},{32,40},{40,32},{48,56},{56,48},{64,72... | collective-permute-start | bytes 6291464 | tf_op jit(solution)/shard_map/ppermute | solution.py:542
  75.6 13.3 %all-to-all-start.1 = ((bf16[4,2,2,128,128]{4,3,2,1,0:T(8,128)(2,1)}), bf16[4,2,2,128,128]{4,3,2,1,0:T(8,128)(2,1)S(1)}, u32[]{:S(2)}, u32[]{:S(2)}) async-start(bf16[4,2,2,128,128]{4,3,2,1,0:T(8,128)(2,1)} %spread.1), calls=%async_computation.1 | async-start | bytes 1048576 | tf_op jit(solution)/shard_map/all_to_all | solution.py:544
